TPU v7x, 32 devices: a whole 2x2x4 slice. The times are simulated.
32 devices in a mesh: grp: 2 (over y), clu: 4 (over z), row: 4 (over x, core).
Axes of the slice: x: 2, y: 2, z: 4, core: 2. Of those that a mesh axis runs over, the one named last changes fastest.
Arguments:
- slip: float32 [8192, 256], P(('grp', 'clu', 'row')), parts along dimension 0, may hold values from -6 to 6
- state: float32 [8192, 256], P(('grp', 'clu', 'row')), parts along dimension 0, may hold values from 0 to 1
- load: float32 [8192, 256], P(('grp', 'clu', 'row')), parts along dimension 0, may hold values from -6 to 6
- friction_a: float32 [8192], P(('grp', 'clu', 'row')), parts along dimension 0, may hold values from 1 to 3
- near_blocks: bfloat16 [3584, 128, 128], P(('grp', 'clu', 'row')), parts along dimension 0, may hold values from -0.0625 to 0.0625
- near_pairs: int32 [3584, 2], P(('grp', 'clu', 'row')), parts along dimension 0, may hold values from 0 to 31, as said below
- far_u: bfloat16 [128, 4, 32, 256], P(('grp', 'clu', 'row')), parts along dimension 0, may hold values from -0.25 to 0.25
- far_v: bfloat16 [128, 4, 32, 256], P(('grp', 'clu', 'row')), parts along dimension 0, may hold values from -0.375 to 0.375
- far_rank: int32 [128, 4], P(('grp', 'clu', 'row')), parts along dimension 0, may hold values from 1 to 32
Outputs:
- slip_next: float32 [8192, 256], P(('grp', 'clu', 'row')), parts along dimension 0
- state_next: float32 [8192, 256], P(('grp', 'clu', 'row')), parts along dimension 0
There are 2 independent parts, one for each index of `grp`. A program takes and returns all parts, laid end to end along the dimension named above; each array names one. Nothing has to cross between parts.
Inputs may be any that keep to these rules, and one draw needn't show every extreme that they name: `near_pairs`: rows k * 112 to (k + 1) * 112 - 1 belong to device k = c * 4 + r of clu+row; their target cluster lies in group c (clusters c * 8 to (c + 1) * 8 - 1) and their source cluster within 4 clusters of the target. Pairs may repeat; their blocks add.
All inputs are finite; a program needn't handle non-finite values.
Results may differ from a plain program's by a relative error of at most 0.00036.
Values may be sent and summed in bfloat16 or wider, within the bound.
No kernel may reach another device: no remote copies, remote signals or barrier semaphores. Data moves between devices by JAX's collectives and lax.ppermute only.
A program may use at most 128 MiB of HBM per device.

v0:
```python
import jax
import jax.numpy as jnp
from jax import lax
from jax.sharding import PartitionSpec as P

REACH = 4


step_size = 0.2


def padded(array, sides, width):
    for axis, dim in sides:
        devices, length = (lax.axis_size(axis), array.shape[dim])
        up = [(i, (i + 1) % devices) for i in range(devices - 1)]
        down = [(j, i) for i, j in up]
        last = lax.slice_in_dim(array, length - width, length, axis=dim)
        first = lax.slice_in_dim(array, 0, width, axis=dim)
        before = lax.ppermute(last, axis, up)
        after = lax.ppermute(first, axis, down)
        array = jnp.concatenate([before, array, after], axis=dim)
    return array


def slip_rates(stress, state, load, friction_a):
    softness = friction_a[:, None]
    velocity = 2.0 * jnp.exp(-state / softness) * jnp.sinh((stress + load) / (2.0 * softness))
    speed = jnp.abs(velocity)
    drift = jnp.exp(-state) - speed / (1.0 + speed)
    return (velocity, drift)


def near_stress(group_half, near_blocks, near_pairs):
    rows_all, members = group_half.shape
    leaf = near_blocks.shape[1]
    clusters = rows_all // leaf
    window = padded(group_half, (("clu", 0),), REACH * leaf)
    tiles = window.reshape(clusters + 2 * REACH, leaf, members)
    first = lax.axis_index("clu") * clusters
    picked = jnp.take(tiles, near_pairs[:, 1] - first + REACH, axis=0)
    product = jnp.einsum("kij,kjm->kim", near_blocks, picked, preferred_element_type=jnp.float32)
    owner = near_pairs[:, 0] - first
    onehot = (owner[None, :] == jnp.arange(clusters, dtype=jnp.int32)[:, None]).astype(jnp.float32)
    summed = jnp.einsum("tk,kim->tim", onehot, product, precision=lax.Precision.HIGHEST)
    return summed.reshape(rows_all, members)


def far_stress(own_half, far_u, far_v, far_rank):
    targets, sources, rank_cols, elems = far_u.shape
    members = own_half.shape[1]
    piece = lax.all_gather(own_half, "clu", axis=0, tiled=True)
    count = piece.shape[0] // elems
    blocks_in = piece.reshape(count, elems, members)
    coeffs = jnp.einsum("tkre,kem->tkrm", far_v, blocks_in, preferred_element_type=jnp.float32)
    column = lax.broadcasted_iota(jnp.int32, (1, 1, rank_cols, 1), 2)
    coeffs = jnp.where(column < far_rank[:, :, None, None], coeffs, 0.0).astype(jnp.bfloat16)
    total = jnp.einsum("tkre,tkrm->tem", far_u, coeffs, preferred_element_type=jnp.float32)
    return total.reshape(targets * elems, members)


def body(slip, state, load, friction_a, near_blocks, near_pairs, far_u, far_v, far_rank):

    def partial_stress(group_half, own_half):
        return near_stress(group_half, near_blocks, near_pairs) + far_stress(
            own_half, far_u, far_v, far_rank
        )

    def section_stress(field):
        own_half = field.astype(jnp.bfloat16)
        group_half = lax.all_gather(own_half, "row", axis=0, tiled=True)
        partial_value = partial_stress(group_half, own_half)
        return lax.psum_scatter(partial_value, "row", scatter_dimension=0, tiled=True)

    velocity_one, drift_one = slip_rates(section_stress(slip), state, load, friction_a)
    slip_mid = slip + step_size * velocity_one
    state_mid = state + step_size * drift_one
    velocity_two, drift_two = slip_rates(section_stress(slip_mid), state_mid, load, friction_a)
    slip_next = slip + 0.5 * step_size * (velocity_one + velocity_two)
    state_next = state + 0.5 * step_size * (drift_one + drift_two)
    return (slip_next, state_next)


def solution(mesh):
    placed = (
        P(("grp", "clu", "row"), None),
        P(("grp", "clu", "row"), None),
        P(("grp", "clu", "row"), None),
        P(("grp", "clu", "row")),
        P(("grp", "clu", "row"), None, None),
        P(("grp", "clu", "row"), None),
        P(("grp", "clu", "row"), None, None, None),
        P(("grp", "clu", "row"), None, None, None),
        P(("grp", "clu", "row"), None),
    )
    return jax.shard_map(
        body,
        mesh=mesh,
        in_specs=placed,
        out_specs=(P(("grp", "clu", "row"), None), P(("grp", "clu", "row"), None)),
        check_vma=False,
    )
```

profile of v0, /device:TPU:0, one launch (start us, length us, event | category | flops | bytes accessed | tf_op | source)
XLA Modules:
  0.0 228.3 jit_solution(13960135347473245515)
XLA Ops:
  7.2 0.0 copy-start
  7.2 0.0 reduce-scatter.3.cloned.1.call-start
  7.2 1.0 convert_element_type.14
  8.2 8.6 %all_gather.12 = bf16[1024,256]{1,0:T(8,128)(2,1)S(1)} all-gather(bf16[256,256]{1,0:T(8,128)(2,1)S(1)} %convert_element_type.14), channel_id=1, replica_groups=mesh['grp'=2,'clu'=4,'row'=4] {'row'}, dimensions={0}, use_global_device_ids=true | all-gather | bytes 655360 | tf_op jit(solution)/shard_map/all_gather | solution.py:70
  16.9 3.5 %collective-permute-start = (bf16[512,256]{1,0:T(8,128)(2,1)S(1)}, bf16[512,256]{1,0:T(8,128)(2,1)S(1)}, u32[]{:S(2)}, u32[]{:S(2)}) collective-permute-start(bf16[512,256]{1,0:T(8,128)(2,1)S(1)} %get-tuple-element.11), channel_id=1, source_target_pairs={{0,4},{4,8},{8,12},{1,5},{5,9},{9,13},{2,6},{6,10},{10,14},{3,7},{... | collective-permute-start | bytes 786440 | tf_op jit(solution)/shard_map/ppermute | solution.py:19
  20.4 1.3 collective-permute-start.1
  21.7 0.7 compare_and_fusion
  22.4 0.7 subtract_bitcast_fusion
  23.1 20.7 %all_gather.13 = bf16[1024,256]{1,0:T(8,128)(2,1)S(1)} all-gather(bf16[256,256]{1,0:T(8,128)(2,1)S(1)} %convert_element_type.14), channel_id=1, replica_groups=mesh['grp'=2,'clu'=4,'row'=4] {'clu'}, dimensions={0}, use_global_device_ids=true | all-gather | bytes 655360 | tf_op jit(solution)/shard_map/all_gather | solution.py:51
  43.8 0.8 iota_compare_fusion
  44.5 0.0 copy-done
  44.5 1.4 fusion.17
  46.0 0.0 collective-permute-done
  46.0 0.0 collective-permute-done.1
  46.0 1.0 pad_maximum_fusion
  47.0 6.3 %gather_fusion = bf16[112,128,256]{2,1,0:T(8,128)(2,1)} fusion(bf16[16,128,256]{2,1,0:T(8,128)(2,1)S(1)} %bitcast.66, s32[1024]{0:T(1024)S(1)} %pad_clamp_fusion), kind=kCustom, calls=%fused_computation.clone | custom fusion | bytes 14680512 | tf_op jit(solution)/shard_map/jit(_take)/gather | solution.py:40
  53.3 11.6 %fusion.6 = f32[112,256,128]{2,1,0:T(8,128)} fusion(bf16[112,128,128]{2,1,0:T(8,128)(2,1)} %param.15, bf16[112,128,256]{2,1,0:T(8,128)(2,1)} %gather_fusion, pred[112]{0:T(512)(128)(4,1)S(1)} %get-tuple-element.7), kind=kOutput, calls=%fused_computation.8 | convolution fusion | flops 943194112 | bytes 25690224 | tf_op jit(solution)/shard_map/kij,kjm->kim/dot_general | solution.py:41
  64.9 15.2 %copy.13 = f32[112,256,128]{1,0,2:T(8,128)} copy(f32[112,256,128]{2,1,0:T(8,128)} %fusion.6) | data formatting | bytes 29360128 | tf_op jit(solution)/shard_map/kij,kjm->kim/dot_general | solution.py:41
  80.1 0.0 copy-start.8
  80.1 0.0 copy-start.2
  80.1 0.0 copy-start.4
  80.1 0.0 copy-start.6
  80.1 8.1 %fusion.2 = f32[8,128,256]{2,0,1:T(8,128)S(1)} fusion(f32[112,256,128]{1,0,2:T(8,128)} %copy.13, s32[112]{0:T(128)S(1)} %subtract_bitcast_fusion), kind=kOutput, calls=%fused_computation.4 | convolution fusion | flops 352322432 | bytes 15729088 | tf_op jit(solution)/shard_map/tk,kim->tim/dot_general | solution.py:44
  88.3 0.0 copy-start.3
  88.3 0.3 copy.11
  88.6 1.1 bitcast_add_fusion.1
  89.7 0.0 reduce-scatter.3.cloned.1.call-update
  89.7 0.0 reduce-scatter.5.cloned.1.call-start
  89.8 0.0 copy-done.8
  89.8 23.0 %reduce-scatter.3.cloned.1.call-done = f32[256,256]{1,0:T(8,128)} async-done(((f32[1024,256]{1,0:T(8,128)}), f32[256,256]{1,0:T(8,128)}) %reduce-scatter.3.cloned.1.call-update) | async-done | bytes 262160 | tf_op jit(solution)/shard_map/reduce_scatter | solution.py:72
  112.8 0.0 copy-done.2
  112.8 0.0 copy-done.4
  112.8 0.0 copy-done.6
  112.8 1.4 add_convert_fusion
  114.2 6.8 %all_gather.14 = bf16[1024,256]{1,0:T(8,128)(2,1)S(1)} all-gather(bf16[256,256]{1,0:T(8,128)(2,1)S(1)} %get-tuple-element.5), channel_id=1, replica_groups=mesh['grp'=2,'clu'=4,'row'=4] {'row'}, dimensions={0}, use_global_device_ids=true | all-gather | bytes 655360 | tf_op jit(solution)/shard_map/all_gather | solution.py:70
  121.0 16.1 %all_gather.15 = bf16[1024,256]{1,0:T(8,128)(2,1)S(1)} all-gather(bf16[256,256]{1,0:T(8,128)(2,1)S(1)} %get-tuple-element.5), channel_id=1, replica_groups=mesh['grp'=2,'clu'=4,'row'=4] {'clu'}, dimensions={0}, use_global_device_ids=true | all-gather | bytes 655360 | tf_op jit(solution)/shard_map/all_gather | solution.py:51
  137.0 0.8 fusion.44
  137.8 4.3 %collective-permute-start.2 = (bf16[512,256]{1,0:T(8,128)(2,1)}, bf16[512,256]{1,0:T(8,128)(2,1)}, u32[]{:S(2)}, u32[]{:S(2)}) collective-permute-start(bf16[512,256]{1,0:T(8,128)(2,1)} %get-tuple-element.9), channel_id=1, source_target_pairs={{0,4},{4,8},{8,12},{1,5},{5,9},{9,13},{2,6},{6,10},{10,14},{3,7},{... | collective-permute-start | bytes 786440 | tf_op jit(solution)/shard_map/ppermute | solution.py:19
  142.2 1.5 collective-permute-start.3
  143.6 0.0 copy-done.3
  143.7 0.5 fusion.16
  144.1 1.5 collective-permute-done.2
  145.7 5.1 %collective-permute-done.3 = bf16[512,256]{1,0:T(8,128)(2,1)} collective-permute-done((bf16[512,256]{1,0:T(8,128)(2,1)}, bf16[512,256]{1,0:T(8,128)(2,1)}, u32[]{:S(2)}, u32[]{:S(2)}) %collective-permute-start.3) | collective-permute-done | bytes 262176 | tf_op jit(solution)/shard_map/ppermute | solution.py:20
  150.7 1.1 pad_maximum_fusion.1
  151.8 6.3 %gather_fusion.1 = bf16[112,128,256]{2,1,0:T(8,128)(2,1)} fusion(bf16[16,128,256]{2,1,0:T(8,128)(2,1)S(1)} %bitcast.65, s32[1024]{0:T(1024)S(1)} %pad_clamp_fusion), kind=kCustom, calls=%fused_computation.1.clone | custom fusion | bytes 14680512 | tf_op jit(solution)/shard_map/jit(_take)/gather | solution.py:40
  158.1 11.6 %fusion.4 = f32[112,256,128]{2,1,0:T(8,128)} fusion(bf16[112,128,128]{2,1,0:T(8,128)(2,1)} %param.15, bf16[112,128,256]{2,1,0:T(8,128)(2,1)} %gather_fusion.1, pred[112]{0:T(512)(128)(4,1)S(1)} %get-tuple-element.7), kind=kOutput, calls=%fused_computation.6 | convolution fusion | flops 943194112 | bytes 25690224 | tf_op jit(solution)/shard_map/kij,kjm->kim/dot_general | solution.py:41
  169.7 15.2 %copy.15 = f32[112,256,128]{1,0,2:T(8,128)} copy(f32[112,256,128]{2,1,0:T(8,128)} %fusion.4) | data formatting | bytes 29360128 | tf_op jit(solution)/shard_map/kij,kjm->kim/dot_general | solution.py:41
  184.9 0.0 copy-start.5
  184.9 0.0 copy-start.7
  184.9 0.0 copy-start.1
  184.9 8.1 %fusion = f32[8,128,256]{2,0,1:T(8,128)S(1)} fusion(f32[112,256,128]{1,0,2:T(8,128)} %copy.15, s32[112]{0:T(128)S(1)} %subtract_bitcast_fusion), kind=kOutput, calls=%fused_computation.2 | convolution fusion | flops 352322432 | bytes 15729088 | tf_op jit(solution)/shard_map/tk,kim->tim/dot_general | solution.py:44
  193.1 0.3 copy.12
  193.4 1.1 bitcast_add_fusion
  194.5 0.0 reduce-scatter.5.cloned.1.call-update
  194.5 23.9 %reduce-scatter.5.cloned.1.call-done = f32[256,256]{1,0:T(8,128)} async-done(((f32[1024,256]{1,0:T(8,128)}), f32[256,256]{1,0:T(8,128)}) %reduce-scatter.5.cloned.1.call-update) | async-done | bytes 262160 | tf_op jit(solution)/shard_map/reduce_scatter | solution.py:72
  218.5 0.0 copy-done.5
  218.5 0.0 copy-done.7
  218.5 2.3 fusion.28
  220.7 0.8 multiply_add_fusion
  221.5 0.0 copy-done.1
  (3 shorter events, 0.0 us)
Async XLA Ops:
  7.2 37.3 %copy-start = (bf16[4,4,32,256]{3,2,1,0:T(8,128)(2,1)S(1)}, bf16[4,4,32,256]{3,2,1,0:T(8,128)(2,1)}, u32[]{:S(2)}) copy-start(bf16[4,4,32,256]{3,2,1,0:T(8,128)(2,1)} %param.17) | copy-start | bytes 786436
  7.2 105.6 %reduce-scatter.3.cloned.1.call-start = ((), (), s32[]{:S(2)}) async-start(), calls=%async_computation.2 | async-start | bytes 1310720 | tf_op jit(solution)/shard_map/reduce_scatter | solution.py:72
  16.9 29.1 %collective-permute-start = (bf16[512,256]{1,0:T(8,128)(2,1)S(1)}, bf16[512,256]{1,0:T(8,128)(2,1)S(1)}, u32[]{:S(2)}, u32[]{:S(2)}) collective-permute-start(bf16[512,256]{1,0:T(8,128)(2,1)S(1)} %get-tuple-element.11), channel_id=1, source_target_pairs={{0,4},{4,8},{8,12},{1,5},{5,9},{9,13},{2,6},{6,10},{10,14},{3,7},{... | collective-permute-start | bytes 786440 | tf_op jit(solution)/shard_map/ppermute | solution.py:19
  20.4 25.6 %collective-permute-start.1 = (bf16[512,256]{1,0:T(8,128)(2,1)S(1)}, bf16[512,256]{1,0:T(8,128)(2,1)}, u32[]{:S(2)}, u32[]{:S(2)}) collective-permute-start(bf16[512,256]{1,0:T(8,128)(2,1)S(1)} %get-tuple-element.12), channel_id=1, source_target_pairs={{4,0},{8,4},{12,8},{5,1},{9,5},{13,9},{6,2},{10,6},{14,10},{7,3},{... | collective-permute-start | bytes 786440 | tf_op jit(solution)/shard_map/ppermute | solution.py:20
  80.1 9.7 %copy-start.8 = (f32[256]{0:T(256)S(1)}, f32[256]{0:T(256)}, u32[]{:S(2)}) copy-start(f32[256]{0:T(256)} %param.14) | copy-start | bytes 3076
  80.1 32.7 %copy-start.2 = (f32[256,256]{1,0:T(8,128)S(1)}, f32[256,256]{1,0:T(8,128)}, u32[]{:S(2)}) copy-start(f32[256,256]{1,0:T(8,128)} %param.11) | copy-start | bytes 786436
  80.1 32.7 %copy-start.4 = (f32[256,256]{1,0:T(8,128)S(1)}, f32[256,256]{1,0:T(8,128)}, u32[]{:S(2)}) copy-start(f32[256,256]{1,0:T(8,128)} %param.13) | copy-start | bytes 786436
  80.1 32.7 %copy-start.6 = (f32[256,256]{1,0:T(8,128)S(1)}, f32[256,256]{1,0:T(8,128)}, u32[]{:S(2)}) copy-start(f32[256,256]{1,0:T(8,128)} %param.12) | copy-start | bytes 786436
  88.3 55.4 %copy-start.3 = (bf16[4,4,32,256]{3,2,1,0:T(8,128)(2,1)S(1)}, bf16[4,4,32,256]{3,2,1,0:T(8,128)(2,1)}, u32[]{:S(2)}) copy-start(bf16[4,4,32,256]{3,2,1,0:T(8,128)(2,1)} %param.18) | copy-start | bytes 786436
  89.7 128.7 %reduce-scatter.5.cloned.1.call-start = ((), (), s32[]{:S(2)}) async-start(), calls=%async_computation.3 | async-start | bytes 1310720 | tf_op jit(solution)/shard_map/reduce_scatter | solution.py:72
  137.8 7.8 %collective-permute-start.2 = (bf16[512,256]{1,0:T(8,128)(2,1)}, bf16[512,256]{1,0:T(8,128)(2,1)}, u32[]{:S(2)}, u32[]{:S(2)}) collective-permute-start(bf16[512,256]{1,0:T(8,128)(2,1)} %get-tuple-element.9), channel_id=1, source_target_pairs={{0,4},{4,8},{8,12},{1,5},{5,9},{9,13},{2,6},{6,10},{10,14},{3,7},{... | collective-permute-start | bytes 786440 | tf_op jit(solution)/shard_map/ppermute | solution.py:19
  142.2 8.6 %collective-permute-start.3 = (bf16[512,256]{1,0:T(8,128)(2,1)}, bf16[512,256]{1,0:T(8,128)(2,1)}, u32[]{:S(2)}, u32[]{:S(2)}) collective-permute-start(bf16[512,256]{1,0:T(8,128)(2,1)} %get-tuple-element.10), channel_id=1, source_target_pairs={{4,0},{8,4},{12,8},{5,1},{9,5},{13,9},{6,2},{10,6},{14,10},{7,3},{... | collective-permute-start | bytes 786440 | tf_op jit(solution)/shard_map/ppermute | solution.py:20
  184.9 33.5 %copy-start.5 = (f32[256,256]{1,0:T(8,128)S(1)}, f32[256,256]{1,0:T(8,128)}, u32[]{:S(2)}) copy-start(f32[256,256]{1,0:T(8,128)} %param.13) | copy-start | bytes 786436
  184.9 33.5 %copy-start.7 = (f32[256,256]{1,0:T(8,128)S(1)}, f32[256,256]{1,0:T(8,128)}, u32[]{:S(2)}) copy-start(f32[256,256]{1,0:T(8,128)} %param.12) | copy-start | bytes 786436
  184.9 36.5 %copy-start.1 = (bf16[4,4,32,256]{3,2,1,0:T(8,128)(2,1)S(1)}, bf16[4,4,32,256]{3,2,1,0:T(8,128)(2,1)}, u32[]{:S(2)}) copy-start(bf16[4,4,32,256]{3,2,1,0:T(8,128)(2,1)} %param.17) | copy-start | bytes 786436
Sparse Core Ops, SparseCore 0:
  89.8 22.8 reduce-scatter.2
  194.7 23.7 reduce-scatter.4
where the time goes:
time: 229 us; the launch traced here: 228 us
  waiting for transfers between devices  53.5 us (23%)
  blocking collectives  52.1 us (23%)
  local copies, waits for them, and re-layouts  44.6 us (19%)
  matrix products  41.4 us (18%)
  between operations  14.2 us (6%)
  other arithmetic  11.8 us (5%)
  starting transfers between devices  10.7 us (5%)
    reduce_scatter x2, waiting for transfers between devices, section_stress(): lax.psum_scatter(partial_value, 'row', scatter_dimension=0, tiled=True)  46.9 us
    all_gather x2, blocking collectives, far_stress(): piece = lax.all_gather(own_half, 'clu', axis=0, tiled=True)  36.7 us
    dot_general x2, local copies, waits for them, and re-layouts, near_stress(): jnp.einsum('kij,kjm->kim', near_blocks, picked, preferred_element_type=jn...  30.5 us
    dot_general x2, matrix products, near_stress(): jnp.einsum('kij,kjm->kim', near_blocks, picked, preferred_element_type=jn...  23.2 us
    dot_general x2, matrix products, near_stress(): jnp.einsum('tk,kim->tim', onehot, product, precision=lax.Precision.HIGHEST)  16.3 us
    all_gather x2, blocking collectives, section_stress(): group_half = lax.all_gather(own_half, 'row', axis=0, tiled=True)  15.4 us
    gather x2, local copies, waits for them, and re-layouts, near_stress(): picked = jnp.take(tiles, near_pairs[:, 1] - first + REACH, axis=0)  12.5 us
    ppermute x2, starting transfers between devices, padded(): before = lax.ppermute(last, axis, up)  7.83 us
  transfers between devices with their start and end apart: 6, of which 4 were waited for; matrix products, arithmetic and copies ran while one was open for 2% of the time, Pallas kernels for 0%

commit v1 on v0

v1 whole, which is shorter than its diff:
```python
import functools

import jax
import jax.numpy as jnp
from jax import lax
from jax.experimental import pallas as pl
from jax.experimental.pallas import tpu as pltpu
from jax.sharding import PartitionSpec as P

REACH = 4
CORES = 2
STEP = 0.2
UNROLL = 16


def core_swap(array):
    devices = lax.axis_size("row")
    return lax.ppermute(array, "row", [(i, i ^ 1) for i in range(devices)])


def chip_shift(array, step):
    devices = lax.axis_size("row")
    pairs = [(i, (i + CORES * step) % devices) for i in range(devices)]
    return lax.ppermute(array, "row", pairs)


def group_shift(array, step):
    groups = lax.axis_size("clu")
    return lax.ppermute(array, "clu", [(i, (i + step) % groups) for i in range(groups)])


def group_next(array, step):
    groups = lax.axis_size("clu")
    pairs = [(i, i + step) for i in range(groups) if 0 <= i + step < groups]
    return lax.ppermute(array, "clu", pairs)


def stress_kernel(leaf, src, dst, place, blocks, window, far_u, coeffs, out):
    targets, groups, rank, elems = far_u.shape
    members = window.shape[1]
    chips = targets // CORES
    group, chip, core = place[0], place[1], place[2]
    for other in range(CORES):
        for ahead in range(chips):
            target = lax.rem(chip + ahead, chips) * CORES + (core ^ other)
            bases = [far_u[target, lax.rem(group + s, groups)] for s in range(groups)]
            parts = [coeffs[s, target] for s in range(groups)]
            out[pl.ds((other * chips + ahead) * elems, elems), :] = lax.dot_general(
                jnp.concatenate(bases, axis=0),
                jnp.concatenate(parts, axis=0),
                (((0,), (0,)), ((), ())),
                preferred_element_type=jnp.float32,
            )
    count = blocks.shape[0]
    unroll = UNROLL if count % UNROLL == 0 else 1

    def step(i, carry):
        products = []
        for u in range(unroll):
            j = i * unroll + u
            rows = window[pl.ds(pl.multiple_of(src[j] * leaf, leaf), leaf), :]
            products.append(jnp.dot(blocks[j], rows, preferred_element_type=jnp.float32))
        for u in range(unroll):
            j = i * unroll + u
            out[pl.ds(pl.multiple_of(dst[j] * leaf, leaf), leaf), :] += products[u]
        return carry

    lax.fori_loop(0, count // unroll, step, 0)


def partial_stress(src, dst, place, blocks, window, far_u, coeffs):
    targets, groups, rank, elems = far_u.shape
    count, leaf, _ = blocks.shape
    members = window.shape[1]
    vmem = pl.BlockSpec(memory_space=pltpu.VMEM)
    smem = pl.BlockSpec(memory_space=pltpu.SMEM)
    return pl.pallas_call(
        functools.partial(stress_kernel, leaf),
        out_shape=jax.ShapeDtypeStruct((targets * elems, members), jnp.float32),
        in_specs=[smem, smem, smem, vmem, vmem, vmem, vmem],
        out_specs=vmem,
        compiler_params=pltpu.CompilerParams(vmem_limit_bytes=40 * 1024 * 1024),
        cost_estimate=pl.CostEstimate(
            flops=2 * members * (count * leaf * leaf + targets * groups * rank * elems),
            bytes_accessed=2 * count * leaf * leaf + 8 * targets * elems * members,
            transcendentals=0,
        ),
    )(src, dst, place, blocks, window, far_u, coeffs)


def slip_rates(stress, state, load, friction_a):
    softness = friction_a[:, None]
    velocity = 2.0 * jnp.exp(-state / softness) * jnp.sinh((stress + load) / (2.0 * softness))
    speed = jnp.abs(velocity)
    drift = jnp.exp(-state) - speed / (1.0 + speed)
    return (velocity, drift)


def body(slip, state, load, friction_a, near_blocks, near_pairs, far_u, far_v, far_rank):
    elems, members = slip.shape
    leaf = near_blocks.shape[1]
    own = elems // leaf
    devices, groups = lax.axis_size("row"), lax.axis_size("clu")
    chips = devices // CORES
    clusters = devices * own
    assert REACH <= CORES * own
    group, row = lax.axis_index("clu"), lax.axis_index("row")
    chip, core = row // CORES, row % CORES
    place = jnp.stack([group, chip, core]).astype(jnp.int32)

    source = near_pairs[:, 1] - group * clusters
    before, after = source < 0, source >= clusters
    local = jnp.where(before, source + clusters, jnp.where(after, source - clusters, source))
    holder = local // own
    piece = jnp.where(
        before,
        chips,
        jnp.where(after, chips + 1, (chip - holder // CORES + chips) % chips),
    )
    other = (holder % CORES) ^ core
    src = ((other * (chips + 2) + piece) * own + local % own).astype(jnp.int32)
    target = near_pairs[:, 0] - group * clusters
    owner = target // own
    ahead = (owner // CORES - chip + chips) % chips
    dst = ((((owner % CORES) ^ core) * chips + ahead) * own + target % own).astype(jnp.int32)

    rank = far_u.shape[2]
    column = lax.broadcasted_iota(jnp.int32, (1, 1, rank, 1), 2)
    bases = jnp.where(column < far_rank[:, :, None, None], far_v, jnp.zeros_like(far_v))
    held = []
    for s in range(groups):
        there = lax.dynamic_index_in_dim(bases, (group + s) % groups, axis=1, keepdims=False)
        held.append(there if s == 0 else group_shift(there, s))
    held = jnp.stack(held).reshape(groups * devices * rank, elems)

    def section_stress(field):
        half = field.astype(jnp.bfloat16)
        coeffs = jnp.dot(held, half, preferred_element_type=jnp.float32).astype(jnp.bfloat16)
        coeffs = coeffs.reshape(groups, devices, rank, members)
        coeffs = jnp.stack(
            [coeffs[s] if s == 0 else group_shift(coeffs[s], -s) for s in range(groups)]
        )
        pieces = [half] + [chip_shift(half, s) for s in range(1, chips)]
        near = jnp.stack(pieces)
        last = lax.dynamic_index_in_dim(near, (chip + 1) % chips, axis=0, keepdims=False)
        first = lax.dynamic_index_in_dim(near, chip, axis=0, keepdims=False)
        ends = jnp.stack([group_next(last, 1), group_next(first, -1)])
        window = jnp.concatenate([near, ends, core_swap(near), core_swap(ends)], axis=0)
        window = window.reshape(-1, members)
        partial = partial_stress(src, dst, place, near_blocks, window, far_u, coeffs)
        partial = partial.reshape(CORES, chips, elems, members)
        joined = [partial[0, s] + core_swap(partial[1, s]) for s in range(chips)]
        total = joined[0]
        for s in range(1, chips):
            total = total + chip_shift(joined[s].astype(jnp.bfloat16), s).astype(jnp.float32)
        return total

    velocity_one, drift_one = slip_rates(section_stress(slip), state, load, friction_a)
    slip_mid = slip + STEP * velocity_one
    state_mid = state + STEP * drift_one
    velocity_two, drift_two = slip_rates(section_stress(slip_mid), state_mid, load, friction_a)
    slip_next = slip + 0.5 * STEP * (velocity_one + velocity_two)
    state_next = state + 0.5 * STEP * (drift_one + drift_two)
    return (slip_next, state_next)


def solution(mesh):
    placed = (
        P(("grp", "clu", "row"), None),
        P(("grp", "clu", "row"), None),
        P(("grp", "clu", "row"), None),
        P(("grp", "clu", "row")),
        P(("grp", "clu", "row"), None, None),
        P(("grp", "clu", "row"), None),
        P(("grp", "clu", "row"), None, None, None),
        P(("grp", "clu", "row"), None, None, None),
        P(("grp", "clu", "row"), None),
    )
    return jax.shard_map(
        body,
        mesh=mesh,
        in_specs=placed,
        out_specs=(P(("grp", "clu", "row"), None), P(("grp", "clu", "row"), None)),
        check_vma=False,
    )
```

time: 229 us -> 75.1 us (0.33)
  blocking collectives: 52.1 us -> 0 us
  local copies, waits for them, and re-layouts: 44.6 us -> 0.32 us
  matrix products: 41.4 us -> 0.45 us
  waiting for transfers between devices: 53.5 us -> 23.1 us
  starting transfers between devices: 10.7 us -> 35.1 us
  between operations: 14.2 us -> 1.07 us
  Pallas kernels: 0 us -> 7.96 us
  other arithmetic: 11.8 us -> 6.81 us
    all_gather x4 -> x0, blocking collectives: 52.1 us -> none  [the longest x2 36.7 us: far_stress(): piece = lax.all_gather(own_half, 'clu', axis=0, tiled=True)]
    reduce_scatter x2 -> x0, waiting for transfers between devices: 46.9 us -> none  [section_stress(): lax.psum_scatter(partial_value, 'row', scatter_dimension=0, tiled=True)]
    dot_general x6 -> x2, matrix products: 41.4 us -> 0.45 us  [section_stress(): jnp.dot(held, half, preferred_element_type=jnp.float32).astype(jnp.bfloat16)]
    dot_general x4 -> x0, local copies, waits for them, and re-layouts: 31.1 us -> none  [the longest x2 30.5 us: near_stress(): jnp.einsum('kij,kjm->kim', near_blocks, picked, preferred_element_type=jn...]
    ppermute x4 -> x25, starting transfers between devices: 10.6 us -> 35.1 us  [the longest x9 15.8 us: group_shift(): lax.ppermute(array, 'clu', [(i, (i + step) % groups) for i in range(group...]
    ppermute x4 -> x25, waiting for transfers between devices: 6.61 us -> 23.1 us  [the longest x4 9.06 us: chip_shift(): return lax.ppermute(array, 'row', pairs)]
    gather x2 -> x0, local copies, waits for them, and re-layouts: 12.5 us -> none  [near_stress(): picked = jnp.take(tiles, near_pairs[:, 1] - first + REACH, axis=0)]
    pallas_call x0 -> x2, Pallas kernels: none -> 7.96 us  [partial_stress(): pl.pallas_call(functools.partial(stress_kernel, leaf), out_shape=jax.Shap...]
  transfers between devices with their start and end apart: 6 -> 25, of which waited for: 4 -> 13; matrix products, arithmetic and copies ran while one was open for 2% -> 4% of each run, Pallas kernels for 0% -> 0%
where the time goes in v1:
time: 75.1 us; the launch traced here: 74.8 us
  starting transfers between devices  35.1 us (47%)
  waiting for transfers between devices  23.1 us (31%)
  Pallas kernels  7.96 us (11%)
  other arithmetic  6.81 us (9%)
  between operations  1.07 us (1%)
    ppermute x9, starting transfers between devices, group_shift(): lax.ppermute(array, 'clu', [(i, (i + step) % groups) for i in range(group...  15.8 us
    ppermute x4, starting transfers between devices, group_next(): return lax.ppermute(array, 'clu', pairs)  11.7 us
    ppermute x4, waiting for transfers between devices, chip_shift(): return lax.ppermute(array, 'row', pairs)  9.06 us
    pallas_call x2, Pallas kernels, partial_stress(): pl.pallas_call(functools.partial(stress_kernel, leaf), out_shape=jax.Shap...  7.96 us
    ppermute x4, starting transfers between devices, chip_shift(): return lax.ppermute(array, 'row', pairs)  6.15 us
    ppermute x8, waiting for transfers between devices, core_swap(): return lax.ppermute(array, 'row', [(i, i ^ 1) for i in range(devices)])  4.95 us
    ppermute x4, waiting for transfers between devices, group_next(): return lax.ppermute(array, 'clu', pairs)  4.68 us
    ppermute x9, waiting for transfers between devices, group_shift(): lax.ppermute(array, 'clu', [(i, (i + step) % groups) for i in range(group...  4.44 us
  transfers between devices with their start and end apart: 25, of which 13 were waited for; matrix products, arithmetic and copies ran while one was open for 4% of the time, Pallas kernels for 0%

profile of v1, /device:TPU:0, one launch (start us, length us, event | category | flops | bytes accessed | tf_op | source)
XLA Modules:
  0.0 74.8 jit_solution(18053324130156569938)
XLA Ops:
  0.7 0.8 %iota_compare_fusion = pred[4,4,32]{2,1,0:T(4,128)(4,1)S(1)} fusion(s32[4,4]{1,0:T(4,128)} %param.17), kind=kLoop, calls=%fused_computation.82 | loop fusion | flops 512 | bytes 576 | tf_op jit(solution)/shard_map/lt | solution.py:129
  1.4 1.1 %broadcast_select_fusion = bf16[4,4,32,256]{3,2,1,0:T(8,128)(2,1)S(1)} fusion(bf16[4,4,32,256]{3,2,1,0:T(8,128)(2,1)} %param.16, pred[4,4,32]{2,1,0:T(4,128)(4,1)S(1)} %iota_compare_fusion), kind=kLoop, calls=%fused_computation.57 | loop fusion | flops 131072 | bytes 524800 | tf_op jit(solution)/shard_map/jit(_where)/select_n | solution.py:129
  2.6 5.1 %collective-permute-start.7 = (bf16[4,32,256]{2,1,0:T(8,128)(2,1)S(1)}, bf16[4,32,256]{2,1,0:T(8,128)(2,1)S(1)}, u32[]{:S(2)}, u32[]{:S(2)}) collective-permute-start(bf16[4,32,256]{2,1,0:T(8,128)(2,1)S(1)} %get-tuple-element.24), channel_id=1, source_target_pairs={{0,12},{4,0},{8,4},{12,8},{1,13},{5,1},{9,5},{13,9},{2,14},{6,2},{... | collective-permute-start | bytes 196616 | tf_op jit(solution)/shard_map/ppermute | solution.py:29
  7.7 0.0 collective-permute-start.6
  7.7 1.0 %collective-permute-start.5 = (bf16[4,32,256]{2,1,0:T(8,128)(2,1)S(1)}, bf16[4,32,256]{2,1,0:T(8,128)(2,1)S(1)}, u32[]{:S(2)}, u32[]{:S(2)}) collective-permute-start(bf16[4,32,256]{2,1,0:T(8,128)(2,1)S(1)} %get-tuple-element.26), channel_id=1, source_target_pairs={{0,4},{4,8},{8,12},{12,0},{1,5},{5,9},{9,13},{13,1},{2,6},{6,10},{... | collective-permute-start | bytes 196616 | tf_op jit(solution)/shard_map/ppermute | solution.py:29
  8.7 1.0 %constant_dynamic-update-slice_fusion.5 = (bf16[8,256,256]{2,1,0:T(8,128)(2,1)S(1)}, bf16[256,256]{1,0:T(8,128)(2,1)S(1)}) fusion(f32[256,256]{1,0:T(8,128)} %param.9), kind=kLoop, calls=%fused_computation.75 | loop fusion | flops 65535 | bytes 524288
  9.7 1.6 %collective-permute-start = (bf16[256,256]{1,0:T(8,128)(2,1)S(1)}, bf16[256,256]{1,0:T(8,128)(2,1)S(1)}, u32[]{:S(2)}, u32[]{:S(2)}) collective-permute-start(bf16[256,256]{1,0:T(8,128)(2,1)S(1)} %get-tuple-element.8), channel_id=1, source_target_pairs={{0,2},{1,3},{2,0},{3,1},{4,6},{5,7},{6,4},{7,5},{8,10},{9,11},{10,... | collective-permute-start | bytes 393224 | tf_op jit(solution)/shard_map/ppermute | solution.py:24
  11.3 0.9 %fusion.33 = (s32[112]{0:T(128)S(1)}, s32[112]{0:T(128)S(1)}) fusion(s32[112,2]{0,1:T(2,128)} %param.14, s32[]{:T(128)} %select_n.117, s32[]{:T(128)} %select_n.116, s32[]{:T(128)S(6)} %mul.49), kind=kLoop, calls=%fused_computation.115 | loop fusion | flops 13664 | bytes 1804 | tf_op jit(solution)/shard_map/add | solution.py:125
  12.1 0.1 pad_add_fusion.place
  12.2 0.0 collective-permute-done.7
  12.2 2.0 %collective-permute-done.6 = bf16[4,32,256]{2,1,0:T(8,128)(2,1)S(1)} collective-permute-done((bf16[4,32,256]{2,1,0:T(8,128)(2,1)S(1)}, bf16[4,32,256]{2,1,0:T(8,128)(2,1)S(1)}, u32[]{:S(2)}, u32[]{:S(2)}) %collective-permute-start.6) | collective-permute-done | bytes 65568 | tf_op jit(solution)/shard_map/ppermute | solution.py:29
  14.2 0.0 collective-permute-done.5
  14.2 0.2 convolution_convert_fusion.1
  14.5 0.6 collective-permute-start.10
  15.1 1.9 %collective-permute-start.9 = (bf16[4,32,256]{2,1,0:T(8,128)(2,1)S(1)}, bf16[4,32,256]{2,1,0:T(8,128)(2,1)S(1)}, u32[]{:S(2)}, u32[]{:S(2)}) collective-permute-start(bf16[4,32,256]{2,1,0:T(8,128)(2,1)S(1)} %bitcast.159), channel_id=1, source_target_pairs={{0,8},{4,12},{8,0},{12,4},{1,9},{5,13},{9,1},{13,5},{2,10},{6,14},... | collective-permute-start | bytes 196616 | tf_op jit(solution)/shard_map/ppermute | solution.py:29
  17.0 2.2 %collective-permute-start.8 = (bf16[4,32,256]{2,1,0:T(8,128)(2,1)S(1)}, bf16[4,32,256]{2,1,0:T(8,128)(2,1)S(1)}, u32[]{:S(2)}, u32[]{:S(2)}) collective-permute-start(bf16[4,32,256]{2,1,0:T(8,128)(2,1)S(1)} %bitcast.157), channel_id=1, source_target_pairs={{0,12},{4,0},{8,4},{12,8},{1,13},{5,1},{9,5},{13,9},{2,14},{6,2},{... | collective-permute-start | bytes 196616 | tf_op jit(solution)/shard_map/ppermute | solution.py:29
  19.2 0.0 collective-permute-done
  19.2 0.1 fusion.30
  19.3 1.3 %collective-permute-start.2 = (bf16[256,256]{1,0:T(8,128)(2,1)S(1)}, bf16[256,256]{1,0:T(8,128)(2,1)S(1)}, u32[]{:S(2)}, u32[]{:S(2)}) collective-permute-start(bf16[256,256]{1,0:T(8,128)(2,1)S(1)} %get-tuple-element.27), channel_id=1, source_target_pairs={{4,0},{8,4},{12,8},{5,1},{9,5},{13,9},{6,2},{10,6},{14,10},{7,3},{... | collective-permute-start | bytes 393224 | tf_op jit(solution)/shard_map/ppermute | solution.py:35
  20.6 4.6 %collective-permute-start.1 = (bf16[256,256]{1,0:T(8,128)(2,1)S(1)}, bf16[256,256]{1,0:T(8,128)(2,1)S(1)}, u32[]{:S(2)}, u32[]{:S(2)}) collective-permute-start(bf16[256,256]{1,0:T(8,128)(2,1)S(1)} %get-tuple-element.28), channel_id=1, source_target_pairs={{0,4},{4,8},{8,12},{1,5},{5,9},{9,13},{2,6},{6,10},{10,14},{3,7},{... | collective-permute-start | bytes 393224 | tf_op jit(solution)/shard_map/ppermute | solution.py:35
  25.3 0.0 collective-permute-done.10
  25.3 0.1 collective-permute-start.3
  25.4 0.0 collective-permute-done.9
  25.4 0.8 %collective-permute-done.2 = bf16[256,256]{1,0:T(8,128)(2,1)S(1)} collective-permute-done((bf16[256,256]{1,0:T(8,128)(2,1)S(1)}, bf16[256,256]{1,0:T(8,128)(2,1)S(1)}, u32[]{:S(2)}, u32[]{:S(2)}) %collective-permute-start.2) | collective-permute-done | bytes 131104 | tf_op jit(solution)/shard_map/ppermute | solution.py:35
  26.2 1.5 %collective-permute-done.1 = bf16[256,256]{1,0:T(8,128)(2,1)S(1)} collective-permute-done((bf16[256,256]{1,0:T(8,128)(2,1)S(1)}, bf16[256,256]{1,0:T(8,128)(2,1)S(1)}, u32[]{:S(2)}, u32[]{:S(2)}) %collective-permute-start.1) | collective-permute-done | bytes 131104 | tf_op jit(solution)/shard_map/ppermute | solution.py:35
  27.7 0.1 collective-permute-start.4
  27.9 1.4 %collective-permute-done.4 = bf16[2,256,256]{2,1,0:T(8,128)(2,1)S(1)} collective-permute-done((bf16[2,256,256]{2,1,0:T(8,128)(2,1)S(1)}, bf16[2,256,256]{2,1,0:T(8,128)(2,1)S(1)}, u32[]{:S(2)}, u32[]{:S(2)}) %collective-permute-start.4) | collective-permute-done | bytes 262176 | tf_op jit(solution)/shard_map/ppermute | solution.py:18
  29.4 0.0 copy-start.5
  29.4 0.0 copy-start.2
  29.4 0.0 copy-start.3
  29.4 0.0 copy-start.4
  29.4 4.0 %shard_map.104 = f32[1024,256]{1,0:T(8,128)S(1)} custom-call(s32[112]{0:T(128)S(1)} %get-tuple-element.30.src, s32[112]{0:T(128)S(1)} %get-tuple-element.29.dst, s32[3]{0:T(128)S(1)} %pad_add_fusion.place, bf16[112,128,128]{2,1,0:T(8,128)(2,1)S(1)} %copy-done, bf16[2048,256]{1,0:T(8,128)(2,1)S(1)} %bitcast.137, bf16[4,4,32,256]{3,2,1,0:T(8,128)(2,1)S(1)} %copy-done.1, ...), custom_call_target="tpu_custom_call" | custom-call | flops 1006632960 | bytes 5767168 | tf_op jit(solution)/shard_map/pallas_call | solution.py:77
  33.5 0.2 collective-permute-start.12
  33.7 0.4 collective-permute-start.11
  34.1 1.0 %collective-permute-done.12 = f32[256,256]{1,0:T(8,128)S(1)} collective-permute-done((f32[256,256]{1,0:T(8,128)S(1)}, f32[256,256]{1,0:T(8,128)S(1)}, u32[]{:S(2)}, u32[]{:S(2)}) %collective-permute-start.12) | collective-permute-done | bytes 262176 | tf_op jit(solution)/shard_map/ppermute | solution.py:18
  35.1 1.6 %collective-permute-start.13 = (bf16[256,256]{1,0:T(8,128)(2,1)S(1)}, bf16[256,256]{1,0:T(8,128)(2,1)S(1)}, u32[]{:S(2)}, u32[]{:S(2)}) collective-permute-start(bf16[256,256]{1,0:T(8,128)(2,1)S(1)} %fusion.18), channel_id=1, source_target_pairs={{0,2},{1,3},{2,0},{3,1},{4,6},{5,7},{6,4},{7,5},{8,10},{9,11},{10,... | collective-permute-start | bytes 393224 | tf_op jit(solution)/shard_map/ppermute | solution.py:24
  36.7 0.0 collective-permute-done.11
  36.7 4.0 %collective-permute-done.13 = bf16[256,256]{1,0:T(8,128)(2,1)S(1)} collective-permute-done((bf16[256,256]{1,0:T(8,128)(2,1)S(1)}, bf16[256,256]{1,0:T(8,128)(2,1)S(1)}, u32[]{:S(2)}, u32[]{:S(2)}) %collective-permute-start.13) | collective-permute-done | bytes 131104 | tf_op jit(solution)/shard_map/ppermute | solution.py:24
  40.8 0.4 constant_dynamic-update-slice_fusion.11
  41.2 0.2 convolution_convert_fusion
  41.4 2.5 %collective-permute-start.21 = (bf16[4,32,256]{2,1,0:T(8,128)(2,1)S(1)}, bf16[4,32,256]{2,1,0:T(8,128)(2,1)S(1)}, u32[]{:S(2)}, u32[]{:S(2)}) collective-permute-start(bf16[4,32,256]{2,1,0:T(8,128)(2,1)S(1)} %bitcast.167), channel_id=1, source_target_pairs={{0,4},{4,8},{8,12},{12,0},{1,5},{5,9},{9,13},{13,1},{2,6},{6,10},{... | collective-permute-start | bytes 196616 | tf_op jit(solution)/shard_map/ppermute | solution.py:29
  43.9 1.1 %collective-permute-start.20 = (bf16[4,32,256]{2,1,0:T(8,128)(2,1)S(1)}, bf16[4,32,256]{2,1,0:T(8,128)(2,1)S(1)}, u32[]{:S(2)}, u32[]{:S(2)}) collective-permute-start(bf16[4,32,256]{2,1,0:T(8,128)(2,1)S(1)} %bitcast.165), channel_id=1, source_target_pairs={{0,8},{4,12},{8,0},{12,4},{1,9},{5,13},{9,1},{13,5},{2,10},{6,14},... | collective-permute-start | bytes 196616 | tf_op jit(solution)/shard_map/ppermute | solution.py:29
  45.1 1.3 %collective-permute-start.19 = (bf16[4,32,256]{2,1,0:T(8,128)(2,1)S(1)}, bf16[4,32,256]{2,1,0:T(8,128)(2,1)S(1)}, u32[]{:S(2)}, u32[]{:S(2)}) collective-permute-start(bf16[4,32,256]{2,1,0:T(8,128)(2,1)S(1)} %bitcast.163), channel_id=1, source_target_pairs={{0,12},{4,0},{8,4},{12,8},{1,13},{5,1},{9,5},{13,9},{2,14},{6,2},{... | collective-permute-start | bytes 196616 | tf_op jit(solution)/shard_map/ppermute | solution.py:29
  46.4 1.5 %collective-permute-start.14 = (bf16[256,256]{1,0:T(8,128)(2,1)S(1)}, bf16[256,256]{1,0:T(8,128)(2,1)S(1)}, u32[]{:S(2)}, u32[]{:S(2)}) collective-permute-start(bf16[256,256]{1,0:T(8,128)(2,1)S(1)} %get-tuple-element.5), channel_id=1, source_target_pairs={{0,2},{1,3},{2,0},{3,1},{4,6},{5,7},{6,4},{7,5},{8,10},{9,11},{10,... | collective-permute-start | bytes 393224 | tf_op jit(solution)/shard_map/ppermute | solution.py:24
  47.9 0.0 collective-permute-done.21
  47.9 2.5 %collective-permute-done.20 = bf16[4,32,256]{2,1,0:T(8,128)(2,1)S(1)} collective-permute-done((bf16[4,32,256]{2,1,0:T(8,128)(2,1)S(1)}, bf16[4,32,256]{2,1,0:T(8,128)(2,1)S(1)}, u32[]{:S(2)}, u32[]{:S(2)}) %collective-permute-start.20) | collective-permute-done | bytes 65568 | tf_op jit(solution)/shard_map/ppermute | solution.py:29
  50.3 0.0 collective-permute-done.19
  50.4 1.0 %collective-permute-done.14 = bf16[256,256]{1,0:T(8,128)(2,1)S(1)} collective-permute-done((bf16[256,256]{1,0:T(8,128)(2,1)S(1)}, bf16[256,256]{1,0:T(8,128)(2,1)S(1)}, u32[]{:S(2)}, u32[]{:S(2)}) %collective-permute-start.14) | collective-permute-done | bytes 131104 | tf_op jit(solution)/shard_map/ppermute | solution.py:24
  51.4 0.1 fusion.26
  51.5 1.3 %collective-permute-start.16 = (bf16[256,256]{1,0:T(8,128)(2,1)S(1)}, bf16[256,256]{1,0:T(8,128)(2,1)S(1)}, u32[]{:S(2)}, u32[]{:S(2)}) collective-permute-start(bf16[256,256]{1,0:T(8,128)(2,1)S(1)} %get-tuple-element.17), channel_id=1, source_target_pairs={{4,0},{8,4},{12,8},{5,1},{9,5},{13,9},{6,2},{10,6},{14,10},{7,3},{... | collective-permute-start | bytes 393224 | tf_op jit(solution)/shard_map/ppermute | solution.py:35
  52.8 4.6 %collective-permute-start.15 = (bf16[256,256]{1,0:T(8,128)(2,1)S(1)}, bf16[256,256]{1,0:T(8,128)(2,1)S(1)}, u32[]{:S(2)}, u32[]{:S(2)}) collective-permute-start(bf16[256,256]{1,0:T(8,128)(2,1)S(1)} %get-tuple-element.18), channel_id=1, source_target_pairs={{0,4},{4,8},{8,12},{1,5},{5,9},{9,13},{2,6},{6,10},{10,14},{3,7},{... | collective-permute-start | bytes 393224 | tf_op jit(solution)/shard_map/ppermute | solution.py:35
  57.4 0.1 collective-permute-start.17
  57.4 0.9 %collective-permute-done.16 = bf16[256,256]{1,0:T(8,128)(2,1)S(1)} collective-permute-done((bf16[256,256]{1,0:T(8,128)(2,1)S(1)}, bf16[256,256]{1,0:T(8,128)(2,1)S(1)}, u32[]{:S(2)}, u32[]{:S(2)}) %collective-permute-start.16) | collective-permute-done | bytes 131104 | tf_op jit(solution)/shard_map/ppermute | solution.py:35
  58.4 1.5 %collective-permute-done.15 = bf16[256,256]{1,0:T(8,128)(2,1)S(1)} collective-permute-done((bf16[256,256]{1,0:T(8,128)(2,1)S(1)}, bf16[256,256]{1,0:T(8,128)(2,1)S(1)}, u32[]{:S(2)}, u32[]{:S(2)}) %collective-permute-start.15) | collective-permute-done | bytes 131104 | tf_op jit(solution)/shard_map/ppermute | solution.py:35
  59.9 0.1 collective-permute-start.18
  60.0 1.4 %collective-permute-done.18 = bf16[2,256,256]{2,1,0:T(8,128)(2,1)S(1)} collective-permute-done((bf16[2,256,256]{2,1,0:T(8,128)(2,1)S(1)}, bf16[2,256,256]{2,1,0:T(8,128)(2,1)S(1)}, u32[]{:S(2)}, u32[]{:S(2)}) %collective-permute-start.18) | collective-permute-done | bytes 262176 | tf_op jit(solution)/shard_map/ppermute | solution.py:18
  61.5 3.9 %shard_map.105 = f32[1024,256]{1,0:T(8,128)S(1)} custom-call(s32[112]{0:T(128)S(1)} %get-tuple-element.30.src, s32[112]{0:T(128)S(1)} %get-tuple-element.29.dst, s32[3]{0:T(128)S(1)} %pad_add_fusion.place, bf16[112,128,128]{2,1,0:T(8,128)(2,1)S(1)} %copy-done, bf16[2048,256]{1,0:T(8,128)(2,1)S(1)} %bitcast.136, bf16[4,4,32,256]{3,2,1,0:T(8,128)(2,1)S(1)} %copy-done.1, ...), custom_call_target="tpu_custom_call" | custom-call | flops 1006632960 | bytes 5767168 | tf_op jit(solution)/shard_map/pallas_call | solution.py:77
  65.5 0.2 collective-permute-start.23
  65.7 0.4 collective-permute-start.22
  66.1 1.0 %collective-permute-done.23 = f32[256,256]{1,0:T(8,128)S(1)} collective-permute-done((f32[256,256]{1,0:T(8,128)S(1)}, f32[256,256]{1,0:T(8,128)S(1)}, u32[]{:S(2)}, u32[]{:S(2)}) %collective-permute-start.23) | collective-permute-done | bytes 262176 | tf_op jit(solution)/shard_map/ppermute | solution.py:18
  67.1 1.6 %collective-permute-start.24 = (bf16[256,256]{1,0:T(8,128)(2,1)S(1)}, bf16[256,256]{1,0:T(8,128)(2,1)S(1)}, u32[]{:S(2)}, u32[]{:S(2)}) collective-permute-start(bf16[256,256]{1,0:T(8,128)(2,1)S(1)} %fusion.12), channel_id=1, source_target_pairs={{0,2},{1,3},{2,0},{3,1},{4,6},{5,7},{6,4},{7,5},{8,10},{9,11},{10,... | collective-permute-start | bytes 393224 | tf_op jit(solution)/shard_map/ppermute | solution.py:24
  68.7 4.0 %collective-permute-done.24 = bf16[256,256]{1,0:T(8,128)(2,1)S(1)} collective-permute-done((bf16[256,256]{1,0:T(8,128)(2,1)S(1)}, bf16[256,256]{1,0:T(8,128)(2,1)S(1)}, u32[]{:S(2)}, u32[]{:S(2)}) %collective-permute-start.24) | collective-permute-done | bytes 131104 | tf_op jit(solution)/shard_map/ppermute | solution.py:24
  72.7 1.3 %fusion.10 = (f32[256,256]{1,0:T(8,128)}, f32[256,256]{1,0:T(8,128)S(1)}) fusion(f32[256,256]{1,0:T(8,128)S(1)} %copy-done.4, f32[256,256]{1,0:T(8,128)S(1)} %get-tuple-element.6, f32[256]{0:T(256)S(1)} %broadcast_multiply_fusion, f32[256,256]{1,0:T(8,128)S(1)} %copy-done.3, bf16[256,256]{1,0:T(8,128)(2,1)S(1)} %collective-permute-done.24, ...), kind=kLoop, calls=%fused_computation.26 | loop fusion | flops 2162688 | bytes 1968128 | tf_op jit(solution)/shard_map/add | solution.py:163
  74.1 0.8 %multiply_add_fusion = f32[256,256]{1,0:T(8,128)} fusion(f32[256,256]{1,0:T(8,128)S(1)} %copy-done.2, f32[256,256]{1,0:T(8,128)S(1)} %get-tuple-element.6, f32[256,256]{1,0:T(8,128)S(1)} %get-tuple-element.3), kind=kLoop, calls=%fused_computation.52 | loop fusion | flops 196608 | bytes 1048576 | tf_op jit(solution)/shard_map/add | solution.py:162
  (37 shorter events, 0.6 us)
Async XLA Ops:
  1.4 27.9 %copy-start.1 = (bf16[4,4,32,256]{3,2,1,0:T(8,128)(2,1)S(1)}, bf16[4,4,32,256]{3,2,1,0:T(8,128)(2,1)}, u32[]{:S(2)}) copy-start(bf16[4,4,32,256]{3,2,1,0:T(8,128)(2,1)} %far_u.3) | copy-start | bytes 786436
  2.6 9.6 %collective-permute-start.7 = (bf16[4,32,256]{2,1,0:T(8,128)(2,1)S(1)}, bf16[4,32,256]{2,1,0:T(8,128)(2,1)S(1)}, u32[]{:S(2)}, u32[]{:S(2)}) collective-permute-start(bf16[4,32,256]{2,1,0:T(8,128)(2,1)S(1)} %get-tuple-element.24), channel_id=1, source_target_pairs={{0,12},{4,0},{8,4},{12,8},{1,13},{5,1},{9,5},{13,9},{2,14},{6,2},{... | collective-permute-start | bytes 196616 | tf_op jit(solution)/shard_map/ppermute | solution.py:29
  7.7 6.5 %collective-permute-start.6 = (bf16[4,32,256]{2,1,0:T(8,128)(2,1)S(1)}, bf16[4,32,256]{2,1,0:T(8,128)(2,1)S(1)}, u32[]{:S(2)}, u32[]{:S(2)}) collective-permute-start(bf16[4,32,256]{2,1,0:T(8,128)(2,1)S(1)} %get-tuple-element.25), channel_id=1, source_target_pairs={{0,8},{4,12},{8,0},{12,4},{1,9},{5,13},{9,1},{13,5},{2,10},{6,14},... | collective-permute-start | bytes 196616 | tf_op jit(solution)/shard_map/ppermute | solution.py:29
  7.7 6.5 %collective-permute-start.5 = (bf16[4,32,256]{2,1,0:T(8,128)(2,1)S(1)}, bf16[4,32,256]{2,1,0:T(8,128)(2,1)S(1)}, u32[]{:S(2)}, u32[]{:S(2)}) collective-permute-start(bf16[4,32,256]{2,1,0:T(8,128)(2,1)S(1)} %get-tuple-element.26), channel_id=1, source_target_pairs={{0,4},{4,8},{8,12},{12,0},{1,5},{5,9},{9,13},{13,1},{2,6},{6,10},{... | collective-permute-start | bytes 196616 | tf_op jit(solution)/shard_map/ppermute | solution.py:29
  9.7 9.5 %collective-permute-start = (bf16[256,256]{1,0:T(8,128)(2,1)S(1)}, bf16[256,256]{1,0:T(8,128)(2,1)S(1)}, u32[]{:S(2)}, u32[]{:S(2)}) collective-permute-start(bf16[256,256]{1,0:T(8,128)(2,1)S(1)} %get-tuple-element.8), channel_id=1, source_target_pairs={{0,2},{1,3},{2,0},{3,1},{4,6},{5,7},{6,4},{7,5},{8,10},{9,11},{10,... | collective-permute-start | bytes 393224 | tf_op jit(solution)/shard_map/ppermute | solution.py:24
  11.3 18.1 %copy-start = (bf16[112,128,128]{2,1,0:T(8,128)(2,1)S(1)}, bf16[112,128,128]{2,1,0:T(8,128)(2,1)}, u32[]{:S(2)}) copy-start(bf16[112,128,128]{2,1,0:T(8,128)(2,1)} %blocks.3) | copy-start | bytes 11010052
  14.5 10.8 %collective-permute-start.10 = (bf16[4,32,256]{2,1,0:T(8,128)(2,1)S(1)}, bf16[4,32,256]{2,1,0:T(8,128)(2,1)S(1)}, u32[]{:S(2)}, u32[]{:S(2)}) collective-permute-start(bf16[4,32,256]{2,1,0:T(8,128)(2,1)S(1)} %bitcast.162), channel_id=1, source_target_pairs={{0,4},{4,8},{8,12},{12,0},{1,5},{5,9},{9,13},{13,1},{2,6},{6,10},{... | collective-permute-start | bytes 196616 | tf_op jit(solution)/shard_map/ppermute | solution.py:29
  15.1 10.3 %collective-permute-start.9 = (bf16[4,32,256]{2,1,0:T(8,128)(2,1)S(1)}, bf16[4,32,256]{2,1,0:T(8,128)(2,1)S(1)}, u32[]{:S(2)}, u32[]{:S(2)}) collective-permute-start(bf16[4,32,256]{2,1,0:T(8,128)(2,1)S(1)} %bitcast.159), channel_id=1, source_target_pairs={{0,8},{4,12},{8,0},{12,4},{1,9},{5,13},{9,1},{13,5},{2,10},{6,14},... | collective-permute-start | bytes 196616 | tf_op jit(solution)/shard_map/ppermute | solution.py:29
  17.0 8.4 %collective-permute-start.8 = (bf16[4,32,256]{2,1,0:T(8,128)(2,1)S(1)}, bf16[4,32,256]{2,1,0:T(8,128)(2,1)S(1)}, u32[]{:S(2)}, u32[]{:S(2)}) collective-permute-start(bf16[4,32,256]{2,1,0:T(8,128)(2,1)S(1)} %bitcast.157), channel_id=1, source_target_pairs={{0,12},{4,0},{8,4},{12,8},{1,13},{5,1},{9,5},{13,9},{2,14},{6,2},{... | collective-permute-start | bytes 196616 | tf_op jit(solution)/shard_map/ppermute | solution.py:29
  19.3 6.9 %collective-permute-start.2 = (bf16[256,256]{1,0:T(8,128)(2,1)S(1)}, bf16[256,256]{1,0:T(8,128)(2,1)S(1)}, u32[]{:S(2)}, u32[]{:S(2)}) collective-permute-start(bf16[256,256]{1,0:T(8,128)(2,1)S(1)} %get-tuple-element.27), channel_id=1, source_target_pairs={{4,0},{8,4},{12,8},{5,1},{9,5},{13,9},{6,2},{10,6},{14,10},{7,3},{... | collective-permute-start | bytes 393224 | tf_op jit(solution)/shard_map/ppermute | solution.py:35
  20.6 7.1 %collective-permute-start.1 = (bf16[256,256]{1,0:T(8,128)(2,1)S(1)}, bf16[256,256]{1,0:T(8,128)(2,1)S(1)}, u32[]{:S(2)}, u32[]{:S(2)}) collective-permute-start(bf16[256,256]{1,0:T(8,128)(2,1)S(1)} %get-tuple-element.28), channel_id=1, source_target_pairs={{0,4},{4,8},{8,12},{1,5},{5,9},{9,13},{2,6},{6,10},{10,14},{3,7},{... | collective-permute-start | bytes 393224 | tf_op jit(solution)/shard_map/ppermute | solution.py:35
  25.3 2.6 %collective-permute-start.3 = (bf16[2,256,256]{2,1,0:T(8,128)(2,1)S(1)}, bf16[2,256,256]{2,1,0:T(8,128)(2,1)S(1)}, u32[]{:S(2)}, u32[]{:S(2)}) collective-permute-start(bf16[2,256,256]{2,1,0:T(8,128)(2,1)S(1)} %pad_maximum_fusion), channel_id=1, source_target_pairs={{0,1},{1,0},{2,3},{3,2},{4,5},{5,4},{6,7},{7,6},{8,9},{9,8},{10,11... | collective-permute-start | bytes 786440 | tf_op jit(solution)/shard_map/ppermute | solution.py:18
  27.7 1.6 %collective-permute-start.4 = (bf16[2,256,256]{2,1,0:T(8,128)(2,1)S(1)}, bf16[2,256,256]{2,1,0:T(8,128)(2,1)S(1)}, u32[]{:S(2)}, u32[]{:S(2)}) collective-permute-start(bf16[2,256,256]{2,1,0:T(8,128)(2,1)S(1)} %pad_maximum_fusion.2), channel_id=1, source_target_pairs={{0,1},{1,0},{2,3},{3,2},{4,5},{5,4},{6,7},{7,6},{8,9},{9,8},{10,11... | collective-permute-start | bytes 786440 | tf_op jit(solution)/shard_map/ppermute | solution.py:18
  29.4 7.3 %copy-start.5 = (f32[256]{0:T(256)S(1)}, f32[256]{0:T(256)}, u32[]{:S(2)}) copy-start(f32[256]{0:T(256)} %param.12) | copy-start | bytes 3076
  29.4 11.4 %copy-start.2 = (f32[256,256]{1,0:T(8,128)S(1)}, f32[256,256]{1,0:T(8,128)}, u32[]{:S(2)}) copy-start(f32[256,256]{1,0:T(8,128)} %param.9) | copy-start | bytes 786436
  29.4 11.3 %copy-start.3 = (f32[256,256]{1,0:T(8,128)S(1)}, f32[256,256]{1,0:T(8,128)}, u32[]{:S(2)}) copy-start(f32[256,256]{1,0:T(8,128)} %param.11) | copy-start | bytes 786436
  29.4 11.3 %copy-start.4 = (f32[256,256]{1,0:T(8,128)S(1)}, f32[256,256]{1,0:T(8,128)}, u32[]{:S(2)}) copy-start(f32[256,256]{1,0:T(8,128)} %param.10) | copy-start | bytes 786436
  33.5 1.6 %collective-permute-start.12 = (f32[256,256]{1,0:T(8,128)S(1)}, f32[256,256]{1,0:T(8,128)S(1)}, u32[]{:S(2)}, u32[]{:S(2)}) collective-permute-start(f32[256,256]{1,0:T(8,128)S(1)} %get-tuple-element.12), channel_id=1, source_target_pairs={{0,1},{1,0},{2,3},{3,2},{4,5},{5,4},{6,7},{7,6},{8,9},{9,8},{10,11... | collective-permute-start | bytes 786440 | tf_op jit(solution)/shard_map/ppermute | solution.py:18
  33.7 3.0 %collective-permute-start.11 = (f32[256,256]{1,0:T(8,128)S(1)}, f32[256,256]{1,0:T(8,128)S(1)}, u32[]{:S(2)}, u32[]{:S(2)}) collective-permute-start(f32[256,256]{1,0:T(8,128)S(1)} %get-tuple-element.11), channel_id=1, source_target_pairs={{0,1},{1,0},{2,3},{3,2},{4,5},{5,4},{6,7},{7,6},{8,9},{9,8},{10,11... | collective-permute-start | bytes 786440 | tf_op jit(solution)/shard_map/ppermute | solution.py:18
  35.1 5.6 %collective-permute-start.13 = (bf16[256,256]{1,0:T(8,128)(2,1)S(1)}, bf16[256,256]{1,0:T(8,128)(2,1)S(1)}, u32[]{:S(2)}, u32[]{:S(2)}) collective-permute-start(bf16[256,256]{1,0:T(8,128)(2,1)S(1)} %fusion.18), channel_id=1, source_target_pairs={{0,2},{1,3},{2,0},{3,1},{4,6},{5,7},{6,4},{7,5},{8,10},{9,11},{10,... | collective-permute-start | bytes 393224 | tf_op jit(solution)/shard_map/ppermute | solution.py:24
  41.4 6.4 %collective-permute-start.21 = (bf16[4,32,256]{2,1,0:T(8,128)(2,1)S(1)}, bf16[4,32,256]{2,1,0:T(8,128)(2,1)S(1)}, u32[]{:S(2)}, u32[]{:S(2)}) collective-permute-start(bf16[4,32,256]{2,1,0:T(8,128)(2,1)S(1)} %bitcast.167), channel_id=1, source_target_pairs={{0,4},{4,8},{8,12},{12,0},{1,5},{5,9},{9,13},{13,1},{2,6},{6,10},{... | collective-permute-start | bytes 196616 | tf_op jit(solution)/shard_map/ppermute | solution.py:29
  43.9 6.4 %collective-permute-start.20 = (bf16[4,32,256]{2,1,0:T(8,128)(2,1)S(1)}, bf16[4,32,256]{2,1,0:T(8,128)(2,1)S(1)}, u32[]{:S(2)}, u32[]{:S(2)}) collective-permute-start(bf16[4,32,256]{2,1,0:T(8,128)(2,1)S(1)} %bitcast.165), channel_id=1, source_target_pairs={{0,8},{4,12},{8,0},{12,4},{1,9},{5,13},{9,1},{13,5},{2,10},{6,14},... | collective-permute-start | bytes 196616 | tf_op jit(solution)/shard_map/ppermute | solution.py:29
  45.1 5.2 %collective-permute-start.19 = (bf16[4,32,256]{2,1,0:T(8,128)(2,1)S(1)}, bf16[4,32,256]{2,1,0:T(8,128)(2,1)S(1)}, u32[]{:S(2)}, u32[]{:S(2)}) collective-permute-start(bf16[4,32,256]{2,1,0:T(8,128)(2,1)S(1)} %bitcast.163), channel_id=1, source_target_pairs={{0,12},{4,0},{8,4},{12,8},{1,13},{5,1},{9,5},{13,9},{2,14},{6,2},{... | collective-permute-start | bytes 196616 | tf_op jit(solution)/shard_map/ppermute | solution.py:29
  46.4 5.0 %collective-permute-start.14 = (bf16[256,256]{1,0:T(8,128)(2,1)S(1)}, bf16[256,256]{1,0:T(8,128)(2,1)S(1)}, u32[]{:S(2)}, u32[]{:S(2)}) collective-permute-start(bf16[256,256]{1,0:T(8,128)(2,1)S(1)} %get-tuple-element.5), channel_id=1, source_target_pairs={{0,2},{1,3},{2,0},{3,1},{4,6},{5,7},{6,4},{7,5},{8,10},{9,11},{10,... | collective-permute-start | bytes 393224 | tf_op jit(solution)/shard_map/ppermute | solution.py:24
  51.5 6.9 %collective-permute-start.16 = (bf16[256,256]{1,0:T(8,128)(2,1)S(1)}, bf16[256,256]{1,0:T(8,128)(2,1)S(1)}, u32[]{:S(2)}, u32[]{:S(2)}) collective-permute-start(bf16[256,256]{1,0:T(8,128)(2,1)S(1)} %get-tuple-element.17), channel_id=1, source_target_pairs={{4,0},{8,4},{12,8},{5,1},{9,5},{13,9},{6,2},{10,6},{14,10},{7,3},{... | collective-permute-start | bytes 393224 | tf_op jit(solution)/shard_map/ppermute | solution.py:35
  52.8 7.1 %collective-permute-start.15 = (bf16[256,256]{1,0:T(8,128)(2,1)S(1)}, bf16[256,256]{1,0:T(8,128)(2,1)S(1)}, u32[]{:S(2)}, u32[]{:S(2)}) collective-permute-start(bf16[256,256]{1,0:T(8,128)(2,1)S(1)} %get-tuple-element.18), channel_id=1, source_target_pairs={{0,4},{4,8},{8,12},{1,5},{5,9},{9,13},{2,6},{6,10},{10,14},{3,7},{... | collective-permute-start | bytes 393224 | tf_op jit(solution)/shard_map/ppermute | solution.py:35
  57.4 2.6 %collective-permute-start.17 = (bf16[2,256,256]{2,1,0:T(8,128)(2,1)S(1)}, bf16[2,256,256]{2,1,0:T(8,128)(2,1)S(1)}, u32[]{:S(2)}, u32[]{:S(2)}) collective-permute-start(bf16[2,256,256]{2,1,0:T(8,128)(2,1)S(1)} %pad_maximum_fusion.1), channel_id=1, source_target_pairs={{0,1},{1,0},{2,3},{3,2},{4,5},{5,4},{6,7},{7,6},{8,9},{9,8},{10,11... | collective-permute-start | bytes 786440 | tf_op jit(solution)/shard_map/ppermute | solution.py:18
  59.9 1.6 %collective-permute-start.18 = (bf16[2,256,256]{2,1,0:T(8,128)(2,1)S(1)}, bf16[2,256,256]{2,1,0:T(8,128)(2,1)S(1)}, u32[]{:S(2)}, u32[]{:S(2)}) collective-permute-start(bf16[2,256,256]{2,1,0:T(8,128)(2,1)S(1)} %pad_maximum_fusion.5), channel_id=1, source_target_pairs={{0,1},{1,0},{2,3},{3,2},{4,5},{5,4},{6,7},{7,6},{8,9},{9,8},{10,11... | collective-permute-start | bytes 786440 | tf_op jit(solution)/shard_map/ppermute | solution.py:18
  65.5 1.6 %collective-permute-start.23 = (f32[256,256]{1,0:T(8,128)S(1)}, f32[256,256]{1,0:T(8,128)S(1)}, u32[]{:S(2)}, u32[]{:S(2)}) collective-permute-start(f32[256,256]{1,0:T(8,128)S(1)} %get-tuple-element.10), channel_id=1, source_target_pairs={{0,1},{1,0},{2,3},{3,2},{4,5},{5,4},{6,7},{7,6},{8,9},{9,8},{10,11... | collective-permute-start | bytes 786440 | tf_op jit(solution)/shard_map/ppermute | solution.py:18
  65.7 3.0 %collective-permute-start.22 = (f32[256,256]{1,0:T(8,128)S(1)}, f32[256,256]{1,0:T(8,128)S(1)}, u32[]{:S(2)}, u32[]{:S(2)}) collective-permute-start(f32[256,256]{1,0:T(8,128)S(1)} %get-tuple-element.9), channel_id=1, source_target_pairs={{0,1},{1,0},{2,3},{3,2},{4,5},{5,4},{6,7},{7,6},{8,9},{9,8},{10,11... | collective-permute-start | bytes 786440 | tf_op jit(solution)/shard_map/ppermute | solution.py:18
  67.1 5.6 %collective-permute-start.24 = (bf16[256,256]{1,0:T(8,128)(2,1)S(1)}, bf16[256,256]{1,0:T(8,128)(2,1)S(1)}, u32[]{:S(2)}, u32[]{:S(2)}) collective-permute-start(bf16[256,256]{1,0:T(8,128)(2,1)S(1)} %fusion.12), channel_id=1, source_target_pairs={{0,2},{1,3},{2,0},{3,1},{4,6},{5,7},{6,4},{7,5},{8,10},{9,11},{10,... | collective-permute-start | bytes 393224 | tf_op jit(solution)/shard_map/ppermute | solution.py:24

commit v2 on v1

v2 whole, which is shorter than its diff:
```python
import functools

import jax
import jax.numpy as jnp
from jax import lax
from jax.experimental import pallas as pl
from jax.experimental.pallas import tpu as pltpu
from jax.sharding import PartitionSpec as P

REACH = 4
CORES = 2
STEP = 0.2
UNROLL = 16


def core_swap(array):
    devices = lax.axis_size("row")
    return lax.ppermute(array, "row", [(i, i ^ 1) for i in range(devices)])


def chip_shift(array, step):
    devices = lax.axis_size("row")
    pairs = [(i, (i + CORES * step) % devices) for i in range(devices)]
    return lax.ppermute(array, "row", pairs)


def group_shift(array, step):
    groups = lax.axis_size("clu")
    return lax.ppermute(array, "clu", [(i, (i + step) % groups) for i in range(groups)])


def gathered_blocks(leaf, inside, src, dst, blocks, window, out, block_list, row_list):
    count = blocks.shape[0]
    spare = out.shape[0] // leaf - 1

    def sort(j, found):
        block_list[found] = j
        row_list[found] = dst[j]
        return found + inside(src[j]).astype(jnp.int32)

    found = lax.fori_loop(0, count, sort, jnp.int32(0), unroll=8)
    for u in range(UNROLL):
        block_list[found + u] = 0
        row_list[found + u] = spare

    def step(i, carry):
        products = []
        for u in range(UNROLL):
            j = block_list[i * UNROLL + u]
            row = lax.rem(src[j], window.shape[0] // leaf)
            rows = window[pl.ds(pl.multiple_of(row * leaf, leaf), leaf), :]
            products.append(jnp.dot(blocks[j], rows, preferred_element_type=jnp.float32))
        for u in range(UNROLL):
            row = row_list[i * UNROLL + u]
            out[pl.ds(pl.multiple_of(row * leaf, leaf), leaf), :] += products[u]
        return carry

    lax.fori_loop(0, pl.cdiv(found, UNROLL), step, 0)


def inner_kernel(leaf, src, dst, blocks, window, out, block_list, row_list):
    out[...] = jnp.zeros_like(out)
    held = window.shape[0] // leaf
    gathered_blocks(leaf, lambda s: s < held, src, dst, blocks, window, out, block_list, row_list)


def outer_kernel(
    leaf, src, dst, place, blocks, window, far_u, coeffs, inner, out, block_list, row_list
):
    targets, groups, rank, elems = far_u.shape
    chips = targets // CORES
    group, chip, core = place[0], place[1], place[2]
    for other in range(CORES):
        for ahead in range(chips):
            target = lax.rem(chip + ahead, chips) * CORES + (core ^ other)
            bases = [far_u[target, lax.rem(group + s, groups)] for s in range(groups)]
            parts = [coeffs[s, target] for s in range(groups)]
            rows = pl.ds((other * chips + ahead) * elems, elems)
            out[rows, :] = inner[rows, :] + lax.dot_general(
                jnp.concatenate(bases, axis=0),
                jnp.concatenate(parts, axis=0),
                (((0,), (0,)), ((), ())),
                preferred_element_type=jnp.float32,
            )
    held = window.shape[0] // leaf
    gathered_blocks(leaf, lambda s: s >= held, src, dst, blocks, window, out, block_list, row_list)


VMEM = pl.BlockSpec(memory_space=pltpu.VMEM)
SMEM = pl.BlockSpec(memory_space=pltpu.SMEM)


def stress_call(kernel, rows, members, count, flops, nbytes, specs):
    return pl.pallas_call(
        kernel,
        out_shape=jax.ShapeDtypeStruct((rows, members), jnp.float32),
        in_specs=specs,
        out_specs=VMEM,
        scratch_shapes=[
            pltpu.SMEM((count + UNROLL,), jnp.int32),
            pltpu.SMEM((count + UNROLL,), jnp.int32),
        ],
        compiler_params=pltpu.CompilerParams(vmem_limit_bytes=40 * 1024 * 1024),
        cost_estimate=pl.CostEstimate(flops=flops, bytes_accessed=nbytes, transcendentals=0),
    )


def inner_stress(src, dst, blocks, window, rows):
    count, leaf, _ = blocks.shape
    members = window.shape[1]
    call = stress_call(
        functools.partial(inner_kernel, leaf),
        rows + leaf,
        members,
        count,
        2 * members * count * leaf * leaf,
        4 * rows * members,
        [SMEM, SMEM, VMEM, VMEM],
    )
    return call(src, dst, blocks, window)


def outer_stress(src, dst, place, blocks, window, far_u, coeffs, inner):
    targets, groups, rank, elems = far_u.shape
    count, leaf, _ = blocks.shape
    rows, members = inner.shape
    call = stress_call(
        functools.partial(outer_kernel, leaf),
        rows,
        members,
        count,
        members * (count * leaf * leaf + 2 * targets * groups * rank * elems),
        8 * rows * members,
        [SMEM, SMEM, SMEM, VMEM, VMEM, VMEM, VMEM, VMEM],
    )
    return call(src, dst, place, blocks, window, far_u, coeffs, inner)


def slip_rates(stress, state, load, friction_a):
    softness = friction_a[:, None]
    velocity = 2.0 * jnp.exp(-state / softness) * jnp.sinh((stress + load) / (2.0 * softness))
    speed = jnp.abs(velocity)
    drift = jnp.exp(-state) - speed / (1.0 + speed)
    return (velocity, drift)


def body(slip, state, load, friction_a, near_blocks, near_pairs, far_u, far_v, far_rank):
    elems, members = slip.shape
    leaf = near_blocks.shape[1]
    own = elems // leaf
    devices, groups = lax.axis_size("row"), lax.axis_size("clu")
    chips = devices // CORES
    clusters = devices * own
    assert REACH <= CORES * own
    group, row = lax.axis_index("clu"), lax.axis_index("row")
    chip, core = row // CORES, row % CORES
    place = jnp.stack([group, chip, core]).astype(jnp.int32)

    source = near_pairs[:, 1] - group * clusters
    before, after = source < 0, source >= clusters
    local = jnp.where(before, source + clusters, jnp.where(after, source - clusters, source))
    holder = local // own
    piece = jnp.where(
        before, (chip + 1) % chips, jnp.where(after, chip, (chip - holder // CORES + chips) % chips)
    )
    window_of = jnp.where(before | after, CORES, 0) + ((holder % CORES) ^ core)
    src = ((window_of * chips + piece) * own + local % own).astype(jnp.int32)
    target = near_pairs[:, 0] - group * clusters
    owner = target // own
    ahead = (owner // CORES - chip + chips) % chips
    dst = ((((owner % CORES) ^ core) * chips + ahead) * own + target % own).astype(jnp.int32)

    rank = far_u.shape[2]
    column = lax.broadcasted_iota(jnp.int32, (1, 1, rank, 1), 2)
    bases = jnp.where(column < far_rank[:, :, None, None], far_v, jnp.zeros_like(far_v))
    bases = [
        lax.dynamic_index_in_dim(bases, (group + s) % groups, axis=1, keepdims=False).reshape(
            devices * rank, elems
        )
        for s in range(groups)
    ]

    def with_mate(pieces):
        both = jnp.stack(pieces)
        return jnp.stack([both, core_swap(both)]).reshape(-1, members)

    def section_stress(field):
        half = field.astype(jnp.bfloat16)
        near = [half] + [chip_shift(half, s) for s in range(1, chips)]
        column = [half] + [group_shift(half, -s) for s in range(1, groups)]
        straight = jnp.where(chip == chips - 1, column[groups - 1], column[1])
        ends = [straight] + [chip_shift(straight, s) for s in range(1, chips)]
        inner = inner_stress(src, dst, near_blocks, with_mate(near), devices * elems)
        coeffs = [
            jnp.dot(bases[s], column[s], preferred_element_type=jnp.float32)
            .astype(jnp.bfloat16)
            .reshape(devices, rank, members)
            for s in range(groups)
        ]
        partial = outer_stress(
            src, dst, place, near_blocks, with_mate(ends), far_u, jnp.stack(coeffs), inner
        )
        partial = partial[: devices * elems].reshape(CORES, chips, elems, members)
        joined = [partial[0, s] + core_swap(partial[1, s]) for s in range(chips)]
        total = joined[0]
        for s in range(1, chips):
            total = total + chip_shift(joined[s].astype(jnp.bfloat16), s).astype(jnp.float32)
        return total

    velocity_one, drift_one = slip_rates(section_stress(slip), state, load, friction_a)
    slip_mid = slip + STEP * velocity_one
    state_mid = state + STEP * drift_one
    velocity_two, drift_two = slip_rates(section_stress(slip_mid), state_mid, load, friction_a)
    slip_next = slip + 0.5 * STEP * (velocity_one + velocity_two)
    state_next = state + 0.5 * STEP * (drift_one + drift_two)
    return (slip_next, state_next)


def solution(mesh):
    placed = (
        P(("grp", "clu", "row"), None),
        P(("grp", "clu", "row"), None),
        P(("grp", "clu", "row"), None),
        P(("grp", "clu", "row")),
        P(("grp", "clu", "row"), None, None),
        P(("grp", "clu", "row"), None),
        P(("grp", "clu", "row"), None, None, None),
        P(("grp", "clu", "row"), None, None, None),
        P(("grp", "clu", "row"), None),
    )
    return jax.shard_map(
        body,
        mesh=mesh,
        in_specs=placed,
        out_specs=(P(("grp", "clu", "row"), None), P(("grp", "clu", "row"), None)),
        check_vma=False,
    )
```

time: 75.1 us -> 73.9 us (0.984)
  starting transfers between devices: 35.1 us -> 19.8 us
  waiting for transfers between devices: 23.1 us -> 31.5 us
  Pallas kernels: 7.96 us -> 11.9 us
  local copies, waits for them, and re-layouts: 0.32 us -> 1.15 us
  matrix products: 0.45 us -> 1.26 us
    ppermute x4 -> x0, starting transfers between devices: 11.7 us -> none  [group_next(): return lax.ppermute(array, 'clu', pairs)]
    ppermute x9 -> x6, waiting for transfers between devices: 4.44 us -> 13 us  [group_shift(): lax.ppermute(array, 'clu', [(i, (i + step) % groups) for i in range(group...]
    ppermute x4 -> x6, waiting for transfers between devices: 9.06 us -> 16.3 us  [chip_shift(): return lax.ppermute(array, 'row', pairs)]
    ppermute x4 -> x0, waiting for transfers between devices: 4.68 us -> none  [group_next(): return lax.ppermute(array, 'clu', pairs)]
    ppermute x9 -> x6, starting transfers between devices: 15.8 us -> 11.2 us  [group_shift(): lax.ppermute(array, 'clu', [(i, (i + step) % groups) for i in range(group...]
    pallas_call x2 -> x4, Pallas kernels: 7.96 us -> 11.9 us  [the longest x2 7.48 us: inner_stress(): return call(src, dst, blocks, window)]
    ppermute x8, waiting for transfers between devices: 4.95 us -> 2.18 us  [core_swap(): return lax.ppermute(array, 'row', [(i, i ^ 1) for i in range(devices)])]
    convert_element_type x0 -> x2, other arithmetic: none -> 1.45 us  [section_stress(): half = field.astype(jnp.bfloat16)]
  transfers between devices with their start and end apart: 25 -> 20, of which waited for: 13 -> 10; matrix products, arithmetic and copies ran while one was open for 4% -> 6% of each run, Pallas kernels for 0% -> 10%
where the time goes in v2:
time: 73.9 us; the launch traced here: 73.7 us
  waiting for transfers between devices  31.5 us (43%)
  starting transfers between devices  19.8 us (27%)
  Pallas kernels  11.9 us (16%)
  other arithmetic  7 us (9%)
  matrix products  1.26 us (2%)
  local copies, waits for them, and re-layouts  1.15 us (2%)
  between operations  1.11 us (2%)
    ppermute x6, waiting for transfers between devices, chip_shift(): return lax.ppermute(array, 'row', pairs)  16.3 us
    ppermute x6, waiting for transfers between devices, group_shift(): lax.ppermute(array, 'clu', [(i, (i + step) % groups) for i in range(group...  13 us
    ppermute x6, starting transfers between devices, group_shift(): lax.ppermute(array, 'clu', [(i, (i + step) % groups) for i in range(group...  11.2 us
    pallas_call x2, Pallas kernels, inner_stress(): return call(src, dst, blocks, window)  7.48 us
    ppermute x6, starting transfers between devices, chip_shift(): return lax.ppermute(array, 'row', pairs)  7.08 us
    pallas_call x2, Pallas kernels, outer_stress(): return call(src, dst, place, blocks, window, far_u, coeffs, inner)  4.38 us
    ppermute x8, waiting for transfers between devices, core_swap(): return lax.ppermute(array, 'row', [(i, i ^ 1) for i in range(devices)])  2.18 us
    ppermute x8, starting transfers between devices, core_swap(): return lax.ppermute(array, 'row', [(i, i ^ 1) for i in range(devices)])  1.56 us
  transfers between devices with their start and end apart: 20, of which 10 were waited for; matrix products, arithmetic and copies ran while one was open for 6% of the time, Pallas kernels for 10%

profile of v2, /device:TPU:0, one launch (start us, length us, event | category | flops | bytes accessed | tf_op | source)
XLA Modules:
  0.0 73.7 jit_solution(4003924575593629369)
XLA Ops:
  0.6 1.0 %convert_element_type.42 = bf16[256,256]{1,0:T(8,128)(2,1)S(1)} convert(f32[256,256]{1,0:T(8,128)} %param.9) | non-fusion elementwise | flops 65536 | bytes 393216 | tf_op jit(solution)/shard_map/convert_element_type | solution.py:188
  1.6 3.0 %collective-permute-start.5 = (bf16[256,256]{1,0:T(8,128)(2,1)S(1)}, bf16[256,256]{1,0:T(8,128)(2,1)S(1)}, u32[]{:S(2)}, u32[]{:S(2)}) collective-permute-start(bf16[256,256]{1,0:T(8,128)(2,1)S(1)} %convert_element_type.42), channel_id=1, source_target_pairs={{0,2},{1,3},{2,0},{3,1},{4,6},{5,7},{6,4},{7,5},{8,10},{9,11},{10,... | collective-permute-start | bytes 393224 | tf_op jit(solution)/shard_map/ppermute | solution.py:24
  4.6 3.6 %collective-permute-start.1 = (bf16[256,256]{1,0:T(8,128)(2,1)S(1)}, bf16[256,256]{1,0:T(8,128)(2,1)S(1)}, u32[]{:S(2)}, u32[]{:S(2)}) collective-permute-start(bf16[256,256]{1,0:T(8,128)(2,1)S(1)} %convert_element_type.42), channel_id=1, source_target_pairs={{0,12},{4,0},{8,4},{12,8},{1,13},{5,1},{9,5},{13,9},{2,14},{6,2},{... | collective-permute-start | bytes 393224 | tf_op jit(solution)/shard_map/ppermute | solution.py:29
  8.2 1.0 %collective-permute-start = (bf16[256,256]{1,0:T(8,128)(2,1)S(1)}, bf16[256,256]{1,0:T(8,128)(2,1)S(1)}, u32[]{:S(2)}, u32[]{:S(2)}) collective-permute-start(bf16[256,256]{1,0:T(8,128)(2,1)S(1)} %convert_element_type.42), channel_id=1, source_target_pairs={{0,4},{4,8},{8,12},{12,0},{1,5},{5,9},{9,13},{13,1},{2,6},{6,10},{... | collective-permute-start | bytes 393224 | tf_op jit(solution)/shard_map/ppermute | solution.py:29
  9.2 1.0 %convert_bitcast_fusion = bf16[1,256,256]{2,1,0:T(8,128)(2,1)S(1)} fusion(f32[256,256]{1,0:T(8,128)} %param.9), kind=kLoop, calls=%fused_computation.117 | loop fusion | flops 65536 | bytes 393216 | tf_op jit(solution)/shard_map/stack | solution.py:184
  10.3 0.8 %iota_compare_fusion = pred[4,4,32]{2,1,0:T(4,128)(4,1)S(1)} fusion(s32[4,4]{1,0:T(4,128)} %param.17), kind=kLoop, calls=%fused_computation.61 | loop fusion | flops 512 | bytes 576 | tf_op jit(solution)/shard_map/lt | solution.py:175
  11.0 1.1 %broadcast_select_fusion = bf16[4,4,32,256]{3,2,1,0:T(8,128)(2,1)S(1)} fusion(bf16[4,4,32,256]{3,2,1,0:T(8,128)(2,1)} %param.16, pred[4,4,32]{2,1,0:T(4,128)(4,1)S(1)} %iota_compare_fusion), kind=kLoop, calls=%fused_computation.58 | loop fusion | flops 131072 | bytes 524800 | tf_op jit(solution)/shard_map/jit(_where)/select_n | solution.py:175
  12.1 0.2 convolution_convert_fusion.7
  12.4 0.1 pad_add_fusion.place
  12.5 0.0 collective-permute-done.5
  12.5 0.1 collective-permute-start.6
  12.6 0.0 collective-permute-done.1
  12.6 4.6 %collective-permute-done = bf16[256,256]{1,0:T(8,128)(2,1)S(1)} collective-permute-done((bf16[256,256]{1,0:T(8,128)(2,1)S(1)}, bf16[256,256]{1,0:T(8,128)(2,1)S(1)}, u32[]{:S(2)}, u32[]{:S(2)}) %collective-permute-start) | collective-permute-done | bytes 131104 | tf_op jit(solution)/shard_map/ppermute | solution.py:29
  17.2 0.6 collective-permute-start.2
  17.8 0.2 convolution_convert_fusion.6
  18.0 0.2 convolution_convert_fusion.4
  18.2 0.9 %collective-permute-done.4 = bf16[256,256]{1,0:T(8,128)(2,1)S(1)} collective-permute-done((bf16[256,256]{1,0:T(8,128)(2,1)S(1)}, bf16[256,256]{1,0:T(8,128)(2,1)S(1)}, u32[]{:S(2)}, u32[]{:S(2)}) %collective-permute-start.4) | collective-permute-done | bytes 131104 | tf_op jit(solution)/shard_map/ppermute | solution.py:29
  19.0 0.2 convolution_convert_fusion.5
  19.2 3.1 %collective-permute-done.2 = bf16[256,256]{1,0:T(8,128)(2,1)S(1)} collective-permute-done((bf16[256,256]{1,0:T(8,128)(2,1)S(1)}, bf16[256,256]{1,0:T(8,128)(2,1)S(1)}, u32[]{:S(2)}, u32[]{:S(2)}) %collective-permute-start.2) | collective-permute-done | bytes 131104 | tf_op jit(solution)/shard_map/ppermute | solution.py:24
  22.3 0.1 collective-permute-start.3
  22.4 0.0 collective-permute-done.6
  22.4 0.1 pad_maximum_fusion.1
  22.5 3.7 %shard_map.104.inner = f32[1152,256]{1,0:T(8,128)S(1)} custom-call(s32[112]{0:T(128)S(1)} %get-tuple-element.23.src, s32[112]{0:T(128)S(1)} %get-tuple-element.22.dst, bf16[112,128,128]{2,1,0:T(8,128)(2,1)S(1)} %copy-done, bf16[1024,256]{1,0:T(8,128)(2,1)S(1)} %bitcast.139), custom_call_target="tpu_custom_call" | custom-call | flops 939524096 | bytes 1048576 | tf_op jit(solution)/shard_map/pallas_call | solution.py:120
  26.3 0.0 copy-start.1
  26.3 0.1 pad_maximum_fusion
  26.3 0.9 %copy-done.1 = bf16[4,4,32,256]{3,2,1,0:T(8,128)(2,1)S(1)} copy-done((bf16[4,4,32,256]{3,2,1,0:T(8,128)(2,1)S(1)}, bf16[4,4,32,256]{3,2,1,0:T(8,128)(2,1)}, u32[]{:S(2)}) %copy-start.1) | copy-done | bytes 262168
  27.2 2.2 %shard_map.105 = f32[1152,256]{1,0:T(8,128)S(1)} custom-call(s32[112]{0:T(128)S(1)} %get-tuple-element.23.src, s32[112]{0:T(128)S(1)} %get-tuple-element.22.dst, s32[3]{0:T(128)S(1)} %pad_add_fusion.place, bf16[112,128,128]{2,1,0:T(8,128)(2,1)S(1)} %copy-done, bf16[1024,256]{1,0:T(8,128)(2,1)S(1)} %bitcast.142, bf16[4,4,32,256]{3,2,1,0:T(8,128)(2,1)S(1)} %copy-done.1, ...), custom_call_target="tpu_custom_call" | custom-call | flops 536870912 | bytes 2359296 | tf_op jit(solution)/shard_map/pallas_call | solution.py:136
  29.4 0.1 slice.48
  29.5 0.0 copy-start.5
  29.5 0.0 copy-start.2
  29.5 0.0 copy-start.3
  29.5 0.0 copy-start.4
  29.6 0.6 collective-permute-start.8
  30.1 0.1 collective-permute-start.7
  30.2 1.1 %collective-permute-done.8 = f32[256,256]{1,0:T(8,128)S(1)} collective-permute-done((f32[256,256]{1,0:T(8,128)S(1)}, f32[256,256]{1,0:T(8,128)S(1)}, u32[]{:S(2)}, u32[]{:S(2)}) %collective-permute-start.8) | collective-permute-done | bytes 262176 | tf_op jit(solution)/shard_map/ppermute | solution.py:18
  31.3 0.6 collective-permute-start.9
  32.0 5.2 %collective-permute-done.9 = bf16[256,256]{1,0:T(8,128)(2,1)S(1)} collective-permute-done((bf16[256,256]{1,0:T(8,128)(2,1)S(1)}, bf16[256,256]{1,0:T(8,128)(2,1)S(1)}, u32[]{:S(2)}, u32[]{:S(2)}) %collective-permute-start.9) | collective-permute-done | bytes 131104 | tf_op jit(solution)/shard_map/ppermute | solution.py:24
  37.2 0.5 add_convert_fusion
  37.7 0.6 collective-permute-start.15
  38.3 2.1 %collective-permute-start.11 = (bf16[256,256]{1,0:T(8,128)(2,1)S(1)}, bf16[256,256]{1,0:T(8,128)(2,1)S(1)}, u32[]{:S(2)}, u32[]{:S(2)}) collective-permute-start(bf16[256,256]{1,0:T(8,128)(2,1)S(1)} %get-tuple-element.4), channel_id=1, source_target_pairs={{0,12},{4,0},{8,4},{12,8},{1,13},{5,1},{9,5},{13,9},{2,14},{6,2},{... | collective-permute-start | bytes 393224 | tf_op jit(solution)/shard_map/ppermute | solution.py:29
  40.4 2.5 %collective-permute-start.14 = (bf16[256,256]{1,0:T(8,128)(2,1)S(1)}, bf16[256,256]{1,0:T(8,128)(2,1)S(1)}, u32[]{:S(2)}, u32[]{:S(2)}) collective-permute-start(bf16[256,256]{1,0:T(8,128)(2,1)S(1)} %get-tuple-element.4), channel_id=1, source_target_pairs={{0,8},{4,12},{8,0},{12,4},{1,9},{5,13},{9,1},{13,5},{2,10},{6,14},... | collective-permute-start | bytes 393224 | tf_op jit(solution)/shard_map/ppermute | solution.py:29
  42.8 2.0 %collective-permute-start.10 = (bf16[256,256]{1,0:T(8,128)(2,1)S(1)}, bf16[256,256]{1,0:T(8,128)(2,1)S(1)}, u32[]{:S(2)}, u32[]{:S(2)}) collective-permute-start(bf16[256,256]{1,0:T(8,128)(2,1)S(1)} %get-tuple-element.4), channel_id=1, source_target_pairs={{0,4},{4,8},{8,12},{12,0},{1,5},{5,9},{9,13},{13,1},{2,6},{6,10},{... | collective-permute-start | bytes 393224 | tf_op jit(solution)/shard_map/ppermute | solution.py:29
  44.8 0.2 convolution_convert_fusion.3
  45.1 0.1 collective-permute-start.16
  45.2 7.4 %collective-permute-done.10 = bf16[256,256]{1,0:T(8,128)(2,1)S(1)} collective-permute-done((bf16[256,256]{1,0:T(8,128)(2,1)S(1)}, bf16[256,256]{1,0:T(8,128)(2,1)S(1)}, u32[]{:S(2)}, u32[]{:S(2)}) %collective-permute-start.10) | collective-permute-done | bytes 131104 | tf_op jit(solution)/shard_map/ppermute | solution.py:29
  52.6 1.1 %collective-permute-start.12 = (bf16[256,256]{1,0:T(8,128)(2,1)S(1)}, bf16[256,256]{1,0:T(8,128)(2,1)S(1)}, u32[]{:S(2)}, u32[]{:S(2)}) collective-permute-start(bf16[256,256]{1,0:T(8,128)(2,1)S(1)} %broadcast_select_fusion.1), channel_id=1, source_target_pairs={{0,2},{1,3},{2,0},{3,1},{4,6},{5,7},{6,4},{7,5},{8,10},{9,11},{10,... | collective-permute-start | bytes 393224 | tf_op jit(solution)/shard_map/ppermute | solution.py:24
  53.7 0.2 convolution_convert_fusion.2
  53.8 0.2 convolution_convert_fusion
  54.0 0.2 collective-permute-done.14
  54.2 0.2 convolution_convert_fusion.1
  54.3 3.3 %collective-permute-done.12 = bf16[256,256]{1,0:T(8,128)(2,1)S(1)} collective-permute-done((bf16[256,256]{1,0:T(8,128)(2,1)S(1)}, bf16[256,256]{1,0:T(8,128)(2,1)S(1)}, u32[]{:S(2)}, u32[]{:S(2)}) %collective-permute-start.12) | collective-permute-done | bytes 131104 | tf_op jit(solution)/shard_map/ppermute | solution.py:24
  57.6 0.1 collective-permute-start.13
  57.8 0.1 pad_maximum_fusion.3
  57.8 3.7 %shard_map.106.inner = f32[1152,256]{1,0:T(8,128)S(1)} custom-call(s32[112]{0:T(128)S(1)} %get-tuple-element.23.src, s32[112]{0:T(128)S(1)} %get-tuple-element.22.dst, bf16[112,128,128]{2,1,0:T(8,128)(2,1)S(1)} %copy-done, bf16[1024,256]{1,0:T(8,128)(2,1)S(1)} %bitcast.140), custom_call_target="tpu_custom_call" | custom-call | flops 939524096 | bytes 1048576 | tf_op jit(solution)/shard_map/pallas_call | solution.py:120
  61.6 0.1 pad_maximum_fusion.2
  61.7 2.2 %shard_map.107 = f32[1152,256]{1,0:T(8,128)S(1)} custom-call(s32[112]{0:T(128)S(1)} %get-tuple-element.23.src, s32[112]{0:T(128)S(1)} %get-tuple-element.22.dst, s32[3]{0:T(128)S(1)} %pad_add_fusion.place, bf16[112,128,128]{2,1,0:T(8,128)(2,1)S(1)} %copy-done, bf16[1024,256]{1,0:T(8,128)(2,1)S(1)} %bitcast.141, bf16[4,4,32,256]{3,2,1,0:T(8,128)(2,1)S(1)} %copy-done.1, ...), custom_call_target="tpu_custom_call" | custom-call | flops 536870912 | bytes 2359296 | tf_op jit(solution)/shard_map/pallas_call | solution.py:136
  63.8 0.1 slice.53
  64.0 0.6 collective-permute-start.18
  64.5 0.1 collective-permute-start.17
  64.6 1.1 %collective-permute-done.18 = f32[256,256]{1,0:T(8,128)S(1)} collective-permute-done((f32[256,256]{1,0:T(8,128)S(1)}, f32[256,256]{1,0:T(8,128)S(1)}, u32[]{:S(2)}, u32[]{:S(2)}) %collective-permute-start.18) | collective-permute-done | bytes 262176 | tf_op jit(solution)/shard_map/ppermute | solution.py:18
  65.7 1.1 %collective-permute-start.19 = (bf16[256,256]{1,0:T(8,128)(2,1)S(1)}, bf16[256,256]{1,0:T(8,128)(2,1)S(1)}, u32[]{:S(2)}, u32[]{:S(2)}) collective-permute-start(bf16[256,256]{1,0:T(8,128)(2,1)S(1)} %fusion.12), channel_id=1, source_target_pairs={{0,2},{1,3},{2,0},{3,1},{4,6},{5,7},{6,4},{7,5},{8,10},{9,11},{10,... | collective-permute-start | bytes 393224 | tf_op jit(solution)/shard_map/ppermute | solution.py:24
  66.9 4.7 %collective-permute-done.19 = bf16[256,256]{1,0:T(8,128)(2,1)S(1)} collective-permute-done((bf16[256,256]{1,0:T(8,128)(2,1)S(1)}, bf16[256,256]{1,0:T(8,128)(2,1)S(1)}, u32[]{:S(2)}, u32[]{:S(2)}) %collective-permute-start.19) | collective-permute-done | bytes 131104 | tf_op jit(solution)/shard_map/ppermute | solution.py:24
  71.6 1.3 %fusion.10 = (f32[256,256]{1,0:T(8,128)}, f32[256,256]{1,0:T(8,128)S(1)}) fusion(f32[256,256]{1,0:T(8,128)S(1)} %copy-done.4, f32[256,256]{1,0:T(8,128)S(1)} %get-tuple-element.5, f32[256]{0:T(256)S(1)} %broadcast_multiply_fusion, f32[256,256]{1,0:T(8,128)S(1)} %copy-done.3, bf16[256,256]{1,0:T(8,128)(2,1)S(1)} %collective-permute-done.19, ...), kind=kLoop, calls=%fused_computation.26 | loop fusion | flops 2162688 | bytes 1968128 | tf_op jit(solution)/shard_map/add | solution.py:215
  72.9 0.8 %multiply_add_fusion = f32[256,256]{1,0:T(8,128)} fusion(f32[256,256]{1,0:T(8,128)S(1)} %copy-done.2, f32[256,256]{1,0:T(8,128)S(1)} %get-tuple-element.5, f32[256,256]{1,0:T(8,128)S(1)} %get-tuple-element.3), kind=kLoop, calls=%fused_computation.53 | loop fusion | flops 196608 | bytes 1048576 | tf_op jit(solution)/shard_map/add | solution.py:214
  (31 shorter events, 0.5 us)
Async XLA Ops:
  0.6 11.7 %copy-start.6 = (s32[112,2]{0,1:T(2,128)S(1)}, s32[112,2]{0,1:T(2,128)}, u32[]{:S(2)}) copy-start(s32[112,2]{0,1:T(2,128)} %param.14) | copy-start | bytes 2692
  1.6 10.9 %collective-permute-start.5 = (bf16[256,256]{1,0:T(8,128)(2,1)S(1)}, bf16[256,256]{1,0:T(8,128)(2,1)S(1)}, u32[]{:S(2)}, u32[]{:S(2)}) collective-permute-start(bf16[256,256]{1,0:T(8,128)(2,1)S(1)} %convert_element_type.42), channel_id=1, source_target_pairs={{0,2},{1,3},{2,0},{3,1},{4,6},{5,7},{6,4},{7,5},{8,10},{9,11},{10,... | collective-permute-start | bytes 393224 | tf_op jit(solution)/shard_map/ppermute | solution.py:24
  4.6 8.0 %collective-permute-start.1 = (bf16[256,256]{1,0:T(8,128)(2,1)S(1)}, bf16[256,256]{1,0:T(8,128)(2,1)S(1)}, u32[]{:S(2)}, u32[]{:S(2)}) collective-permute-start(bf16[256,256]{1,0:T(8,128)(2,1)S(1)} %convert_element_type.42), channel_id=1, source_target_pairs={{0,12},{4,0},{8,4},{12,8},{1,13},{5,1},{9,5},{13,9},{2,14},{6,2},{... | collective-permute-start | bytes 393224 | tf_op jit(solution)/shard_map/ppermute | solution.py:29
  8.2 10.8 %collective-permute-start.4 = (bf16[256,256]{1,0:T(8,128)(2,1)S(1)}, bf16[256,256]{1,0:T(8,128)(2,1)S(1)}, u32[]{:S(2)}, u32[]{:S(2)}) collective-permute-start(bf16[256,256]{1,0:T(8,128)(2,1)S(1)} %convert_element_type.42), channel_id=1, source_target_pairs={{0,8},{4,12},{8,0},{12,4},{1,9},{5,13},{9,1},{13,5},{2,10},{6,14},... | collective-permute-start | bytes 393224 | tf_op jit(solution)/shard_map/ppermute | solution.py:29
  8.2 9.0 %collective-permute-start = (bf16[256,256]{1,0:T(8,128)(2,1)S(1)}, bf16[256,256]{1,0:T(8,128)(2,1)S(1)}, u32[]{:S(2)}, u32[]{:S(2)}) collective-permute-start(bf16[256,256]{1,0:T(8,128)(2,1)S(1)} %convert_element_type.42), channel_id=1, source_target_pairs={{0,4},{4,8},{8,12},{12,0},{1,5},{5,9},{9,13},{13,1},{2,6},{6,10},{... | collective-permute-start | bytes 393224 | tf_op jit(solution)/shard_map/ppermute | solution.py:29
  12.5 10.0 %copy-start = (bf16[112,128,128]{2,1,0:T(8,128)(2,1)S(1)}, bf16[112,128,128]{2,1,0:T(8,128)(2,1)}, u32[]{:S(2)}) copy-start(bf16[112,128,128]{2,1,0:T(8,128)(2,1)} %blocks.7) | copy-start | bytes 11010052
  12.5 9.9 %collective-permute-start.6 = (bf16[2,256,256]{2,1,0:T(8,128)(2,1)S(1)}, bf16[2,256,256]{2,1,0:T(8,128)(2,1)S(1)}, u32[]{:S(2)}, u32[]{:S(2)}) collective-permute-start(bf16[2,256,256]{2,1,0:T(8,128)(2,1)S(1)} %get-tuple-element.15), channel_id=1, source_target_pairs={{0,1},{1,0},{2,3},{3,2},{4,5},{5,4},{6,7},{7,6},{8,9},{9,8},{10,11... | collective-permute-start | bytes 786440 | tf_op jit(solution)/shard_map/ppermute | solution.py:18
  17.2 5.0 %collective-permute-start.2 = (bf16[256,256]{1,0:T(8,128)(2,1)S(1)}, bf16[256,256]{1,0:T(8,128)(2,1)S(1)}, u32[]{:S(2)}, u32[]{:S(2)}) collective-permute-start(bf16[256,256]{1,0:T(8,128)(2,1)S(1)} %broadcast_select_fusion.2), channel_id=1, source_target_pairs={{0,2},{1,3},{2,0},{3,1},{4,6},{5,7},{6,4},{7,5},{8,10},{9,11},{10,... | collective-permute-start | bytes 393224 | tf_op jit(solution)/shard_map/ppermute | solution.py:24
  22.3 4.0 %collective-permute-start.3 = (bf16[2,256,256]{2,1,0:T(8,128)(2,1)S(1)}, bf16[2,256,256]{2,1,0:T(8,128)(2,1)S(1)}, u32[]{:S(2)}, u32[]{:S(2)}) collective-permute-start(bf16[2,256,256]{2,1,0:T(8,128)(2,1)S(1)} %get-tuple-element.21), channel_id=1, source_target_pairs={{0,1},{1,0},{2,3},{3,2},{4,5},{5,4},{6,7},{7,6},{8,9},{9,8},{10,11... | collective-permute-start | bytes 786440 | tf_op jit(solution)/shard_map/ppermute | solution.py:18
  26.3 1.0 %copy-start.1 = (bf16[4,4,32,256]{3,2,1,0:T(8,128)(2,1)S(1)}, bf16[4,4,32,256]{3,2,1,0:T(8,128)(2,1)}, u32[]{:S(2)}) copy-start(bf16[4,4,32,256]{3,2,1,0:T(8,128)(2,1)} %far_u.3) | copy-start | bytes 786436
  29.5 2.5 %copy-start.5 = (f32[256]{0:T(256)S(1)}, f32[256]{0:T(256)}, u32[]{:S(2)}) copy-start(f32[256]{0:T(256)} %param.12) | copy-start | bytes 3076
  29.5 7.7 %copy-start.2 = (f32[256,256]{1,0:T(8,128)S(1)}, f32[256,256]{1,0:T(8,128)}, u32[]{:S(2)}) copy-start(f32[256,256]{1,0:T(8,128)} %param.9) | copy-start | bytes 786436
  29.5 7.7 %copy-start.3 = (f32[256,256]{1,0:T(8,128)S(1)}, f32[256,256]{1,0:T(8,128)}, u32[]{:S(2)}) copy-start(f32[256,256]{1,0:T(8,128)} %param.11) | copy-start | bytes 786436
  29.5 7.7 %copy-start.4 = (f32[256,256]{1,0:T(8,128)S(1)}, f32[256,256]{1,0:T(8,128)}, u32[]{:S(2)}) copy-start(f32[256,256]{1,0:T(8,128)} %param.10) | copy-start | bytes 786436
  29.6 1.7 %collective-permute-start.8 = (f32[256,256]{1,0:T(8,128)S(1)}, f32[256,256]{1,0:T(8,128)S(1)}, u32[]{:S(2)}, u32[]{:S(2)}) collective-permute-start(f32[256,256]{1,0:T(8,128)S(1)} %get-tuple-element.9), channel_id=1, source_target_pairs={{0,1},{1,0},{2,3},{3,2},{4,5},{5,4},{6,7},{7,6},{8,9},{9,8},{10,11... | collective-permute-start | bytes 786440 | tf_op jit(solution)/shard_map/ppermute | solution.py:18
  30.1 1.8 %collective-permute-start.7 = (f32[256,256]{1,0:T(8,128)S(1)}, f32[256,256]{1,0:T(8,128)S(1)}, u32[]{:S(2)}, u32[]{:S(2)}) collective-permute-start(f32[256,256]{1,0:T(8,128)S(1)} %get-tuple-element.8), channel_id=1, source_target_pairs={{0,1},{1,0},{2,3},{3,2},{4,5},{5,4},{6,7},{7,6},{8,9},{9,8},{10,11... | collective-permute-start | bytes 786440 | tf_op jit(solution)/shard_map/ppermute | solution.py:18
  31.3 5.8 %collective-permute-start.9 = (bf16[256,256]{1,0:T(8,128)(2,1)S(1)}, bf16[256,256]{1,0:T(8,128)(2,1)S(1)}, u32[]{:S(2)}, u32[]{:S(2)}) collective-permute-start(bf16[256,256]{1,0:T(8,128)(2,1)S(1)} %fusion.18), channel_id=1, source_target_pairs={{0,2},{1,3},{2,0},{3,1},{4,6},{5,7},{6,4},{7,5},{8,10},{9,11},{10,... | collective-permute-start | bytes 393224 | tf_op jit(solution)/shard_map/ppermute | solution.py:24
  37.7 7.3 %collective-permute-start.15 = (bf16[256,256]{1,0:T(8,128)(2,1)S(1)}, bf16[256,256]{1,0:T(8,128)(2,1)S(1)}, u32[]{:S(2)}, u32[]{:S(2)}) collective-permute-start(bf16[256,256]{1,0:T(8,128)(2,1)S(1)} %get-tuple-element.4), channel_id=1, source_target_pairs={{0,2},{1,3},{2,0},{3,1},{4,6},{5,7},{6,4},{7,5},{8,10},{9,11},{10,... | collective-permute-start | bytes 393224 | tf_op jit(solution)/shard_map/ppermute | solution.py:24
  38.3 6.9 %collective-permute-start.11 = (bf16[256,256]{1,0:T(8,128)(2,1)S(1)}, bf16[256,256]{1,0:T(8,128)(2,1)S(1)}, u32[]{:S(2)}, u32[]{:S(2)}) collective-permute-start(bf16[256,256]{1,0:T(8,128)(2,1)S(1)} %get-tuple-element.4), channel_id=1, source_target_pairs={{0,12},{4,0},{8,4},{12,8},{1,13},{5,1},{9,5},{13,9},{2,14},{6,2},{... | collective-permute-start | bytes 393224 | tf_op jit(solution)/shard_map/ppermute | solution.py:29
  40.4 13.8 %collective-permute-start.14 = (bf16[256,256]{1,0:T(8,128)(2,1)S(1)}, bf16[256,256]{1,0:T(8,128)(2,1)S(1)}, u32[]{:S(2)}, u32[]{:S(2)}) collective-permute-start(bf16[256,256]{1,0:T(8,128)(2,1)S(1)} %get-tuple-element.4), channel_id=1, source_target_pairs={{0,8},{4,12},{8,0},{12,4},{1,9},{5,13},{9,1},{13,5},{2,10},{6,14},... | collective-permute-start | bytes 393224 | tf_op jit(solution)/shard_map/ppermute | solution.py:29
  42.8 9.7 %collective-permute-start.10 = (bf16[256,256]{1,0:T(8,128)(2,1)S(1)}, bf16[256,256]{1,0:T(8,128)(2,1)S(1)}, u32[]{:S(2)}, u32[]{:S(2)}) collective-permute-start(bf16[256,256]{1,0:T(8,128)(2,1)S(1)} %get-tuple-element.4), channel_id=1, source_target_pairs={{0,4},{4,8},{8,12},{12,0},{1,5},{5,9},{9,13},{13,1},{2,6},{6,10},{... | collective-permute-start | bytes 393224 | tf_op jit(solution)/shard_map/ppermute | solution.py:29
  45.1 12.7 %collective-permute-start.16 = (bf16[2,256,256]{2,1,0:T(8,128)(2,1)S(1)}, bf16[2,256,256]{2,1,0:T(8,128)(2,1)S(1)}, u32[]{:S(2)}, u32[]{:S(2)}) collective-permute-start(bf16[2,256,256]{2,1,0:T(8,128)(2,1)S(1)} %get-tuple-element.11), channel_id=1, source_target_pairs={{0,1},{1,0},{2,3},{3,2},{4,5},{5,4},{6,7},{7,6},{8,9},{9,8},{10,11... | collective-permute-start | bytes 786440 | tf_op jit(solution)/shard_map/ppermute | solution.py:18
  52.6 5.0 %collective-permute-start.12 = (bf16[256,256]{1,0:T(8,128)(2,1)S(1)}, bf16[256,256]{1,0:T(8,128)(2,1)S(1)}, u32[]{:S(2)}, u32[]{:S(2)}) collective-permute-start(bf16[256,256]{1,0:T(8,128)(2,1)S(1)} %broadcast_select_fusion.1), channel_id=1, source_target_pairs={{0,2},{1,3},{2,0},{3,1},{4,6},{5,7},{6,4},{7,5},{8,10},{9,11},{10,... | collective-permute-start | bytes 393224 | tf_op jit(solution)/shard_map/ppermute | solution.py:24
  57.6 3.9 %collective-permute-start.13 = (bf16[2,256,256]{2,1,0:T(8,128)(2,1)S(1)}, bf16[2,256,256]{2,1,0:T(8,128)(2,1)S(1)}, u32[]{:S(2)}, u32[]{:S(2)}) collective-permute-start(bf16[2,256,256]{2,1,0:T(8,128)(2,1)S(1)} %get-tuple-element.13), channel_id=1, source_target_pairs={{0,1},{1,0},{2,3},{3,2},{4,5},{5,4},{6,7},{7,6},{8,9},{9,8},{10,11... | collective-permute-start | bytes 786440 | tf_op jit(solution)/shard_map/ppermute | solution.py:18
  64.0 1.7 %collective-permute-start.18 = (f32[256,256]{1,0:T(8,128)S(1)}, f32[256,256]{1,0:T(8,128)S(1)}, u32[]{:S(2)}, u32[]{:S(2)}) collective-permute-start(f32[256,256]{1,0:T(8,128)S(1)} %get-tuple-element.7), channel_id=1, source_target_pairs={{0,1},{1,0},{2,3},{3,2},{4,5},{5,4},{6,7},{7,6},{8,9},{9,8},{10,11... | collective-permute-start | bytes 786440 | tf_op jit(solution)/shard_map/ppermute | solution.py:18
  64.5 2.3 %collective-permute-start.17 = (f32[256,256]{1,0:T(8,128)S(1)}, f32[256,256]{1,0:T(8,128)S(1)}, u32[]{:S(2)}, u32[]{:S(2)}) collective-permute-start(f32[256,256]{1,0:T(8,128)S(1)} %get-tuple-element.6), channel_id=1, source_target_pairs={{0,1},{1,0},{2,3},{3,2},{4,5},{5,4},{6,7},{7,6},{8,9},{9,8},{10,11... | collective-permute-start | bytes 786440 | tf_op jit(solution)/shard_map/ppermute | solution.py:18
  65.7 5.8 %collective-permute-start.19 = (bf16[256,256]{1,0:T(8,128)(2,1)S(1)}, bf16[256,256]{1,0:T(8,128)(2,1)S(1)}, u32[]{:S(2)}, u32[]{:S(2)}) collective-permute-start(bf16[256,256]{1,0:T(8,128)(2,1)S(1)} %fusion.12), channel_id=1, source_target_pairs={{0,2},{1,3},{2,0},{3,1},{4,6},{5,7},{6,4},{7,5},{8,10},{9,11},{10,... | collective-permute-start | bytes 393224 | tf_op jit(solution)/shard_map/ppermute | solution.py:24

commit v3 on v1

v3 whole, which is shorter than its diff:
```python
import functools

import jax
import jax.numpy as jnp
from jax import lax
from jax.experimental import pallas as pl
from jax.experimental.pallas import tpu as pltpu
from jax.sharding import PartitionSpec as P

REACH = 4
CORES = 2
STEP = 0.2
WIDTH = 4


def core_swap(array):
    devices = lax.axis_size("row")
    return lax.ppermute(array, "row", [(i, i ^ 1) for i in range(devices)])


def chip_shift(array, step):
    devices = lax.axis_size("row")
    pairs = [(i, (i + CORES * step) % devices) for i in range(devices)]
    return lax.ppermute(array, "row", pairs)


def group_shift(array, step):
    groups = lax.axis_size("clu")
    return lax.ppermute(array, "clu", [(i, (i + step) % groups) for i in range(groups)])


def end_shift(array, step):
    devices, groups = lax.axis_size("row"), lax.axis_size("clu")
    pairs = []
    for c in range(groups):
        for r in range(devices):
            to = c + step if r >= devices - CORES else c - step
            pairs.append((c * devices + r, to % groups * devices + r))
    return lax.ppermute(array, ("clu", "row"), pairs)


def plan_kernel(leaf, spare, src, dst, plan, rows, free):
    places, chunks, targets = plan.shape[1], rows.shape[0], free.shape[0]
    for t in range(targets):
        free[t] = 0
    for i in range(places):
        plan[0, i] = 0
        plan[1, i] = spare
    for i in range(chunks):
        rows[i] = 0

    def put(j, used):
        target = dst[j]
        at = free[target]
        full = (at & (WIDTH - 1)) == 0
        at = jnp.where(full, used * WIDTH, at)
        free[target] = at + 1
        plan[0, at] = j
        plan[1, at] = src[j] * leaf
        rows[lax.shift_right_logical(at, WIDTH.bit_length() - 1)] = target * leaf
        return used + full.astype(jnp.int32)

    lax.fori_loop(0, src.shape[0], put, jnp.int32(0), unroll=4)


def stress_kernel(leaf, groups, place, plan, rows, ranks, blocks, window, far_u, far_v, *rest):
    columns, (out, coeffs) = rest[:groups], rest[groups:]
    targets, _, rank, elems = far_u.shape
    chips, members = targets // CORES, window.shape[1]
    chip, core = place[0], place[1]
    row = lax.broadcasted_iota(jnp.int32, (rank, members), 0)
    for s in range(groups):
        source = place[2 + s]
        product = jnp.dot(
            jnp.concatenate([far_v[t, source] for t in range(targets)], axis=0),
            columns[s][...],
            preferred_element_type=jnp.float32,
        )
        for t in range(targets):
            part = product[t * rank : (t + 1) * rank]
            part = jnp.where(row < ranks[t, source], part, 0.0)
            coeffs[t, s * rank : (s + 1) * rank, :] = part.astype(jnp.bfloat16)
    for other in range(CORES):
        for ahead in range(chips):
            target = lax.rem(chip + ahead, chips) * CORES + (core ^ other)
            out[pl.ds((other * chips + ahead) * elems, elems), :] = lax.dot_general(
                jnp.concatenate([far_u[target, place[2 + s]] for s in range(groups)], axis=0),
                coeffs[target],
                (((0,), (0,)), ((), ())),
                preferred_element_type=jnp.float32,
            )
    products = []
    for i in range(rows.shape[0]):
        places = range(i * WIDTH, (i + 1) * WIDTH)
        sources = [pl.ds(pl.multiple_of(plan[1, p], leaf), leaf) for p in places]
        products.append(
            jnp.dot(
                jnp.concatenate([blocks[plan[0, p]] for p in places], axis=1),
                jnp.concatenate([window[source, :] for source in sources], axis=0),
                preferred_element_type=jnp.float32,
            )
        )
    for i in range(rows.shape[0]):
        out[pl.ds(pl.multiple_of(rows[i], leaf), leaf), :] += products[i]


VMEM = pl.BlockSpec(memory_space=pltpu.VMEM)
SMEM = pl.BlockSpec(memory_space=pltpu.SMEM)
PARAMS = pltpu.CompilerParams(vmem_limit_bytes=16 * 1024 * 1024)


def planned_blocks(src, dst, leaf, targets, spare):
    chunks = (src.shape[0] + targets * (WIDTH - 1)) // WIDTH
    return pl.pallas_call(
        functools.partial(plan_kernel, leaf, spare),
        out_shape=(
            jax.ShapeDtypeStruct((2, chunks * WIDTH), jnp.int32),
            jax.ShapeDtypeStruct((chunks,), jnp.int32),
        ),
        in_specs=[SMEM, SMEM],
        out_specs=(SMEM, SMEM),
        scratch_shapes=[pltpu.SMEM((targets,), jnp.int32)],
        compiler_params=PARAMS,
        cost_estimate=pl.CostEstimate(flops=1024, bytes_accessed=1024, transcendentals=0),
    )(src, dst)


def partial_stress(place, plan, ranks, blocks, window, far_u, far_v, columns):
    targets, groups, rank, elems = far_u.shape
    count, leaf, _ = blocks.shape
    rows, members = targets * elems, window.shape[1]
    return pl.pallas_call(
        functools.partial(stress_kernel, leaf, groups),
        out_shape=jax.ShapeDtypeStruct((rows, members), jnp.float32),
        in_specs=[SMEM] * 4 + [VMEM] * (4 + groups),
        out_specs=VMEM,
        scratch_shapes=[pltpu.VMEM((targets, groups * rank, members), jnp.bfloat16)],
        compiler_params=PARAMS,
        cost_estimate=pl.CostEstimate(
            flops=2 * members * (count * leaf * leaf + 2 * targets * groups * rank * elems),
            bytes_accessed=4 * rows * members,
            transcendentals=0,
        ),
    )(place, plan[0], plan[1], ranks, blocks, window, far_u, far_v, *columns)


def slip_rates(stress, state, load, friction_a):
    softness = friction_a[:, None]
    velocity = 2.0 * jnp.exp(-state / softness) * jnp.sinh((stress + load) / (2.0 * softness))
    speed = jnp.abs(velocity)
    drift = jnp.exp(-state) - speed / (1.0 + speed)
    return (velocity, drift)


def body(slip, state, load, friction_a, near_blocks, near_pairs, far_u, far_v, far_rank):
    elems, members = slip.shape
    leaf = near_blocks.shape[1]
    own = elems // leaf
    devices, groups = lax.axis_size("row"), lax.axis_size("clu")
    chips = devices // CORES
    clusters = devices * own
    assert REACH <= CORES * own
    group, row = lax.axis_index("clu"), lax.axis_index("row")
    chip, core = row // CORES, row % CORES
    toward = jnp.where(chip == chips - 1, -1, 1)
    sources = [group]
    for s in range(1, groups):
        sources.append(group + (toward if s % 2 else -toward) * ((s + 1) // 2))
    sources = [(source + groups) % groups for source in sources]
    place = jnp.stack([chip, core] + sources).astype(jnp.int32)

    source = near_pairs[:, 1] - group * clusters
    before, after = source < 0, source >= clusters
    local = jnp.where(before, source + clusters, jnp.where(after, source - clusters, source))
    holder = local // own
    piece = jnp.where(
        before, (chip + 1) % chips, jnp.where(after, chip, (chip - holder // CORES + chips) % chips)
    )
    piece = piece + jnp.where(before | after, chips, 0)
    src = ((((holder % CORES) ^ core) * 2 * chips + piece) * own + local % own).astype(jnp.int32)
    target = near_pairs[:, 0] - group * clusters
    owner = target // own
    ahead = (owner // CORES - chip + chips) % chips
    dst = ((((owner % CORES) ^ core) * chips + ahead) * own + target % own).astype(jnp.int32)

    plan = planned_blocks(src, dst, leaf, clusters, 4 * chips * elems)
    spare = jnp.zeros((leaf, members), jnp.bfloat16)

    def section_stress(field):
        half = field.astype(jnp.bfloat16)
        straight = end_shift(half, 1)
        near = jnp.concatenate([half] + [chip_shift(half, s) for s in range(1, chips)])
        column = [half, straight, end_shift(half, -1)]
        while len(column) < groups:
            step = 1 if len(column) % 2 else -1
            column.append(end_shift(column[-2], step))
        ends = jnp.concatenate([straight] + [chip_shift(straight, s) for s in range(1, chips)])
        window = jnp.concatenate([near, ends, core_swap(near), core_swap(ends), spare])
        partial = partial_stress(place, plan, far_rank, near_blocks, window, far_u, far_v, column)
        partial = partial.reshape(CORES, chips, elems, members)
        joined = [partial[0, s] + core_swap(partial[1, s]) for s in range(chips)]
        total = joined[0]
        for s in range(1, chips):
            total = total + chip_shift(joined[s].astype(jnp.bfloat16), s).astype(jnp.float32)
        return total

    velocity_one, drift_one = slip_rates(section_stress(slip), state, load, friction_a)
    slip_mid = slip + STEP * velocity_one
    state_mid = state + STEP * drift_one
    velocity_two, drift_two = slip_rates(section_stress(slip_mid), state_mid, load, friction_a)
    slip_next = slip + 0.5 * STEP * (velocity_one + velocity_two)
    state_next = state + 0.5 * STEP * (drift_one + drift_two)
    return (slip_next, state_next)


def solution(mesh):
    placed = (
        P(("grp", "clu", "row"), None),
        P(("grp", "clu", "row"), None),
        P(("grp", "clu", "row"), None),
        P(("grp", "clu", "row")),
        P(("grp", "clu", "row"), None, None),
        P(("grp", "clu", "row"), None),
        P(("grp", "clu", "row"), None, None, None),
        P(("grp", "clu", "row"), None, None, None),
        P(("grp", "clu", "row"), None),
    )
    return jax.shard_map(
        body,
        mesh=mesh,
        in_specs=placed,
        out_specs=(P(("grp", "clu", "row"), None), P(("grp", "clu", "row"), None)),
        check_vma=False,
    )
```

time: 75.1 us -> 61.4 us (0.82)
  starting transfers between devices: 35.1 us -> 24.9 us
  other arithmetic: 6.81 us -> 4.39 us
  waiting for transfers between devices: 23.1 us -> 20.8 us
  local copies, waits for them, and re-layouts: 0.32 us -> 2.39 us
    ppermute x13 -> x6, starting transfers between devices: 27.5 us -> 12.2 us  [end_shift(): return lax.ppermute(array, ('clu', 'row'), pairs)]
    ppermute x4 -> x6, starting transfers between devices: 6.15 us -> 11.3 us  [chip_shift(): return lax.ppermute(array, 'row', pairs)]
    ppermute x13 -> x6, waiting for transfers between devices: 9.12 us -> 6.74 us  [end_shift(): return lax.ppermute(array, ('clu', 'row'), pairs)]
    unnamed x20 -> x26, local copies, waits for them, and re-layouts: 0.14 us -> 2.22 us
    select_n x1 -> x0, other arithmetic: 1.13 us -> none  [body(): jnp.where(column < far_rank[:, :, None, None], far_v, jnp.zeros_like(far_v))]
    lt x1 -> x0, other arithmetic: 0.76 us -> none  [body(): column < far_rank[:, :, None, None]]
    pallas_call x2 -> x3, Pallas kernels: 7.96 us -> 7.67 us  [the longest x2 5.08 us: partial_stress(): pl.pallas_call(functools.partial(stress_kernel, leaf, groups), out_shape=...]
    ppermute x4 -> x6, waiting for transfers between devices: 9.06 us -> 9.13 us  [chip_shift(): return lax.ppermute(array, 'row', pairs)]
  transfers between devices with their start and end apart: 25 -> 20, of which waited for: 13 -> 12; matrix products, arithmetic and copies ran while one was open for 4% -> 2% of each run, Pallas kernels for 0% -> 4%
where the time goes in v3:
time: 61.4 us; the launch traced here: 61.2 us
  starting transfers between devices  24.9 us (41%)
  waiting for transfers between devices  20.8 us (34%)
  Pallas kernels  7.67 us (12%)
  other arithmetic  4.39 us (7%)
  local copies, waits for them, and re-layouts  2.39 us (4%)
  between operations  0.99 us (2%)
    ppermute x6, starting transfers between devices, end_shift(): return lax.ppermute(array, ('clu', 'row'), pairs)  12.2 us
    ppermute x6, starting transfers between devices, chip_shift(): return lax.ppermute(array, 'row', pairs)  11.3 us
    ppermute x6, waiting for transfers between devices, chip_shift(): return lax.ppermute(array, 'row', pairs)  9.13 us
    ppermute x6, waiting for transfers between devices, end_shift(): return lax.ppermute(array, ('clu', 'row'), pairs)  6.74 us
    pallas_call x2, Pallas kernels, partial_stress(): pl.pallas_call(functools.partial(stress_kernel, leaf, groups), out_shape=...  5.08 us
    ppermute x8, waiting for transfers between devices, core_swap(): return lax.ppermute(array, 'row', [(i, i ^ 1) for i in range(devices)])  4.95 us
    pallas_call x1, Pallas kernels, planned_blocks(): pl.pallas_call(functools.partial(plan_kernel, leaf, spare), out_shape=(ja...  2.59 us
    unnamed x26, local copies, waits for them, and re-layouts  2.22 us
  transfers between devices with their start and end apart: 20, of which 12 were waited for; matrix products, arithmetic and copies ran while one was open for 2% of the time, Pallas kernels for 4%

profile of v3, /device:TPU:0, one launch (start us, length us, event | category | flops | bytes accessed | tf_op | source)
XLA Modules:
  0.0 61.2 jit_solution(10048177932596381396)
XLA Ops:
  0.6 1.0 %constant_dynamic-update-slice_fusion.5 = (bf16[2176,256]{1,0:T(8,128)(2,1)S(1)}, bf16[256,256]{1,0:T(8,128)(2,1)S(1)}) fusion(f32[256,256]{1,0:T(8,128)} %param.9), kind=kLoop, calls=%fused_computation.51 | loop fusion | flops 65535 | bytes 524288
  1.6 3.0 %collective-permute-start = (bf16[256,256]{1,0:T(8,128)(2,1)S(1)}, bf16[256,256]{1,0:T(8,128)(2,1)S(1)}, u32[]{:S(2)}, u32[]{:S(2)}) collective-permute-start(bf16[256,256]{1,0:T(8,128)(2,1)S(1)} %get-tuple-element.12.rest_0_), channel_id=1, source_target_pairs={{0,2},{1,3},{2,0},{3,1},{4,6},{5,7},{6,4},{7,5},{8,10},{9,11},{10,... | collective-permute-start | bytes 393224 | tf_op jit(solution)/shard_map/ppermute | solution.py:24
  4.6 3.6 %collective-permute-start.1 = (bf16[256,256]{1,0:T(8,128)(2,1)S(1)}, bf16[256,256]{1,0:T(8,128)(2,1)S(1)}, u32[]{:S(2)}, u32[]{:S(2)}) collective-permute-start(bf16[256,256]{1,0:T(8,128)(2,1)S(1)} %get-tuple-element.12.rest_0_), channel_id=1, source_target_pairs={{0,12},{1,13},{2,6},{3,7},{4,0},{5,1},{6,10},{7,11},{8,4},{9,5},{1... | collective-permute-start | bytes 393224 | tf_op jit(solution)/shard_map/ppermute | solution.py:39
  8.2 0.0 collective-permute-start.5
  8.2 0.8 %fusion.26 = (s32[112]{0:T(128)S(1)}, s32[112]{0:T(128)S(1)}) fusion(s32[112,2]{0,1:T(2,128)} %param.14, s32[]{:T(128)} %select_n.92, s32[]{:T(128)} %select_n.93, s32[]{:T(128)S(6)} %mul.53, s32[]{:T(128)S(6)} %select_n.103), kind=kLoop, calls=%fused_computation.90 | loop fusion | flops 14000 | bytes 1808 | tf_op jit(solution)/shard_map/add | solution.py:184
  9.0 2.6 %shard_map.104 = (s32[2,136]{1,0:T(2,128)S(1)}, s32[34]{0:T(128)S(1)}) custom-call(s32[112]{0:T(128)S(1)} %get-tuple-element.18.src, s32[112]{0:T(128)S(1)} %get-tuple-element.17.dst), custom_call_target="tpu_custom_call" | custom-call | flops 1024 | bytes 1024 | tf_op jit(solution)/shard_map/pallas_call | solution.py:114
  11.6 0.1 stack.27.place
  11.7 0.4 collective-permute-done.1.rest_1_
  12.2 1.0 %collective-permute-start.2 = (bf16[256,256]{1,0:T(8,128)(2,1)S(1)}, bf16[256,256]{1,0:T(8,128)(2,1)S(1)}, u32[]{:S(2)}, u32[]{:S(2)}) collective-permute-start(bf16[256,256]{1,0:T(8,128)(2,1)S(1)} %collective-permute-done.1.rest_1_), channel_id=1, source_target_pairs={{0,2},{1,3},{2,0},{3,1},{4,6},{5,7},{6,4},{7,5},{8,10},{9,11},{10,... | collective-permute-start | bytes 393224 | tf_op jit(solution)/shard_map/ppermute | solution.py:24
  13.1 0.0 collective-permute-done
  13.1 0.1 collective-permute-start.3
  13.2 3.5 %collective-permute-start.6 = (bf16[256,256]{1,0:T(8,128)(2,1)S(1)}, bf16[256,256]{1,0:T(8,128)(2,1)S(1)}, u32[]{:S(2)}, u32[]{:S(2)}) collective-permute-start(bf16[256,256]{1,0:T(8,128)(2,1)S(1)} %collective-permute-done.1.rest_1_), channel_id=1, source_target_pairs={{0,12},{1,13},{2,6},{3,7},{4,0},{5,1},{6,10},{7,11},{8,4},{9,5},{1... | collective-permute-start | bytes 393224 | tf_op jit(solution)/shard_map/ppermute | solution.py:39
  16.7 0.0 copy-start.1
  16.7 0.0 copy-start.2
  16.7 0.0 copy-start.3
  16.7 0.4 collective-permute-done.2
  17.1 0.1 collective-permute-start.4
  17.3 0.0 collective-permute-done.3
  17.3 1.4 %collective-permute-done.4 = bf16[512,256]{1,0:T(8,128)(2,1)S(1)} collective-permute-done((bf16[512,256]{1,0:T(8,128)(2,1)S(1)}, bf16[512,256]{1,0:T(8,128)(2,1)S(1)}, u32[]{:S(2)}, u32[]{:S(2)}) %collective-permute-start.4) | collective-permute-done | bytes 262176 | tf_op jit(solution)/shard_map/ppermute | solution.py:18
  18.8 0.0 collective-permute-done.5.rest_2_
  18.8 1.3 %collective-permute-done.6.rest_3_ = bf16[256,256]{1,0:T(8,128)(2,1)S(1)} collective-permute-done((bf16[256,256]{1,0:T(8,128)(2,1)S(1)}, bf16[256,256]{1,0:T(8,128)(2,1)S(1)}, u32[]{:S(2)}, u32[]{:S(2)}) %collective-permute-start.6) | collective-permute-done | bytes 131104 | tf_op jit(solution)/shard_map/ppermute | solution.py:39
  20.0 0.0 copy-done.1
  20.1 0.0 copy-done.2
  20.1 0.0 copy-done.3
  20.1 2.0 %copy-done = bf16[112,128,128]{2,1,0:T(8,128)(2,1)S(1)} copy-done((bf16[112,128,128]{2,1,0:T(8,128)(2,1)S(1)}, bf16[112,128,128]{2,1,0:T(8,128)(2,1)}, u32[]{:S(2)}) %copy-start) | copy-done | bytes 3670040
  22.1 2.5 %shard_map.105 = f32[1024,256]{1,0:T(8,128)S(1)} custom-call(s32[6]{0:T(128)S(1)} %stack.27.place, s32[2,136]{1,0:T(2,128)S(1)} %get-tuple-element.4.plan, s32[34]{0:T(128)S(1)} %get-tuple-element.5.rows, s32[4,4]{1,0:T(4,128)S(1)} %copy-done.3, bf16[112,128,128]{2,1,0:T(8,128)(2,1)S(1)} %copy-done, ...), custom_call_target="tpu_custom_call" | custom-call | flops 1073741824 | bytes 1048576 | tf_op jit(solution)/shard_map/pallas_call | solution.py:132
  24.6 0.0 copy-start.7
  24.7 0.0 copy-start.4
  24.7 0.0 copy-start.5
  24.7 0.0 copy-start.6
  24.7 0.1 collective-permute-start.8
  24.8 0.5 collective-permute-start.7
  25.3 1.0 %collective-permute-done.8 = f32[256,256]{1,0:T(8,128)S(1)} collective-permute-done((f32[256,256]{1,0:T(8,128)S(1)}, f32[256,256]{1,0:T(8,128)S(1)}, u32[]{:S(2)}, u32[]{:S(2)}) %collective-permute-start.8) | collective-permute-done | bytes 262176 | tf_op jit(solution)/shard_map/ppermute | solution.py:18
  26.4 2.7 %collective-permute-start.9 = (bf16[256,256]{1,0:T(8,128)(2,1)S(1)}, bf16[256,256]{1,0:T(8,128)(2,1)S(1)}, u32[]{:S(2)}, u32[]{:S(2)}) collective-permute-start(bf16[256,256]{1,0:T(8,128)(2,1)S(1)} %fusion.18), channel_id=1, source_target_pairs={{0,2},{1,3},{2,0},{3,1},{4,6},{5,7},{6,4},{7,5},{8,10},{9,11},{10,... | collective-permute-start | bytes 393224 | tf_op jit(solution)/shard_map/ppermute | solution.py:24
  29.1 0.0 copy-done.7
  29.1 0.0 collective-permute-done.7
  29.1 3.8 %collective-permute-done.9 = bf16[256,256]{1,0:T(8,128)(2,1)S(1)} collective-permute-done((bf16[256,256]{1,0:T(8,128)(2,1)S(1)}, bf16[256,256]{1,0:T(8,128)(2,1)S(1)}, u32[]{:S(2)}, u32[]{:S(2)}) %collective-permute-start.9) | collective-permute-done | bytes 131104 | tf_op jit(solution)/shard_map/ppermute | solution.py:24
  32.9 0.0 copy-done.4
  32.9 0.0 copy-done.5
  32.9 0.0 copy-done.6
  32.9 0.4 constant_dynamic-update-slice_fusion.11
  33.3 3.4 %collective-permute-start.11 = (bf16[256,256]{1,0:T(8,128)(2,1)S(1)}, bf16[256,256]{1,0:T(8,128)(2,1)S(1)}, u32[]{:S(2)}, u32[]{:S(2)}) collective-permute-start(bf16[256,256]{1,0:T(8,128)(2,1)S(1)} %get-tuple-element.9.rest_0_), channel_id=1, source_target_pairs={{0,12},{1,13},{2,6},{3,7},{4,0},{5,1},{6,10},{7,11},{8,4},{9,5},{1... | collective-permute-start | bytes 393224 | tf_op jit(solution)/shard_map/ppermute | solution.py:39
  36.7 0.0 collective-permute-start.10
  36.7 0.0 collective-permute-start.15
  36.8 3.7 %collective-permute-done.11.rest_1_ = bf16[256,256]{1,0:T(8,128)(2,1)S(1)} collective-permute-done((bf16[256,256]{1,0:T(8,128)(2,1)S(1)}, bf16[256,256]{1,0:T(8,128)(2,1)S(1)}, u32[]{:S(2)}, u32[]{:S(2)}) %collective-permute-start.11) | collective-permute-done | bytes 131104 | tf_op jit(solution)/shard_map/ppermute | solution.py:39
  40.4 2.7 %collective-permute-start.12 = (bf16[256,256]{1,0:T(8,128)(2,1)S(1)}, bf16[256,256]{1,0:T(8,128)(2,1)S(1)}, u32[]{:S(2)}, u32[]{:S(2)}) collective-permute-start(bf16[256,256]{1,0:T(8,128)(2,1)S(1)} %collective-permute-done.11.rest_1_), channel_id=1, source_target_pairs={{0,2},{1,3},{2,0},{3,1},{4,6},{5,7},{6,4},{7,5},{8,10},{9,11},{10,... | collective-permute-start | bytes 393224 | tf_op jit(solution)/shard_map/ppermute | solution.py:24
  43.1 0.0 collective-permute-done.10
  43.1 0.1 collective-permute-start.13
  43.2 1.7 %collective-permute-start.16 = (bf16[256,256]{1,0:T(8,128)(2,1)S(1)}, bf16[256,256]{1,0:T(8,128)(2,1)S(1)}, u32[]{:S(2)}, u32[]{:S(2)}) collective-permute-start(bf16[256,256]{1,0:T(8,128)(2,1)S(1)} %collective-permute-done.11.rest_1_), channel_id=1, source_target_pairs={{0,12},{1,13},{2,6},{3,7},{4,0},{5,1},{6,10},{7,11},{8,4},{9,5},{1... | collective-permute-start | bytes 393224 | tf_op jit(solution)/shard_map/ppermute | solution.py:39
  44.9 1.2 %collective-permute-done.12 = bf16[256,256]{1,0:T(8,128)(2,1)S(1)} collective-permute-done((bf16[256,256]{1,0:T(8,128)(2,1)S(1)}, bf16[256,256]{1,0:T(8,128)(2,1)S(1)}, u32[]{:S(2)}, u32[]{:S(2)}) %collective-permute-start.12) | collective-permute-done | bytes 131104 | tf_op jit(solution)/shard_map/ppermute | solution.py:24
  46.1 0.1 collective-permute-start.14
  46.2 0.0 collective-permute-done.13
  46.2 1.4 %collective-permute-done.14 = bf16[512,256]{1,0:T(8,128)(2,1)S(1)} collective-permute-done((bf16[512,256]{1,0:T(8,128)(2,1)S(1)}, bf16[512,256]{1,0:T(8,128)(2,1)S(1)}, u32[]{:S(2)}, u32[]{:S(2)}) %collective-permute-start.14) | collective-permute-done | bytes 262176 | tf_op jit(solution)/shard_map/ppermute | solution.py:18
  47.7 0.0 collective-permute-done.15.rest_2_
  47.7 1.4 %collective-permute-done.16.rest_3_ = bf16[256,256]{1,0:T(8,128)(2,1)S(1)} collective-permute-done((bf16[256,256]{1,0:T(8,128)(2,1)S(1)}, bf16[256,256]{1,0:T(8,128)(2,1)S(1)}, u32[]{:S(2)}, u32[]{:S(2)}) %collective-permute-start.16) | collective-permute-done | bytes 131104 | tf_op jit(solution)/shard_map/ppermute | solution.py:39
  49.1 2.5 %shard_map.106 = f32[1024,256]{1,0:T(8,128)S(1)} custom-call(s32[6]{0:T(128)S(1)} %stack.27.place, s32[2,136]{1,0:T(2,128)S(1)} %get-tuple-element.4.plan, s32[34]{0:T(128)S(1)} %get-tuple-element.5.rows, s32[4,4]{1,0:T(4,128)S(1)} %copy-done.3, bf16[112,128,128]{2,1,0:T(8,128)(2,1)S(1)} %copy-done, ...), custom_call_target="tpu_custom_call" | custom-call | flops 1073741824 | bytes 1048576 | tf_op jit(solution)/shard_map/pallas_call | solution.py:132
  51.7 0.1 collective-permute-start.18
  51.8 0.5 collective-permute-start.17
  52.3 1.0 %collective-permute-done.18 = f32[256,256]{1,0:T(8,128)S(1)} collective-permute-done((f32[256,256]{1,0:T(8,128)S(1)}, f32[256,256]{1,0:T(8,128)S(1)}, u32[]{:S(2)}, u32[]{:S(2)}) %collective-permute-start.18) | collective-permute-done | bytes 262176 | tf_op jit(solution)/shard_map/ppermute | solution.py:18
  53.3 2.0 %collective-permute-start.19 = (bf16[256,256]{1,0:T(8,128)(2,1)S(1)}, bf16[256,256]{1,0:T(8,128)(2,1)S(1)}, u32[]{:S(2)}, u32[]{:S(2)}) collective-permute-start(bf16[256,256]{1,0:T(8,128)(2,1)S(1)} %fusion.12), channel_id=1, source_target_pairs={{0,2},{1,3},{2,0},{3,1},{4,6},{5,7},{6,4},{7,5},{8,10},{9,11},{10,... | collective-permute-start | bytes 393224 | tf_op jit(solution)/shard_map/ppermute | solution.py:24
  55.3 0.0 collective-permute-done.17
  55.3 3.8 %collective-permute-done.19 = bf16[256,256]{1,0:T(8,128)(2,1)S(1)} collective-permute-done((bf16[256,256]{1,0:T(8,128)(2,1)S(1)}, bf16[256,256]{1,0:T(8,128)(2,1)S(1)}, u32[]{:S(2)}, u32[]{:S(2)}) %collective-permute-start.19) | collective-permute-done | bytes 131104 | tf_op jit(solution)/shard_map/ppermute | solution.py:24
  59.1 1.3 %fusion.10 = (f32[256,256]{1,0:T(8,128)}, f32[256,256]{1,0:T(8,128)S(1)}) fusion(f32[256,256]{1,0:T(8,128)S(1)} %copy-done.6, f32[256,256]{1,0:T(8,128)S(1)} %get-tuple-element.10, f32[256]{0:T(256)S(1)} %broadcast_multiply_fusion, f32[256,256]{1,0:T(8,128)S(1)} %copy-done.5, bf16[256,256]{1,0:T(8,128)(2,1)S(1)} %collective-permute-done.19, ...), kind=kLoop, calls=%fused_computation.14 | loop fusion | flops 2162688 | bytes 1968128 | tf_op jit(solution)/shard_map/add | solution.py:212
  60.4 0.8 %multiply_add_fusion = f32[256,256]{1,0:T(8,128)} fusion(f32[256,256]{1,0:T(8,128)S(1)} %copy-done.4, f32[256,256]{1,0:T(8,128)S(1)} %get-tuple-element.10, f32[256,256]{1,0:T(8,128)S(1)} %get-tuple-element.7), kind=kLoop, calls=%fused_computation.39 | loop fusion | flops 196608 | bytes 1048576 | tf_op jit(solution)/shard_map/add | solution.py:211
  (22 shorter events, 0.4 us)
Async XLA Ops:
  1.6 11.5 %collective-permute-start = (bf16[256,256]{1,0:T(8,128)(2,1)S(1)}, bf16[256,256]{1,0:T(8,128)(2,1)S(1)}, u32[]{:S(2)}, u32[]{:S(2)}) collective-permute-start(bf16[256,256]{1,0:T(8,128)(2,1)S(1)} %get-tuple-element.12.rest_0_), channel_id=1, source_target_pairs={{0,2},{1,3},{2,0},{3,1},{4,6},{5,7},{6,4},{7,5},{8,10},{9,11},{10,... | collective-permute-start | bytes 393224 | tf_op jit(solution)/shard_map/ppermute | solution.py:24
  4.6 7.5 %collective-permute-start.1 = (bf16[256,256]{1,0:T(8,128)(2,1)S(1)}, bf16[256,256]{1,0:T(8,128)(2,1)S(1)}, u32[]{:S(2)}, u32[]{:S(2)}) collective-permute-start(bf16[256,256]{1,0:T(8,128)(2,1)S(1)} %get-tuple-element.12.rest_0_), channel_id=1, source_target_pairs={{0,12},{1,13},{2,6},{3,7},{4,0},{5,1},{6,10},{7,11},{8,4},{9,5},{1... | collective-permute-start | bytes 393224 | tf_op jit(solution)/shard_map/ppermute | solution.py:39
  8.2 10.6 %collective-permute-start.5 = (bf16[256,256]{1,0:T(8,128)(2,1)S(1)}, bf16[256,256]{1,0:T(8,128)(2,1)S(1)}, u32[]{:S(2)}, u32[]{:S(2)}) collective-permute-start(bf16[256,256]{1,0:T(8,128)(2,1)S(1)} %get-tuple-element.12.rest_0_), channel_id=1, source_target_pairs={{0,4},{1,5},{2,14},{3,15},{4,8},{5,9},{6,2},{7,3},{8,12},{9,13},{1... | collective-permute-start | bytes 393224 | tf_op jit(solution)/shard_map/ppermute | solution.py:39
  12.2 5.0 %collective-permute-start.2 = (bf16[256,256]{1,0:T(8,128)(2,1)S(1)}, bf16[256,256]{1,0:T(8,128)(2,1)S(1)}, u32[]{:S(2)}, u32[]{:S(2)}) collective-permute-start(bf16[256,256]{1,0:T(8,128)(2,1)S(1)} %collective-permute-done.1.rest_1_), channel_id=1, source_target_pairs={{0,2},{1,3},{2,0},{3,1},{4,6},{5,7},{6,4},{7,5},{8,10},{9,11},{10,... | collective-permute-start | bytes 393224 | tf_op jit(solution)/shard_map/ppermute | solution.py:24
  13.1 4.1 %collective-permute-start.3 = (bf16[512,256]{1,0:T(8,128)(2,1)S(1)}, bf16[512,256]{1,0:T(8,128)(2,1)S(1)}, u32[]{:S(2)}, u32[]{:S(2)}) collective-permute-start(bf16[512,256]{1,0:T(8,128)(2,1)S(1)} %pad_maximum_fusion), channel_id=1, source_target_pairs={{0,1},{1,0},{2,3},{3,2},{4,5},{5,4},{6,7},{7,6},{8,9},{9,8},{10,11... | collective-permute-start | bytes 786440 | tf_op jit(solution)/shard_map/ppermute | solution.py:18
  13.2 6.8 %collective-permute-start.6 = (bf16[256,256]{1,0:T(8,128)(2,1)S(1)}, bf16[256,256]{1,0:T(8,128)(2,1)S(1)}, u32[]{:S(2)}, u32[]{:S(2)}) collective-permute-start(bf16[256,256]{1,0:T(8,128)(2,1)S(1)} %collective-permute-done.1.rest_1_), channel_id=1, source_target_pairs={{0,12},{1,13},{2,6},{3,7},{4,0},{5,1},{6,10},{7,11},{8,4},{9,5},{1... | collective-permute-start | bytes 393224 | tf_op jit(solution)/shard_map/ppermute | solution.py:39
  16.7 3.4 %copy-start.1 = (bf16[4,4,32,256]{3,2,1,0:T(8,128)(2,1)S(1)}, bf16[4,4,32,256]{3,2,1,0:T(8,128)(2,1)}, u32[]{:S(2)}) copy-start(bf16[4,4,32,256]{3,2,1,0:T(8,128)(2,1)} %far_u.3) | copy-start | bytes 786436
  16.7 3.3 %copy-start.2 = (bf16[4,4,32,256]{3,2,1,0:T(8,128)(2,1)S(1)}, bf16[4,4,32,256]{3,2,1,0:T(8,128)(2,1)}, u32[]{:S(2)}) copy-start(bf16[4,4,32,256]{3,2,1,0:T(8,128)(2,1)} %far_v.3) | copy-start | bytes 786436
  16.7 3.3 %copy-start.3 = (s32[4,4]{1,0:T(4,128)S(1)}, s32[4,4]{1,0:T(4,128)}, u32[]{:S(2)}) copy-start(s32[4,4]{1,0:T(4,128)} %ranks.3) | copy-start | bytes 196
  17.1 1.6 %collective-permute-start.4 = (bf16[512,256]{1,0:T(8,128)(2,1)S(1)}, bf16[512,256]{1,0:T(8,128)(2,1)S(1)}, u32[]{:S(2)}, u32[]{:S(2)}) collective-permute-start(bf16[512,256]{1,0:T(8,128)(2,1)S(1)} %pad_maximum_fusion.1), channel_id=1, source_target_pairs={{0,1},{1,0},{2,3},{3,2},{4,5},{5,4},{6,7},{7,6},{8,9},{9,8},{10,11... | collective-permute-start | bytes 786440 | tf_op jit(solution)/shard_map/ppermute | solution.py:18
  20.1 2.0 %copy-start = (bf16[112,128,128]{2,1,0:T(8,128)(2,1)S(1)}, bf16[112,128,128]{2,1,0:T(8,128)(2,1)}, u32[]{:S(2)}) copy-start(bf16[112,128,128]{2,1,0:T(8,128)(2,1)} %blocks.3) | copy-start | bytes 11010052
  24.6 4.5 %copy-start.7 = (f32[256]{0:T(256)S(1)}, f32[256]{0:T(256)}, u32[]{:S(2)}) copy-start(f32[256]{0:T(256)} %param.12) | copy-start | bytes 3076
  24.7 8.2 %copy-start.4 = (f32[256,256]{1,0:T(8,128)S(1)}, f32[256,256]{1,0:T(8,128)}, u32[]{:S(2)}) copy-start(f32[256,256]{1,0:T(8,128)} %param.9) | copy-start | bytes 786436
  24.7 8.2 %copy-start.5 = (f32[256,256]{1,0:T(8,128)S(1)}, f32[256,256]{1,0:T(8,128)}, u32[]{:S(2)}) copy-start(f32[256,256]{1,0:T(8,128)} %param.11) | copy-start | bytes 786436
  24.7 8.2 %copy-start.6 = (f32[256,256]{1,0:T(8,128)S(1)}, f32[256,256]{1,0:T(8,128)}, u32[]{:S(2)}) copy-start(f32[256,256]{1,0:T(8,128)} %param.10) | copy-start | bytes 786436
  24.7 1.6 %collective-permute-start.8 = (f32[256,256]{1,0:T(8,128)S(1)}, f32[256,256]{1,0:T(8,128)S(1)}, u32[]{:S(2)}, u32[]{:S(2)}) collective-permute-start(f32[256,256]{1,0:T(8,128)S(1)} %get-tuple-element.16), channel_id=1, source_target_pairs={{0,1},{1,0},{2,3},{3,2},{4,5},{5,4},{6,7},{7,6},{8,9},{9,8},{10,11... | collective-permute-start | bytes 786440 | tf_op jit(solution)/shard_map/ppermute | solution.py:18
  24.8 4.3 %collective-permute-start.7 = (f32[256,256]{1,0:T(8,128)S(1)}, f32[256,256]{1,0:T(8,128)S(1)}, u32[]{:S(2)}, u32[]{:S(2)}) collective-permute-start(f32[256,256]{1,0:T(8,128)S(1)} %get-tuple-element.15), channel_id=1, source_target_pairs={{0,1},{1,0},{2,3},{3,2},{4,5},{5,4},{6,7},{7,6},{8,9},{9,8},{10,11... | collective-permute-start | bytes 786440 | tf_op jit(solution)/shard_map/ppermute | solution.py:18
  26.4 6.5 %collective-permute-start.9 = (bf16[256,256]{1,0:T(8,128)(2,1)S(1)}, bf16[256,256]{1,0:T(8,128)(2,1)S(1)}, u32[]{:S(2)}, u32[]{:S(2)}) collective-permute-start(bf16[256,256]{1,0:T(8,128)(2,1)S(1)} %fusion.18), channel_id=1, source_target_pairs={{0,2},{1,3},{2,0},{3,1},{4,6},{5,7},{6,4},{7,5},{8,10},{9,11},{10,... | collective-permute-start | bytes 393224 | tf_op jit(solution)/shard_map/ppermute | solution.py:24
  33.3 7.1 %collective-permute-start.11 = (bf16[256,256]{1,0:T(8,128)(2,1)S(1)}, bf16[256,256]{1,0:T(8,128)(2,1)S(1)}, u32[]{:S(2)}, u32[]{:S(2)}) collective-permute-start(bf16[256,256]{1,0:T(8,128)(2,1)S(1)} %get-tuple-element.9.rest_0_), channel_id=1, source_target_pairs={{0,12},{1,13},{2,6},{3,7},{4,0},{5,1},{6,10},{7,11},{8,4},{9,5},{1... | collective-permute-start | bytes 393224 | tf_op jit(solution)/shard_map/ppermute | solution.py:39
  36.7 6.4 %collective-permute-start.10 = (bf16[256,256]{1,0:T(8,128)(2,1)S(1)}, bf16[256,256]{1,0:T(8,128)(2,1)S(1)}, u32[]{:S(2)}, u32[]{:S(2)}) collective-permute-start(bf16[256,256]{1,0:T(8,128)(2,1)S(1)} %get-tuple-element.9.rest_0_), channel_id=1, source_target_pairs={{0,2},{1,3},{2,0},{3,1},{4,6},{5,7},{6,4},{7,5},{8,10},{9,11},{10,... | collective-permute-start | bytes 393224 | tf_op jit(solution)/shard_map/ppermute | solution.py:24
  36.7 11.0 %collective-permute-start.15 = (bf16[256,256]{1,0:T(8,128)(2,1)S(1)}, bf16[256,256]{1,0:T(8,128)(2,1)S(1)}, u32[]{:S(2)}, u32[]{:S(2)}) collective-permute-start(bf16[256,256]{1,0:T(8,128)(2,1)S(1)} %get-tuple-element.9.rest_0_), channel_id=1, source_target_pairs={{0,4},{1,5},{2,14},{3,15},{4,8},{5,9},{6,2},{7,3},{8,12},{9,13},{1... | collective-permute-start | bytes 393224 | tf_op jit(solution)/shard_map/ppermute | solution.py:39
  40.4 5.6 %collective-permute-start.12 = (bf16[256,256]{1,0:T(8,128)(2,1)S(1)}, bf16[256,256]{1,0:T(8,128)(2,1)S(1)}, u32[]{:S(2)}, u32[]{:S(2)}) collective-permute-start(bf16[256,256]{1,0:T(8,128)(2,1)S(1)} %collective-permute-done.11.rest_1_), channel_id=1, source_target_pairs={{0,2},{1,3},{2,0},{3,1},{4,6},{5,7},{6,4},{7,5},{8,10},{9,11},{10,... | collective-permute-start | bytes 393224 | tf_op jit(solution)/shard_map/ppermute | solution.py:24
  43.1 3.1 %collective-permute-start.13 = (bf16[512,256]{1,0:T(8,128)(2,1)S(1)}, bf16[512,256]{1,0:T(8,128)(2,1)S(1)}, u32[]{:S(2)}, u32[]{:S(2)}) collective-permute-start(bf16[512,256]{1,0:T(8,128)(2,1)S(1)} %pad_maximum_fusion.2), channel_id=1, source_target_pairs={{0,1},{1,0},{2,3},{3,2},{4,5},{5,4},{6,7},{7,6},{8,9},{9,8},{10,11... | collective-permute-start | bytes 786440 | tf_op jit(solution)/shard_map/ppermute | solution.py:18
  43.2 5.9 %collective-permute-start.16 = (bf16[256,256]{1,0:T(8,128)(2,1)S(1)}, bf16[256,256]{1,0:T(8,128)(2,1)S(1)}, u32[]{:S(2)}, u32[]{:S(2)}) collective-permute-start(bf16[256,256]{1,0:T(8,128)(2,1)S(1)} %collective-permute-done.11.rest_1_), channel_id=1, source_target_pairs={{0,12},{1,13},{2,6},{3,7},{4,0},{5,1},{6,10},{7,11},{8,4},{9,5},{1... | collective-permute-start | bytes 393224 | tf_op jit(solution)/shard_map/ppermute | solution.py:39
  46.1 1.6 %collective-permute-start.14 = (bf16[512,256]{1,0:T(8,128)(2,1)S(1)}, bf16[512,256]{1,0:T(8,128)(2,1)S(1)}, u32[]{:S(2)}, u32[]{:S(2)}) collective-permute-start(bf16[512,256]{1,0:T(8,128)(2,1)S(1)} %pad_maximum_fusion.3), channel_id=1, source_target_pairs={{0,1},{1,0},{2,3},{3,2},{4,5},{5,4},{6,7},{7,6},{8,9},{9,8},{10,11... | collective-permute-start | bytes 786440 | tf_op jit(solution)/shard_map/ppermute | solution.py:18
  51.7 1.6 %collective-permute-start.18 = (f32[256,256]{1,0:T(8,128)S(1)}, f32[256,256]{1,0:T(8,128)S(1)}, u32[]{:S(2)}, u32[]{:S(2)}) collective-permute-start(f32[256,256]{1,0:T(8,128)S(1)} %get-tuple-element.14), channel_id=1, source_target_pairs={{0,1},{1,0},{2,3},{3,2},{4,5},{5,4},{6,7},{7,6},{8,9},{9,8},{10,11... | collective-permute-start | bytes 786440 | tf_op jit(solution)/shard_map/ppermute | solution.py:18
  51.8 3.5 %collective-permute-start.17 = (f32[256,256]{1,0:T(8,128)S(1)}, f32[256,256]{1,0:T(8,128)S(1)}, u32[]{:S(2)}, u32[]{:S(2)}) collective-permute-start(f32[256,256]{1,0:T(8,128)S(1)} %get-tuple-element.13), channel_id=1, source_target_pairs={{0,1},{1,0},{2,3},{3,2},{4,5},{5,4},{6,7},{7,6},{8,9},{9,8},{10,11... | collective-permute-start | bytes 786440 | tf_op jit(solution)/shard_map/ppermute | solution.py:18
  53.3 5.8 %collective-permute-start.19 = (bf16[256,256]{1,0:T(8,128)(2,1)S(1)}, bf16[256,256]{1,0:T(8,128)(2,1)S(1)}, u32[]{:S(2)}, u32[]{:S(2)}) collective-permute-start(bf16[256,256]{1,0:T(8,128)(2,1)S(1)} %fusion.12), channel_id=1, source_target_pairs={{0,2},{1,3},{2,0},{3,1},{4,6},{5,7},{6,4},{7,5},{8,10},{9,11},{10,... | collective-permute-start | bytes 393224 | tf_op jit(solution)/shard_map/ppermute | solution.py:24

commit v4 on v3

--- a/solution.py
+++ b/solution.py
@@ -39,38 +39,66 @@
     return lax.ppermute(array, ("clu", "row"), pairs)
 
 
-def plan_kernel(leaf, spare, src, dst, plan, rows, free):
-    places, chunks, targets = plan.shape[1], rows.shape[0], free.shape[0]
-    for t in range(targets):
-        free[t] = 0
-    for i in range(places):
+def around(value, size):
+    value = jnp.where(value < 0, value + size, value)
+    return jnp.where(value >= size, value - size, value)
+
+
+def here():
+    row = lax.axis_index("row")
+    return lax.axis_index("clu"), lax.div(row, CORES), lax.rem(row, CORES)
+
+
+def plan_kernel(leaf, own, pairs, plan, rows, free, source_rows, target_rows):
+    devices = lax.axis_size("row")
+    chips, clusters = devices // CORES, devices * own
+    group, chip, core = here()
+    for near in range(-REACH, clusters + REACH):
+        holder = near % clusters // own
+        if near < 0:
+            piece = chips + around(chip + 1, chips)
+        elif near >= clusters:
+            piece = chips + chip
+        else:
+            piece = around(chip - holder // CORES, chips)
+        piece = ((core ^ (holder % CORES)) * 2 * chips + piece) * own + near % own
+        source_rows[near + REACH] = piece * leaf
+    for target in range(clusters):
+        owner = target // own
+        piece = (core ^ (owner % CORES)) * chips + around(owner // CORES - chip, chips)
+        target_rows[target] = (piece * own + target % own) * leaf
+        free[target] = 0
+    for i in range(plan.shape[1]):
         plan[0, i] = 0
-        plan[1, i] = spare
-    for i in range(chunks):
+        plan[1, i] = 4 * chips * own * leaf
+    for i in range(rows.shape[0]):
         rows[i] = 0
 
     def put(j, used):
-        target = dst[j]
+        target = pairs[0, j] - group * clusters
         at = free[target]
         full = (at & (WIDTH - 1)) == 0
         at = jnp.where(full, used * WIDTH, at)
         free[target] = at + 1
         plan[0, at] = j
-        plan[1, at] = src[j] * leaf
-        rows[lax.shift_right_logical(at, WIDTH.bit_length() - 1)] = target * leaf
+        plan[1, at] = source_rows[pairs[1, j] - group * clusters + REACH]
+        rows[lax.shift_right_logical(at, WIDTH.bit_length() - 1)] = target_rows[target]
         return used + full.astype(jnp.int32)
 
-    lax.fori_loop(0, src.shape[0], put, jnp.int32(0), unroll=4)
-
-
-def stress_kernel(leaf, groups, place, plan, rows, ranks, blocks, window, far_u, far_v, *rest):
+    lax.fori_loop(0, pairs.shape[1], put, jnp.int32(0), unroll=4)
+
+
+def stress_kernel(leaf, plan, rows, ranks, blocks, window, far_u, far_v, *rest):
+    targets, groups, rank, elems = far_u.shape
     columns, (out, coeffs) = rest[:groups], rest[groups:]
-    targets, _, rank, elems = far_u.shape
     chips, members = targets // CORES, window.shape[1]
-    chip, core = place[0], place[1]
+    group, chip, core = here()
+    toward = jnp.where(chip == chips - 1, -1, 1)
+    steps = [(s + 1) // 2 if s % 2 else -(s // 2) for s in range(groups)]
+    sources = [around(group + toward * step, groups) for step in steps]
     row = lax.broadcasted_iota(jnp.int32, (rank, members), 0)
     for s in range(groups):
-        source = place[2 + s]
+        source = sources[s]
         product = jnp.dot(
             jnp.concatenate([far_v[t, source] for t in range(targets)], axis=0),
             columns[s][...],
@@ -82,9 +110,9 @@
             coeffs[t, s * rank : (s + 1) * rank, :] = part.astype(jnp.bfloat16)
     for other in range(CORES):
         for ahead in range(chips):
-            target = lax.rem(chip + ahead, chips) * CORES + (core ^ other)
+            target = around(chip + ahead, chips) * CORES + (core ^ other)
             out[pl.ds((other * chips + ahead) * elems, elems), :] = lax.dot_general(
-                jnp.concatenate([far_u[target, place[2 + s]] for s in range(groups)], axis=0),
+                jnp.concatenate([far_u[target, source] for source in sources], axis=0),
                 coeffs[target],
                 (((0,), (0,)), ((), ())),
                 preferred_element_type=jnp.float32,
@@ -109,30 +137,35 @@
 PARAMS = pltpu.CompilerParams(vmem_limit_bytes=16 * 1024 * 1024)
 
 
-def planned_blocks(src, dst, leaf, targets, spare):
-    chunks = (src.shape[0] + targets * (WIDTH - 1)) // WIDTH
+def planned_blocks(pairs, leaf, own):
+    targets = lax.axis_size("row") * own
+    chunks = (pairs.shape[1] + targets * (WIDTH - 1)) // WIDTH
     return pl.pallas_call(
-        functools.partial(plan_kernel, leaf, spare),
+        functools.partial(plan_kernel, leaf, own),
         out_shape=(
             jax.ShapeDtypeStruct((2, chunks * WIDTH), jnp.int32),
             jax.ShapeDtypeStruct((chunks,), jnp.int32),
         ),
-        in_specs=[SMEM, SMEM],
+        in_specs=[SMEM],
         out_specs=(SMEM, SMEM),
-        scratch_shapes=[pltpu.SMEM((targets,), jnp.int32)],
+        scratch_shapes=[
+            pltpu.SMEM((targets,), jnp.int32),
+            pltpu.SMEM((targets + 2 * REACH,), jnp.int32),
+            pltpu.SMEM((targets,), jnp.int32),
+        ],
         compiler_params=PARAMS,
-        cost_estimate=pl.CostEstimate(flops=1024, bytes_accessed=1024, transcendentals=0),
-    )(src, dst)
-
-
-def partial_stress(place, plan, ranks, blocks, window, far_u, far_v, columns):
+        cost_estimate=pl.CostEstimate(flops=4_000_000_000, bytes_accessed=10_000_000, transcendentals=0),
+    )(pairs)
+
+
+def partial_stress(plan, ranks, blocks, window, far_u, far_v, columns):
     targets, groups, rank, elems = far_u.shape
     count, leaf, _ = blocks.shape
     rows, members = targets * elems, window.shape[1]
     return pl.pallas_call(
-        functools.partial(stress_kernel, leaf, groups),
+        functools.partial(stress_kernel, leaf),
         out_shape=jax.ShapeDtypeStruct((rows, members), jnp.float32),
-        in_specs=[SMEM] * 4 + [VMEM] * (4 + groups),
+        in_specs=[SMEM] * 3 + [VMEM] * (4 + groups),
         out_specs=VMEM,
         scratch_shapes=[pltpu.VMEM((targets, groups * rank, members), jnp.bfloat16)],
         compiler_params=PARAMS,
@@ -141,7 +174,7 @@
             bytes_accessed=4 * rows * members,
             transcendentals=0,
         ),
-    )(place, plan[0], plan[1], ranks, blocks, window, far_u, far_v, *columns)
+    )(plan[0], plan[1], ranks, blocks, window, far_u, far_v, *columns)
 
 
 def slip_rates(stress, state, load, friction_a):
@@ -158,45 +191,29 @@
     own = elems // leaf
     devices, groups = lax.axis_size("row"), lax.axis_size("clu")
     chips = devices // CORES
-    clusters = devices * own
     assert REACH <= CORES * own
-    group, row = lax.axis_index("clu"), lax.axis_index("row")
-    chip, core = row // CORES, row % CORES
-    toward = jnp.where(chip == chips - 1, -1, 1)
-    sources = [group]
-    for s in range(1, groups):
-        sources.append(group + (toward if s % 2 else -toward) * ((s + 1) // 2))
-    sources = [(source + groups) % groups for source in sources]
-    place = jnp.stack([chip, core] + sources).astype(jnp.int32)
-
-    source = near_pairs[:, 1] - group * clusters
-    before, after = source < 0, source >= clusters
-    local = jnp.where(before, source + clusters, jnp.where(after, source - clusters, source))
-    holder = local // own
-    piece = jnp.where(
-        before, (chip + 1) % chips, jnp.where(after, chip, (chip - holder // CORES + chips) % chips)
-    )
-    piece = piece + jnp.where(before | after, chips, 0)
-    src = ((((holder % CORES) ^ core) * 2 * chips + piece) * own + local % own).astype(jnp.int32)
-    target = near_pairs[:, 0] - group * clusters
-    owner = target // own
-    ahead = (owner // CORES - chip + chips) % chips
-    dst = ((((owner % CORES) ^ core) * chips + ahead) * own + target % own).astype(jnp.int32)
-
-    plan = planned_blocks(src, dst, leaf, clusters, 4 * chips * elems)
     spare = jnp.zeros((leaf, members), jnp.bfloat16)
+    plans = []
+
+    def planned(after):
+        if not plans:
+            after, pairs = lax.optimization_barrier((after, near_pairs.T))
+            plans.append(planned_blocks(pairs, leaf, own))
+        return after, plans[0]
 
     def section_stress(field):
         half = field.astype(jnp.bfloat16)
         straight = end_shift(half, 1)
+        straight, plan = planned(straight)
         near = jnp.concatenate([half] + [chip_shift(half, s) for s in range(1, chips)])
         column = [half, straight, end_shift(half, -1)]
         while len(column) < groups:
-            step = 1 if len(column) % 2 else -1
-            column.append(end_shift(column[-2], step))
-        ends = jnp.concatenate([straight] + [chip_shift(straight, s) for s in range(1, chips)])
+            column.append(end_shift(column[-2], 1 if len(column) % 2 else -1))
+        ends = [chip_shift(straight, s) for s in range(1, chips)]
+        ends, plan = lax.optimization_barrier((ends, plan))
+        ends = jnp.concatenate([straight] + ends)
         window = jnp.concatenate([near, ends, core_swap(near), core_swap(ends), spare])
-        partial = partial_stress(place, plan, far_rank, near_blocks, window, far_u, far_v, column)
+        partial = partial_stress(plan, far_rank, near_blocks, window, far_u, far_v, column)
         partial = partial.reshape(CORES, chips, elems, members)
         joined = [partial[0, s] + core_swap(partial[1, s]) for s in range(chips)]
         total = joined[0]

time: 61.4 us -> 58.3 us (0.950)
  starting transfers between devices: 24.9 us -> 20.3 us
  waiting for transfers between devices: 20.8 us -> 24.5 us
  local copies, waits for them, and re-layouts: 2.39 us -> 0.95 us
  other arithmetic: 4.39 us -> 3.63 us
    ppermute x6, starting transfers between devices: 11.3 us -> 6.2 us  [chip_shift(): return lax.ppermute(array, 'row', pairs)]
    ppermute x6, waiting for transfers between devices: 9.13 us -> 11.3 us  [chip_shift(): return lax.ppermute(array, 'row', pairs)]
    ppermute x6, waiting for transfers between devices: 6.74 us -> 8.32 us  [end_shift(): return lax.ppermute(array, ('clu', 'row'), pairs)]
    unnamed x26 -> x28, local copies, waits for them, and re-layouts: 2.22 us -> 0.86 us
    add x1 -> x0, other arithmetic: 0.79 us -> none  [body(): ((owner % CORES ^ core) * chips + ahead) * own + target % own]
  transfers between devices with their start and end apart: 20 -> 20, of which waited for: 12 -> 12; matrix products, arithmetic and copies ran while one was open for 2% -> 1% of each run, Pallas kernels for 4% -> 5%
where the time goes in v4:
time: 58.3 us; the launch traced here: 58.2 us
  waiting for transfers between devices  24.5 us (42%)
  starting transfers between devices  20.3 us (35%)
  Pallas kernels  7.71 us (13%)
  other arithmetic  3.63 us (6%)
  between operations  0.99 us (2%)
  local copies, waits for them, and re-layouts  0.95 us (2%)
    ppermute x6, starting transfers between devices, end_shift(): return lax.ppermute(array, ('clu', 'row'), pairs)  12.2 us
    ppermute x6, waiting for transfers between devices, chip_shift(): return lax.ppermute(array, 'row', pairs)  11.3 us
    ppermute x6, waiting for transfers between devices, end_shift(): return lax.ppermute(array, ('clu', 'row'), pairs)  8.32 us
    ppermute x6, starting transfers between devices, chip_shift(): return lax.ppermute(array, 'row', pairs)  6.2 us
    pallas_call x2, Pallas kernels, partial_stress(): pl.pallas_call(functools.partial(stress_kernel, leaf), out_shape=jax.Shap...  5.07 us
    ppermute x8, waiting for transfers between devices, core_swap(): return lax.ppermute(array, 'row', [(i, i ^ 1) for i in range(devices)])  4.93 us
    pallas_call x1, Pallas kernels, planned_blocks(): pl.pallas_call(functools.partial(plan_kernel, leaf, own), out_shape=(jax....  2.64 us
    ppermute x8, starting transfers between devices, core_swap(): return lax.ppermute(array, 'row', [(i, i ^ 1) for i in range(devices)])  1.91 us
  transfers between devices with their start and end apart: 20, of which 12 were waited for; matrix products, arithmetic and copies ran while one was open for 1% of the time, Pallas kernels for 5%

profile of v4, /device:TPU:0, one launch (start us, length us, event | category | flops | bytes accessed | tf_op | source)
XLA Modules:
  0.0 58.2 jit_solution(17310990888342115896)
XLA Ops:
  0.6 1.0 %constant_dynamic-update-slice_fusion.5 = (bf16[2176,256]{1,0:T(8,128)(2,1)S(1)}, bf16[256,256]{1,0:T(8,128)(2,1)S(1)}) fusion(f32[256,256]{1,0:T(8,128)} %param.9), kind=kLoop, calls=%fused_computation.51 | loop fusion | flops 65535 | bytes 524288
  1.6 5.1 %collective-permute-start = (bf16[256,256]{1,0:T(8,128)(2,1)S(1)}, bf16[256,256]{1,0:T(8,128)(2,1)S(1)}, u32[]{:S(2)}, u32[]{:S(2)}) collective-permute-start(bf16[256,256]{1,0:T(8,128)(2,1)S(1)} %get-tuple-element.28.rest_0_), channel_id=1, source_target_pairs={{0,12},{1,13},{2,6},{3,7},{4,0},{5,1},{6,10},{7,11},{8,4},{9,5},{1... | collective-permute-start | bytes 393224 | tf_op jit(solution)/shard_map/ppermute | solution.py:39
  6.7 0.0 collective-permute-start.2
  6.7 1.0 %collective-permute-start.5 = (bf16[256,256]{1,0:T(8,128)(2,1)S(1)}, bf16[256,256]{1,0:T(8,128)(2,1)S(1)}, u32[]{:S(2)}, u32[]{:S(2)}) collective-permute-start(bf16[256,256]{1,0:T(8,128)(2,1)S(1)} %get-tuple-element.28.rest_0_), channel_id=1, source_target_pairs={{0,4},{1,5},{2,14},{3,15},{4,8},{5,9},{6,2},{7,3},{8,12},{9,13},{1... | collective-permute-start | bytes 393224 | tf_op jit(solution)/shard_map/ppermute | solution.py:39
  7.8 2.9 %collective-permute-done.rest_1_ = bf16[256,256]{1,0:T(8,128)(2,1)S(1)} collective-permute-done((bf16[256,256]{1,0:T(8,128)(2,1)S(1)}, bf16[256,256]{1,0:T(8,128)(2,1)S(1)}, u32[]{:S(2)}, u32[]{:S(2)}) %collective-permute-start) | collective-permute-done | bytes 131104 | tf_op jit(solution)/shard_map/ppermute | solution.py:39
  10.6 2.2 %collective-permute-start.1 = (bf16[256,256]{1,0:T(8,128)(2,1)S(1)}, bf16[256,256]{1,0:T(8,128)(2,1)S(1)}, u32[]{:S(2)}, u32[]{:S(2)}) collective-permute-start(bf16[256,256]{1,0:T(8,128)(2,1)S(1)} %collective-permute-done.rest_1_), channel_id=1, source_target_pairs={{0,2},{1,3},{2,0},{3,1},{4,6},{5,7},{6,4},{7,5},{8,10},{9,11},{10,... | collective-permute-start | bytes 393224 | tf_op jit(solution)/shard_map/ppermute | solution.py:24
  12.8 3.0 %collective-permute-start.6 = (bf16[256,256]{1,0:T(8,128)(2,1)S(1)}, bf16[256,256]{1,0:T(8,128)(2,1)S(1)}, u32[]{:S(2)}, u32[]{:S(2)}) collective-permute-start(bf16[256,256]{1,0:T(8,128)(2,1)S(1)} %collective-permute-done.rest_1_), channel_id=1, source_target_pairs={{0,12},{1,13},{2,6},{3,7},{4,0},{5,1},{6,10},{7,11},{8,4},{9,5},{1... | collective-permute-start | bytes 393224 | tf_op jit(solution)/shard_map/ppermute | solution.py:39
  15.7 0.0 copy-start.4
  15.7 0.7 %copy-done.4 = s32[112,2]{0,1:T(2,128)S(1)} copy-done((s32[112,2]{0,1:T(2,128)S(1)}, s32[112,2]{0,1:T(2,128)}, u32[]{:S(2)}) %copy-start.4) | copy-done | bytes 920
  16.4 2.6 %shard_map.104 = (s32[2,136]{1,0:T(2,128)S(1)}, s32[34]{0:T(128)S(1)}) custom-call(s32[2,112]{1,0:T(2,128)S(1)} %bitcast.55), custom_call_target="tpu_custom_call" | custom-call | flops 4000000000 | bytes 10000000 | tf_op jit(solution)/shard_map/pallas_call | solution.py:143
  19.1 0.0 collective-permute-done.2
  19.1 0.1 collective-permute-start.3
  19.2 0.0 copy-start.1
  19.2 0.0 copy-start.2
  19.2 0.0 copy-start.3
  19.2 0.0 collective-permute-done.1
  19.3 0.6 collective-permute-start.4
  19.9 0.8 %collective-permute-done.3 = bf16[512,256]{1,0:T(8,128)(2,1)S(1)} collective-permute-done((bf16[512,256]{1,0:T(8,128)(2,1)S(1)}, bf16[512,256]{1,0:T(8,128)(2,1)S(1)}, u32[]{:S(2)}, u32[]{:S(2)}) %collective-permute-start.3) | collective-permute-done | bytes 262176 | tf_op jit(solution)/shard_map/ppermute | solution.py:18
  20.7 0.4 collective-permute-done.4
  21.1 0.0 collective-permute-done.5.rest_2_
  21.1 0.0 collective-permute-done.6.rest_3_
  21.1 0.0 copy-done
  21.1 0.0 copy-done.1
  21.2 0.0 copy-done.2
  21.2 0.0 copy-done.3
  21.2 2.5 %shard_map.105 = f32[1024,256]{1,0:T(8,128)S(1)} custom-call(s32[2,136]{1,0:T(2,128)S(1)} %get-tuple-element.19.plan, s32[34]{0:T(128)S(1)} %get-tuple-element.20.rows, s32[4,4]{1,0:T(4,128)S(1)} %copy-done.3, bf16[112,128,128]{2,1,0:T(8,128)(2,1)S(1)} %copy-done, bf16[2176,256]{1,0:T(8,128)(2,1)S(1)} %broadcast_dynamic-update-slice_fusion.1.window, ...), custom_call_target="tpu_custom_call" | custom-call | flops 1073741824 | bytes 1048576 | tf_op jit(solution)/shard_map/pallas_call | solution.py:165
  23.7 0.0 copy-start.8
  23.7 0.0 copy-start.5
  23.7 0.0 copy-start.6
  23.8 0.0 copy-start.7
  23.8 0.4 collective-permute-start.8
  24.2 0.2 collective-permute-start.7
  24.4 1.0 %collective-permute-done.8 = f32[256,256]{1,0:T(8,128)S(1)} collective-permute-done((f32[256,256]{1,0:T(8,128)S(1)}, f32[256,256]{1,0:T(8,128)S(1)}, u32[]{:S(2)}, u32[]{:S(2)}) %collective-permute-start.8) | collective-permute-done | bytes 262176 | tf_op jit(solution)/shard_map/ppermute | solution.py:18
  25.5 0.1 collective-permute-start.9
  25.5 0.0 copy-done.8
  25.6 0.2 collective-permute-done.7
  25.8 5.4 %collective-permute-done.9 = bf16[256,256]{1,0:T(8,128)(2,1)S(1)} collective-permute-done((bf16[256,256]{1,0:T(8,128)(2,1)S(1)}, bf16[256,256]{1,0:T(8,128)(2,1)S(1)}, u32[]{:S(2)}, u32[]{:S(2)}) %collective-permute-start.9) | collective-permute-done | bytes 131104 | tf_op jit(solution)/shard_map/ppermute | solution.py:24
  31.2 0.0 copy-done.5
  31.2 0.0 copy-done.6
  31.2 0.0 copy-done.7
  31.2 0.4 constant_dynamic-update-slice_fusion.11
  31.7 1.2 %collective-permute-start.10 = (bf16[256,256]{1,0:T(8,128)(2,1)S(1)}, bf16[256,256]{1,0:T(8,128)(2,1)S(1)}, u32[]{:S(2)}, u32[]{:S(2)}) collective-permute-start(bf16[256,256]{1,0:T(8,128)(2,1)S(1)} %get-tuple-element.25.rest_0_), channel_id=1, source_target_pairs={{0,12},{1,13},{2,6},{3,7},{4,0},{5,1},{6,10},{7,11},{8,4},{9,5},{1... | collective-permute-start | bytes 393224 | tf_op jit(solution)/shard_map/ppermute | solution.py:39
  32.9 0.0 collective-permute-start.12
  32.9 1.1 %collective-permute-start.15 = (bf16[256,256]{1,0:T(8,128)(2,1)S(1)}, bf16[256,256]{1,0:T(8,128)(2,1)S(1)}, u32[]{:S(2)}, u32[]{:S(2)}) collective-permute-start(bf16[256,256]{1,0:T(8,128)(2,1)S(1)} %get-tuple-element.25.rest_0_), channel_id=1, source_target_pairs={{0,4},{1,5},{2,14},{3,15},{4,8},{5,9},{6,2},{7,3},{8,12},{9,13},{1... | collective-permute-start | bytes 393224 | tf_op jit(solution)/shard_map/ppermute | solution.py:39
  34.0 4.1 %collective-permute-done.10.rest_1_ = bf16[256,256]{1,0:T(8,128)(2,1)S(1)} collective-permute-done((bf16[256,256]{1,0:T(8,128)(2,1)S(1)}, bf16[256,256]{1,0:T(8,128)(2,1)S(1)}, u32[]{:S(2)}, u32[]{:S(2)}) %collective-permute-start.10) | collective-permute-done | bytes 131104 | tf_op jit(solution)/shard_map/ppermute | solution.py:39
  38.1 2.1 %collective-permute-start.11 = (bf16[256,256]{1,0:T(8,128)(2,1)S(1)}, bf16[256,256]{1,0:T(8,128)(2,1)S(1)}, u32[]{:S(2)}, u32[]{:S(2)}) collective-permute-start(bf16[256,256]{1,0:T(8,128)(2,1)S(1)} %collective-permute-done.10.rest_1_), channel_id=1, source_target_pairs={{0,2},{1,3},{2,0},{3,1},{4,6},{5,7},{6,4},{7,5},{8,10},{9,11},{10,... | collective-permute-start | bytes 393224 | tf_op jit(solution)/shard_map/ppermute | solution.py:24
  40.2 0.0 collective-permute-done.12
  40.2 0.1 collective-permute-start.13
  40.3 0.8 %collective-permute-start.16 = (bf16[256,256]{1,0:T(8,128)(2,1)S(1)}, bf16[256,256]{1,0:T(8,128)(2,1)S(1)}, u32[]{:S(2)}, u32[]{:S(2)}) collective-permute-start(bf16[256,256]{1,0:T(8,128)(2,1)S(1)} %collective-permute-done.10.rest_1_), channel_id=1, source_target_pairs={{0,12},{1,13},{2,6},{3,7},{4,0},{5,1},{6,10},{7,11},{8,4},{9,5},{1... | collective-permute-start | bytes 393224 | tf_op jit(solution)/shard_map/ppermute | solution.py:39
  41.1 2.1 %collective-permute-done.11 = bf16[256,256]{1,0:T(8,128)(2,1)S(1)} collective-permute-done((bf16[256,256]{1,0:T(8,128)(2,1)S(1)}, bf16[256,256]{1,0:T(8,128)(2,1)S(1)}, u32[]{:S(2)}, u32[]{:S(2)}) %collective-permute-start.11) | collective-permute-done | bytes 131104 | tf_op jit(solution)/shard_map/ppermute | solution.py:24
  43.1 0.1 collective-permute-start.14
  43.3 0.0 collective-permute-done.13
  43.3 1.4 %collective-permute-done.14 = bf16[512,256]{1,0:T(8,128)(2,1)S(1)} collective-permute-done((bf16[512,256]{1,0:T(8,128)(2,1)S(1)}, bf16[512,256]{1,0:T(8,128)(2,1)S(1)}, u32[]{:S(2)}, u32[]{:S(2)}) %collective-permute-start.14) | collective-permute-done | bytes 262176 | tf_op jit(solution)/shard_map/ppermute | solution.py:18
  44.8 0.0 collective-permute-done.15.rest_2_
  44.8 1.4 %collective-permute-done.16.rest_3_ = bf16[256,256]{1,0:T(8,128)(2,1)S(1)} collective-permute-done((bf16[256,256]{1,0:T(8,128)(2,1)S(1)}, bf16[256,256]{1,0:T(8,128)(2,1)S(1)}, u32[]{:S(2)}, u32[]{:S(2)}) %collective-permute-start.16) | collective-permute-done | bytes 131104 | tf_op jit(solution)/shard_map/ppermute | solution.py:39
  46.2 2.5 %shard_map.106 = f32[1024,256]{1,0:T(8,128)S(1)} custom-call(s32[2,136]{1,0:T(2,128)S(1)} %get-tuple-element.19.plan, s32[34]{0:T(128)S(1)} %get-tuple-element.20.rows, s32[4,4]{1,0:T(4,128)S(1)} %copy-done.3, bf16[112,128,128]{2,1,0:T(8,128)(2,1)S(1)} %copy-done, bf16[2176,256]{1,0:T(8,128)(2,1)S(1)} %broadcast_dynamic-update-slice_fusion.window, ...), custom_call_target="tpu_custom_call" | custom-call | flops 1073741824 | bytes 1048576 | tf_op jit(solution)/shard_map/pallas_call | solution.py:165
  48.8 0.1 collective-permute-start.18
  48.8 0.5 collective-permute-start.17
  49.3 1.0 %collective-permute-done.18 = f32[256,256]{1,0:T(8,128)S(1)} collective-permute-done((f32[256,256]{1,0:T(8,128)S(1)}, f32[256,256]{1,0:T(8,128)S(1)}, u32[]{:S(2)}, u32[]{:S(2)}) %collective-permute-start.18) | collective-permute-done | bytes 262176 | tf_op jit(solution)/shard_map/ppermute | solution.py:18
  50.4 1.9 %collective-permute-start.19 = (bf16[256,256]{1,0:T(8,128)(2,1)S(1)}, bf16[256,256]{1,0:T(8,128)(2,1)S(1)}, u32[]{:S(2)}, u32[]{:S(2)}) collective-permute-start(bf16[256,256]{1,0:T(8,128)(2,1)S(1)} %fusion.12), channel_id=1, source_target_pairs={{0,2},{1,3},{2,0},{3,1},{4,6},{5,7},{6,4},{7,5},{8,10},{9,11},{10,... | collective-permute-start | bytes 393224 | tf_op jit(solution)/shard_map/ppermute | solution.py:24
  52.3 0.0 collective-permute-done.17
  52.3 3.8 %collective-permute-done.19 = bf16[256,256]{1,0:T(8,128)(2,1)S(1)} collective-permute-done((bf16[256,256]{1,0:T(8,128)(2,1)S(1)}, bf16[256,256]{1,0:T(8,128)(2,1)S(1)}, u32[]{:S(2)}, u32[]{:S(2)}) %collective-permute-start.19) | collective-permute-done | bytes 131104 | tf_op jit(solution)/shard_map/ppermute | solution.py:24
  56.1 1.3 %fusion.10 = (f32[256,256]{1,0:T(8,128)}, f32[256,256]{1,0:T(8,128)S(1)}) fusion(f32[256,256]{1,0:T(8,128)S(1)} %copy-done.7, f32[256,256]{1,0:T(8,128)S(1)} %get-tuple-element.26, f32[256]{0:T(256)S(1)} %broadcast_multiply_fusion, f32[256,256]{1,0:T(8,128)S(1)} %copy-done.6, bf16[256,256]{1,0:T(8,128)(2,1)S(1)} %collective-permute-done.19, ...), kind=kLoop, calls=%fused_computation.14 | loop fusion | flops 2162688 | bytes 1968128 | tf_op jit(solution)/shard_map/add | solution.py:229
  57.4 0.8 %multiply_add_fusion = f32[256,256]{1,0:T(8,128)} fusion(f32[256,256]{1,0:T(8,128)S(1)} %copy-done.5, f32[256,256]{1,0:T(8,128)S(1)} %get-tuple-element.26, f32[256,256]{1,0:T(8,128)S(1)} %get-tuple-element.23), kind=kLoop, calls=%fused_computation.39 | loop fusion | flops 196608 | bytes 1048576 | tf_op jit(solution)/shard_map/add | solution.py:228
  (22 shorter events, 0.4 us)
Async XLA Ops:
  1.6 9.0 %collective-permute-start = (bf16[256,256]{1,0:T(8,128)(2,1)S(1)}, bf16[256,256]{1,0:T(8,128)(2,1)S(1)}, u32[]{:S(2)}, u32[]{:S(2)}) collective-permute-start(bf16[256,256]{1,0:T(8,128)(2,1)S(1)} %get-tuple-element.28.rest_0_), channel_id=1, source_target_pairs={{0,12},{1,13},{2,6},{3,7},{4,0},{5,1},{6,10},{7,11},{8,4},{9,5},{1... | collective-permute-start | bytes 393224 | tf_op jit(solution)/shard_map/ppermute | solution.py:39
  6.7 12.4 %collective-permute-start.2 = (bf16[256,256]{1,0:T(8,128)(2,1)S(1)}, bf16[256,256]{1,0:T(8,128)(2,1)S(1)}, u32[]{:S(2)}, u32[]{:S(2)}) collective-permute-start(bf16[256,256]{1,0:T(8,128)(2,1)S(1)} %get-tuple-element.28.rest_0_), channel_id=1, source_target_pairs={{0,2},{1,3},{2,0},{3,1},{4,6},{5,7},{6,4},{7,5},{8,10},{9,11},{10,... | collective-permute-start | bytes 393224 | tf_op jit(solution)/shard_map/ppermute | solution.py:24
  6.7 14.4 %collective-permute-start.5 = (bf16[256,256]{1,0:T(8,128)(2,1)S(1)}, bf16[256,256]{1,0:T(8,128)(2,1)S(1)}, u32[]{:S(2)}, u32[]{:S(2)}) collective-permute-start(bf16[256,256]{1,0:T(8,128)(2,1)S(1)} %get-tuple-element.28.rest_0_), channel_id=1, source_target_pairs={{0,4},{1,5},{2,14},{3,15},{4,8},{5,9},{6,2},{7,3},{8,12},{9,13},{1... | collective-permute-start | bytes 393224 | tf_op jit(solution)/shard_map/ppermute | solution.py:39
  10.6 8.6 %collective-permute-start.1 = (bf16[256,256]{1,0:T(8,128)(2,1)S(1)}, bf16[256,256]{1,0:T(8,128)(2,1)S(1)}, u32[]{:S(2)}, u32[]{:S(2)}) collective-permute-start(bf16[256,256]{1,0:T(8,128)(2,1)S(1)} %collective-permute-done.rest_1_), channel_id=1, source_target_pairs={{0,2},{1,3},{2,0},{3,1},{4,6},{5,7},{6,4},{7,5},{8,10},{9,11},{10,... | collective-permute-start | bytes 393224 | tf_op jit(solution)/shard_map/ppermute | solution.py:24
  12.8 8.4 %collective-permute-start.6 = (bf16[256,256]{1,0:T(8,128)(2,1)S(1)}, bf16[256,256]{1,0:T(8,128)(2,1)S(1)}, u32[]{:S(2)}, u32[]{:S(2)}) collective-permute-start(bf16[256,256]{1,0:T(8,128)(2,1)S(1)} %collective-permute-done.rest_1_), channel_id=1, source_target_pairs={{0,12},{1,13},{2,6},{3,7},{4,0},{5,1},{6,10},{7,11},{8,4},{9,5},{1... | collective-permute-start | bytes 393224 | tf_op jit(solution)/shard_map/ppermute | solution.py:39
  15.7 0.7 %copy-start.4 = (s32[112,2]{0,1:T(2,128)S(1)}, s32[112,2]{0,1:T(2,128)}, u32[]{:S(2)}) copy-start(s32[112,2]{0,1:T(2,128)} %param.14) | copy-start | bytes 2692
  16.4 4.7 %copy-start = (bf16[112,128,128]{2,1,0:T(8,128)(2,1)S(1)}, bf16[112,128,128]{2,1,0:T(8,128)(2,1)}, u32[]{:S(2)}) copy-start(bf16[112,128,128]{2,1,0:T(8,128)(2,1)} %blocks.3) | copy-start | bytes 11010052
  19.1 1.6 %collective-permute-start.3 = (bf16[512,256]{1,0:T(8,128)(2,1)S(1)}, bf16[512,256]{1,0:T(8,128)(2,1)S(1)}, u32[]{:S(2)}, u32[]{:S(2)}) collective-permute-start(bf16[512,256]{1,0:T(8,128)(2,1)S(1)} %pad_maximum_fusion), channel_id=1, source_target_pairs={{0,1},{1,0},{2,3},{3,2},{4,5},{5,4},{6,7},{7,6},{8,9},{9,8},{10,11... | collective-permute-start | bytes 786440 | tf_op jit(solution)/shard_map/ppermute | solution.py:18
  19.2 1.9 %copy-start.1 = (bf16[4,4,32,256]{3,2,1,0:T(8,128)(2,1)S(1)}, bf16[4,4,32,256]{3,2,1,0:T(8,128)(2,1)}, u32[]{:S(2)}) copy-start(bf16[4,4,32,256]{3,2,1,0:T(8,128)(2,1)} %far_u.3) | copy-start | bytes 786436
  19.2 1.9 %copy-start.2 = (bf16[4,4,32,256]{3,2,1,0:T(8,128)(2,1)S(1)}, bf16[4,4,32,256]{3,2,1,0:T(8,128)(2,1)}, u32[]{:S(2)}) copy-start(bf16[4,4,32,256]{3,2,1,0:T(8,128)(2,1)} %far_v.3) | copy-start | bytes 786436
  19.2 1.9 %copy-start.3 = (s32[4,4]{1,0:T(4,128)S(1)}, s32[4,4]{1,0:T(4,128)}, u32[]{:S(2)}) copy-start(s32[4,4]{1,0:T(4,128)} %ranks.3) | copy-start | bytes 196
  19.3 1.8 %collective-permute-start.4 = (bf16[512,256]{1,0:T(8,128)(2,1)S(1)}, bf16[512,256]{1,0:T(8,128)(2,1)S(1)}, u32[]{:S(2)}, u32[]{:S(2)}) collective-permute-start(bf16[512,256]{1,0:T(8,128)(2,1)S(1)} %pad_maximum_fusion.1), channel_id=1, source_target_pairs={{0,1},{1,0},{2,3},{3,2},{4,5},{5,4},{6,7},{7,6},{8,9},{9,8},{10,11... | collective-permute-start | bytes 786440 | tf_op jit(solution)/shard_map/ppermute | solution.py:18
  23.7 1.8 %copy-start.8 = (f32[256]{0:T(256)S(1)}, f32[256]{0:T(256)}, u32[]{:S(2)}) copy-start(f32[256]{0:T(256)} %param.12) | copy-start | bytes 3076
  23.7 7.5 %copy-start.5 = (f32[256,256]{1,0:T(8,128)S(1)}, f32[256,256]{1,0:T(8,128)}, u32[]{:S(2)}) copy-start(f32[256,256]{1,0:T(8,128)} %param.9) | copy-start | bytes 786436
  23.7 7.5 %copy-start.6 = (f32[256,256]{1,0:T(8,128)S(1)}, f32[256,256]{1,0:T(8,128)}, u32[]{:S(2)}) copy-start(f32[256,256]{1,0:T(8,128)} %param.11) | copy-start | bytes 786436
  23.8 7.5 %copy-start.7 = (f32[256,256]{1,0:T(8,128)S(1)}, f32[256,256]{1,0:T(8,128)}, u32[]{:S(2)}) copy-start(f32[256,256]{1,0:T(8,128)} %param.10) | copy-start | bytes 786436
  23.8 1.6 %collective-permute-start.8 = (f32[256,256]{1,0:T(8,128)S(1)}, f32[256,256]{1,0:T(8,128)S(1)}, u32[]{:S(2)}, u32[]{:S(2)}) collective-permute-start(f32[256,256]{1,0:T(8,128)S(1)} %get-tuple-element.32), channel_id=1, source_target_pairs={{0,1},{1,0},{2,3},{3,2},{4,5},{5,4},{6,7},{7,6},{8,9},{9,8},{10,11... | collective-permute-start | bytes 786440 | tf_op jit(solution)/shard_map/ppermute | solution.py:18
  24.2 1.6 %collective-permute-start.7 = (f32[256,256]{1,0:T(8,128)S(1)}, f32[256,256]{1,0:T(8,128)S(1)}, u32[]{:S(2)}, u32[]{:S(2)}) collective-permute-start(f32[256,256]{1,0:T(8,128)S(1)} %get-tuple-element.31), channel_id=1, source_target_pairs={{0,1},{1,0},{2,3},{3,2},{4,5},{5,4},{6,7},{7,6},{8,9},{9,8},{10,11... | collective-permute-start | bytes 786440 | tf_op jit(solution)/shard_map/ppermute | solution.py:18
  25.5 5.8 %collective-permute-start.9 = (bf16[256,256]{1,0:T(8,128)(2,1)S(1)}, bf16[256,256]{1,0:T(8,128)(2,1)S(1)}, u32[]{:S(2)}, u32[]{:S(2)}) collective-permute-start(bf16[256,256]{1,0:T(8,128)(2,1)S(1)} %fusion.18), channel_id=1, source_target_pairs={{0,2},{1,3},{2,0},{3,1},{4,6},{5,7},{6,4},{7,5},{8,10},{9,11},{10,... | collective-permute-start | bytes 393224 | tf_op jit(solution)/shard_map/ppermute | solution.py:24
  31.7 6.4 %collective-permute-start.10 = (bf16[256,256]{1,0:T(8,128)(2,1)S(1)}, bf16[256,256]{1,0:T(8,128)(2,1)S(1)}, u32[]{:S(2)}, u32[]{:S(2)}) collective-permute-start(bf16[256,256]{1,0:T(8,128)(2,1)S(1)} %get-tuple-element.25.rest_0_), channel_id=1, source_target_pairs={{0,12},{1,13},{2,6},{3,7},{4,0},{5,1},{6,10},{7,11},{8,4},{9,5},{1... | collective-permute-start | bytes 393224 | tf_op jit(solution)/shard_map/ppermute | solution.py:39
  32.9 7.3 %collective-permute-start.12 = (bf16[256,256]{1,0:T(8,128)(2,1)S(1)}, bf16[256,256]{1,0:T(8,128)(2,1)S(1)}, u32[]{:S(2)}, u32[]{:S(2)}) collective-permute-start(bf16[256,256]{1,0:T(8,128)(2,1)S(1)} %get-tuple-element.25.rest_0_), channel_id=1, source_target_pairs={{0,2},{1,3},{2,0},{3,1},{4,6},{5,7},{6,4},{7,5},{8,10},{9,11},{10,... | collective-permute-start | bytes 393224 | tf_op jit(solution)/shard_map/ppermute | solution.py:24
  32.9 11.9 %collective-permute-start.15 = (bf16[256,256]{1,0:T(8,128)(2,1)S(1)}, bf16[256,256]{1,0:T(8,128)(2,1)S(1)}, u32[]{:S(2)}, u32[]{:S(2)}) collective-permute-start(bf16[256,256]{1,0:T(8,128)(2,1)S(1)} %get-tuple-element.25.rest_0_), channel_id=1, source_target_pairs={{0,4},{1,5},{2,14},{3,15},{4,8},{5,9},{6,2},{7,3},{8,12},{9,13},{1... | collective-permute-start | bytes 393224 | tf_op jit(solution)/shard_map/ppermute | solution.py:39
  38.1 5.0 %collective-permute-start.11 = (bf16[256,256]{1,0:T(8,128)(2,1)S(1)}, bf16[256,256]{1,0:T(8,128)(2,1)S(1)}, u32[]{:S(2)}, u32[]{:S(2)}) collective-permute-start(bf16[256,256]{1,0:T(8,128)(2,1)S(1)} %collective-permute-done.10.rest_1_), channel_id=1, source_target_pairs={{0,2},{1,3},{2,0},{3,1},{4,6},{5,7},{6,4},{7,5},{8,10},{9,11},{10,... | collective-permute-start | bytes 393224 | tf_op jit(solution)/shard_map/ppermute | solution.py:24
  40.2 3.1 %collective-permute-start.13 = (bf16[512,256]{1,0:T(8,128)(2,1)S(1)}, bf16[512,256]{1,0:T(8,128)(2,1)S(1)}, u32[]{:S(2)}, u32[]{:S(2)}) collective-permute-start(bf16[512,256]{1,0:T(8,128)(2,1)S(1)} %pad_maximum_fusion.2), channel_id=1, source_target_pairs={{0,1},{1,0},{2,3},{3,2},{4,5},{5,4},{6,7},{7,6},{8,9},{9,8},{10,11... | collective-permute-start | bytes 786440 | tf_op jit(solution)/shard_map/ppermute | solution.py:18
  40.3 5.9 %collective-permute-start.16 = (bf16[256,256]{1,0:T(8,128)(2,1)S(1)}, bf16[256,256]{1,0:T(8,128)(2,1)S(1)}, u32[]{:S(2)}, u32[]{:S(2)}) collective-permute-start(bf16[256,256]{1,0:T(8,128)(2,1)S(1)} %collective-permute-done.10.rest_1_), channel_id=1, source_target_pairs={{0,12},{1,13},{2,6},{3,7},{4,0},{5,1},{6,10},{7,11},{8,4},{9,5},{1... | collective-permute-start | bytes 393224 | tf_op jit(solution)/shard_map/ppermute | solution.py:39
  43.1 1.6 %collective-permute-start.14 = (bf16[512,256]{1,0:T(8,128)(2,1)S(1)}, bf16[512,256]{1,0:T(8,128)(2,1)S(1)}, u32[]{:S(2)}, u32[]{:S(2)}) collective-permute-start(bf16[512,256]{1,0:T(8,128)(2,1)S(1)} %pad_maximum_fusion.3), channel_id=1, source_target_pairs={{0,1},{1,0},{2,3},{3,2},{4,5},{5,4},{6,7},{7,6},{8,9},{9,8},{10,11... | collective-permute-start | bytes 786440 | tf_op jit(solution)/shard_map/ppermute | solution.py:18
  48.8 1.6 %collective-permute-start.18 = (f32[256,256]{1,0:T(8,128)S(1)}, f32[256,256]{1,0:T(8,128)S(1)}, u32[]{:S(2)}, u32[]{:S(2)}) collective-permute-start(f32[256,256]{1,0:T(8,128)S(1)} %get-tuple-element.30), channel_id=1, source_target_pairs={{0,1},{1,0},{2,3},{3,2},{4,5},{5,4},{6,7},{7,6},{8,9},{9,8},{10,11... | collective-permute-start | bytes 786440 | tf_op jit(solution)/shard_map/ppermute | solution.py:18
  48.8 3.4 %collective-permute-start.17 = (f32[256,256]{1,0:T(8,128)S(1)}, f32[256,256]{1,0:T(8,128)S(1)}, u32[]{:S(2)}, u32[]{:S(2)}) collective-permute-start(f32[256,256]{1,0:T(8,128)S(1)} %get-tuple-element.29), channel_id=1, source_target_pairs={{0,1},{1,0},{2,3},{3,2},{4,5},{5,4},{6,7},{7,6},{8,9},{9,8},{10,11... | collective-permute-start | bytes 786440 | tf_op jit(solution)/shard_map/ppermute | solution.py:18
  50.4 5.7 %collective-permute-start.19 = (bf16[256,256]{1,0:T(8,128)(2,1)S(1)}, bf16[256,256]{1,0:T(8,128)(2,1)S(1)}, u32[]{:S(2)}, u32[]{:S(2)}) collective-permute-start(bf16[256,256]{1,0:T(8,128)(2,1)S(1)} %fusion.12), channel_id=1, source_target_pairs={{0,2},{1,3},{2,0},{3,1},{4,6},{5,7},{6,4},{7,5},{8,10},{9,11},{10,... | collective-permute-start | bytes 393224 | tf_op jit(solution)/shard_map/ppermute | solution.py:24

commit v5 on v4

--- a/solution.py
+++ b/solution.py
@@ -10,6 +10,7 @@
 REACH = 4
 CORES = 2
 STEP = 0.2
+LOG_TWO = 0.6931471805599453
 WIDTH = 4
 
 
@@ -85,38 +86,23 @@
         rows[lax.shift_right_logical(at, WIDTH.bit_length() - 1)] = target_rows[target]
         return used + full.astype(jnp.int32)
 
-    lax.fori_loop(0, pairs.shape[1], put, jnp.int32(0), unroll=4)
-
-
-def stress_kernel(leaf, plan, rows, ranks, blocks, window, far_u, far_v, *rest):
-    targets, groups, rank, elems = far_u.shape
-    columns, (out, coeffs) = rest[:groups], rest[groups:]
-    chips, members = targets // CORES, window.shape[1]
-    group, chip, core = here()
-    toward = jnp.where(chip == chips - 1, -1, 1)
-    steps = [(s + 1) // 2 if s % 2 else -(s // 2) for s in range(groups)]
-    sources = [around(group + toward * step, groups) for step in steps]
-    row = lax.broadcasted_iota(jnp.int32, (rank, members), 0)
-    for s in range(groups):
-        source = sources[s]
-        product = jnp.dot(
-            jnp.concatenate([far_v[t, source] for t in range(targets)], axis=0),
-            columns[s][...],
+    lax.fori_loop(0, pairs.shape[1], put, jnp.int32(0), unroll=8)
+
+
+def stress_kernel(leaf, plan, rows, blocks, window, far_u, far_v, *rest):
+    targets, elems, ranks = far_u.shape
+    groups, rank = far_v.shape[0], far_v.shape[1] // targets
+    columns, out = rest[:groups], rest[groups]
+    coeffs = [
+        jnp.dot(far_v[s], columns[s][...], preferred_element_type=jnp.float32).astype(jnp.bfloat16)
+        for s in range(groups)
+    ]
+    for t in range(targets):
+        out[pl.ds(t * elems, elems), :] = jnp.dot(
+            far_u[t],
+            jnp.concatenate([c[t * rank : (t + 1) * rank] for c in coeffs], axis=0),
             preferred_element_type=jnp.float32,
         )
-        for t in range(targets):
-            part = product[t * rank : (t + 1) * rank]
-            part = jnp.where(row < ranks[t, source], part, 0.0)
-            coeffs[t, s * rank : (s + 1) * rank, :] = part.astype(jnp.bfloat16)
-    for other in range(CORES):
-        for ahead in range(chips):
-            target = around(chip + ahead, chips) * CORES + (core ^ other)
-            out[pl.ds((other * chips + ahead) * elems, elems), :] = lax.dot_general(
-                jnp.concatenate([far_u[target, source] for source in sources], axis=0),
-                coeffs[target],
-                (((0,), (0,)), ((), ())),
-                preferred_element_type=jnp.float32,
-            )
     products = []
     for i in range(rows.shape[0]):
         places = range(i * WIDTH, (i + 1) * WIDTH)
@@ -132,6 +118,35 @@
         out[pl.ds(pl.multiple_of(rows[i], leaf), leaf), :] += products[i]
 
 
+def bases_kernel(ranks, far_u, far_v, by_target, by_source):
+    targets, groups, rank, elems = far_u.shape
+    chips = targets // CORES
+    group, chip, core = here()
+    toward = jnp.where(chip == chips - 1, -1, 1)
+    steps = [(s + 1) // 2 if s % 2 else -(s // 2) for s in range(groups)]
+    sources = [around(group + toward * step, groups) for step in steps]
+    row = lax.broadcasted_iota(jnp.int32, (rank, elems), 0)
+    for t in range(targets):
+        other, ahead = t // chips, t % chips
+        target = around(chip + ahead, chips) * CORES + (core ^ other)
+        for s, source in enumerate(sources):
+            kept = jnp.where(row < ranks[target, source], far_v[target, source].astype(jnp.float32), 0.0)
+            by_source[s, t * rank : (t + 1) * rank, :] = kept.astype(jnp.bfloat16)
+        bases = jnp.concatenate([far_u[target, source] for source in sources], axis=0)
+        by_target[t] = bases.astype(jnp.float32).T.astype(jnp.bfloat16)
+
+
+def finish_kernel(near, mate, received, scale, shift, weight, slip, state, slip_out, state_out):
+    stress = near[...] + mate[...]
+    for s in range(received.shape[0]):
+        stress = stress + received[s].astype(jnp.float32)
+    halved = stress * scale[...] + shift[...]
+    velocity = weight[...] * (jnp.exp(halved - LOG_TWO) - jnp.exp(-halved - LOG_TWO))
+    speed = jnp.abs(velocity)
+    slip_out[...] = slip[...] + 0.5 * STEP * velocity
+    state_out[...] = state[...] - 0.5 * STEP * (speed / (1.0 + speed))
+
+
 VMEM = pl.BlockSpec(memory_space=pltpu.VMEM)
 SMEM = pl.BlockSpec(memory_space=pltpu.SMEM)
 PARAMS = pltpu.CompilerParams(vmem_limit_bytes=16 * 1024 * 1024)
@@ -158,28 +173,44 @@
     )(pairs)
 
 
-def partial_stress(plan, ranks, blocks, window, far_u, far_v, columns):
+def arranged_bases(ranks, far_u, far_v):
     targets, groups, rank, elems = far_u.shape
+    return pl.pallas_call(
+        bases_kernel,
+        out_shape=(
+            jax.ShapeDtypeStruct((targets, elems, groups * rank), jnp.bfloat16),
+            jax.ShapeDtypeStruct((groups, targets * rank, elems), jnp.bfloat16),
+        ),
+        in_specs=[SMEM, VMEM, VMEM],
+        out_specs=(VMEM, VMEM),
+        compiler_params=PARAMS,
+        cost_estimate=pl.CostEstimate(flops=1024, bytes_accessed=1_000_000, transcendentals=0),
+    )(ranks, far_u, far_v)
+
+
+def partial_stress(plan, blocks, window, far_u, far_v, columns):
+    targets, elems, ranks = far_u.shape
     count, leaf, _ = blocks.shape
-    rows, members = targets * elems, window.shape[1]
+    members, groups = window.shape[1], len(columns)
     return pl.pallas_call(
         functools.partial(stress_kernel, leaf),
-        out_shape=jax.ShapeDtypeStruct((rows, members), jnp.float32),
-        in_specs=[SMEM] * 3 + [VMEM] * (4 + groups),
+        out_shape=jax.ShapeDtypeStruct((targets * elems, members), jnp.float32),
+        in_specs=[SMEM] * 2 + [VMEM] * (4 + groups),
         out_specs=VMEM,
-        scratch_shapes=[pltpu.VMEM((targets, groups * rank, members), jnp.bfloat16)],
         compiler_params=PARAMS,
         cost_estimate=pl.CostEstimate(
-            flops=2 * members * (count * leaf * leaf + 2 * targets * groups * rank * elems),
-            bytes_accessed=4 * rows * members,
+            flops=2 * members * (count * leaf * leaf + 2 * targets * ranks * elems),
+            bytes_accessed=4 * targets * elems * members,
             transcendentals=0,
         ),
-    )(plan[0], plan[1], ranks, blocks, window, far_u, far_v, *columns)
+    )(plan[0], plan[1], blocks, window, far_u, far_v, *columns)
 
 
 def slip_rates(stress, state, load, friction_a):
     softness = friction_a[:, None]
-    velocity = 2.0 * jnp.exp(-state / softness) * jnp.sinh((stress + load) / (2.0 * softness))
+    halved = (stress + load) / (2.0 * softness)
+    growth = jnp.exp(halved - LOG_TWO) - jnp.exp(-halved - LOG_TWO)
+    velocity = 2.0 * jnp.exp(-state / softness) * growth
     speed = jnp.abs(velocity)
     drift = jnp.exp(-state) - speed / (1.0 + speed)
     return (velocity, drift)
@@ -197,37 +228,58 @@
 
     def planned(after):
         if not plans:
-            after, pairs = lax.optimization_barrier((after, near_pairs.T))
-            plans.append(planned_blocks(pairs, leaf, own))
+            pairs = near_pairs.T
+            after, *tables = lax.optimization_barrier((after, far_rank, far_u, far_v))
+            plans.append((planned_blocks(pairs, leaf, own), arranged_bases(*tables)))
         return after, plans[0]
 
     def section_stress(field):
         half = field.astype(jnp.bfloat16)
         straight = end_shift(half, 1)
-        straight, plan = planned(straight)
+        straight, (plan, bases) = planned(straight)
         near = jnp.concatenate([half] + [chip_shift(half, s) for s in range(1, chips)])
         column = [half, straight, end_shift(half, -1)]
         while len(column) < groups:
             column.append(end_shift(column[-2], 1 if len(column) % 2 else -1))
         ends = [chip_shift(straight, s) for s in range(1, chips)]
-        ends, plan = lax.optimization_barrier((ends, plan))
+        ends, plan, bases = lax.optimization_barrier((ends, plan, bases))
         ends = jnp.concatenate([straight] + ends)
-        window = jnp.concatenate([near, ends, core_swap(near), core_swap(ends), spare])
-        partial = partial_stress(plan, far_rank, near_blocks, window, far_u, far_v, column)
+        others = [core_swap(near[:elems]), core_swap(near[elems:])]
+        window = jnp.concatenate([near, ends] + others + [core_swap(ends), spare])
+        partial = partial_stress(plan, near_blocks, window, *bases, column)
         partial = partial.reshape(CORES, chips, elems, members)
-        joined = [partial[0, s] + core_swap(partial[1, s]) for s in range(chips)]
-        total = joined[0]
-        for s in range(1, chips):
-            total = total + chip_shift(joined[s].astype(jnp.bfloat16), s).astype(jnp.float32)
-        return total
-
-    velocity_one, drift_one = slip_rates(section_stress(slip), state, load, friction_a)
+        joined = [core_swap(partial[1, s]) for s in range(chips)]
+        sent = [(partial[0, s] + joined[s]).astype(jnp.bfloat16) for s in range(1, chips)]
+        return partial[0, 0], joined[0], [chip_shift(sent[s - 1], s) for s in range(1, chips)]
+
+    near, mate, received = section_stress(slip)
+    stress_one = near + mate
+    for part in received:
+        stress_one = stress_one + part.astype(jnp.float32)
+    velocity_one, drift_one = slip_rates(stress_one, state, load, friction_a)
     slip_mid = slip + STEP * velocity_one
+    near, mate, received = section_stress(slip_mid)
+
     state_mid = state + STEP * drift_one
-    velocity_two, drift_two = slip_rates(section_stress(slip_mid), state_mid, load, friction_a)
-    slip_next = slip + 0.5 * STEP * (velocity_one + velocity_two)
-    state_next = state + 0.5 * STEP * (drift_one + drift_two)
-    return (slip_next, state_next)
+    softness = friction_a[:, None]
+    scale = jnp.broadcast_to(1.0 / (2.0 * softness), slip.shape)
+    shift = load * scale
+    weight = 2.0 * jnp.exp(-state_mid / softness)
+    slip_most = slip + 0.5 * STEP * velocity_one
+    state_most = state + 0.5 * STEP * (drift_one + jnp.exp(-state_mid))
+    return pl.pallas_call(
+        finish_kernel,
+        out_shape=(
+            jax.ShapeDtypeStruct(slip.shape, jnp.float32),
+            jax.ShapeDtypeStruct(slip.shape, jnp.float32),
+        ),
+        in_specs=[VMEM] * 8,
+        out_specs=(VMEM, VMEM),
+        compiler_params=PARAMS,
+        cost_estimate=pl.CostEstimate(
+            flops=16 * slip.size, bytes_accessed=32 * slip.size, transcendentals=2 * slip.size
+        ),
+    )(near, mate, jnp.stack(received), scale, shift, weight, slip_most, state_most)
 
 
 def solution(mesh):

time: 58.3 us -> 54.3 us (0.931)
  waiting for transfers between devices: 24.5 us -> 18.7 us
  starting transfers between devices: 20.3 us -> 22.7 us
  other arithmetic: 3.63 us -> 1.67 us
  Pallas kernels: 7.71 us -> 8.96 us
    ppermute x6, waiting for transfers between devices: 8.32 us -> 4.07 us  [end_shift(): return lax.ppermute(array, ('clu', 'row'), pairs)]
    ppermute x6, starting transfers between devices: 6.2 us -> 8.07 us  [chip_shift(): return lax.ppermute(array, 'row', pairs)]
    pallas_call x0 -> x2, Pallas kernels: none -> 1.7 us  [the longest x1 0.95 us: body(): pl.pallas_call(finish_kernel, out_shape=(jax.ShapeDtypeStruct(slip.shape,...]
    ppermute x6, waiting for transfers between devices: 11.3 us -> 9.69 us  [chip_shift(): return lax.ppermute(array, 'row', pairs)]
    add x2, other arithmetic: 2.08 us -> 0.55 us  [the longest x1 0.39 us: body(): state_most = state + 0.5 * STEP * (drift_one + jnp.exp(-state_mid))]
    ppermute x6, starting transfers between devices: 12.2 us -> 13.3 us  [end_shift(): return lax.ppermute(array, ('clu', 'row'), pairs)]
    ppermute x8 -> x10, starting transfers between devices: 1.91 us -> 1.36 us  [core_swap(): return lax.ppermute(array, 'row', [(i, i ^ 1) for i in range(devices)])]
    ppermute x8 -> x10, waiting for transfers between devices: 4.93 us -> 4.97 us  [core_swap(): return lax.ppermute(array, 'row', [(i, i ^ 1) for i in range(devices)])]
  transfers between devices with their start and end apart: 20 -> 22, of which waited for: 12 -> 11; matrix products, arithmetic and copies ran while one was open for 1% -> 1% of each run, Pallas kernels for 5% -> 6%
where the time goes in v5:
time: 54.3 us; the launch traced here: 54.1 us
  starting transfers between devices  22.7 us (42%)
  waiting for transfers between devices  18.7 us (34%)
  Pallas kernels  8.96 us (17%)
  other arithmetic  1.67 us (3%)
  local copies, waits for them, and re-layouts  1.07 us (2%)
  between operations  0.99 us (2%)
    ppermute x6, starting transfers between devices, end_shift(): return lax.ppermute(array, ('clu', 'row'), pairs)  13.3 us
    ppermute x6, waiting for transfers between devices, chip_shift(): return lax.ppermute(array, 'row', pairs)  9.69 us
    ppermute x6, starting transfers between devices, chip_shift(): return lax.ppermute(array, 'row', pairs)  8.07 us
    ppermute x10, waiting for transfers between devices, core_swap(): return lax.ppermute(array, 'row', [(i, i ^ 1) for i in range(devices)])  4.97 us
    pallas_call x2, Pallas kernels, partial_stress(): pl.pallas_call(functools.partial(stress_kernel, leaf), out_shape=jax.Shap...  4.73 us
    ppermute x6, waiting for transfers between devices, end_shift(): return lax.ppermute(array, ('clu', 'row'), pairs)  4.07 us
    pallas_call x1, Pallas kernels, planned_blocks(): pl.pallas_call(functools.partial(plan_kernel, leaf, own), out_shape=(jax....  2.54 us
    ppermute x10, starting transfers between devices, core_swap(): return lax.ppermute(array, 'row', [(i, i ^ 1) for i in range(devices)])  1.36 us
  transfers between devices with their start and end apart: 22, of which 11 were waited for; matrix products, arithmetic and copies ran while one was open for 1% of the time, Pallas kernels for 6%

profile of v5, /device:TPU:0, one launch (start us, length us, event | category | flops | bytes accessed | tf_op | source)
XLA Modules:
  0.0 54.1 jit_solution(3116801186686379657)
XLA Ops:
  0.6 1.0 %constant_dynamic-update-slice_fusion.7 = (bf16[2176,256]{1,0:T(8,128)(2,1)S(1)}, bf16[256,256]{1,0:T(8,128)(2,1)S(1)}) fusion(f32[256,256]{1,0:T(8,128)} %param.9), kind=kLoop, calls=%fused_computation.34 | loop fusion | flops 65535 | bytes 524288
  1.6 5.1 %collective-permute-start = (bf16[256,256]{1,0:T(8,128)(2,1)S(1)}, bf16[256,256]{1,0:T(8,128)(2,1)S(1)}, u32[]{:S(2)}, u32[]{:S(2)}) collective-permute-start(bf16[256,256]{1,0:T(8,128)(2,1)S(1)} %get-tuple-element.43.rest_0_), channel_id=1, source_target_pairs={{0,12},{1,13},{2,6},{3,7},{4,0},{5,1},{6,10},{7,11},{8,4},{9,5},{1... | collective-permute-start | bytes 393224 | tf_op jit(solution)/shard_map/ppermute | solution.py:40
  6.7 0.0 collective-permute-start.2
  6.7 0.0 collective-permute-start.3
  6.7 1.0 %collective-permute-start.6 = (bf16[256,256]{1,0:T(8,128)(2,1)S(1)}, bf16[256,256]{1,0:T(8,128)(2,1)S(1)}, u32[]{:S(2)}, u32[]{:S(2)}) collective-permute-start(bf16[256,256]{1,0:T(8,128)(2,1)S(1)} %get-tuple-element.43.rest_0_), channel_id=1, source_target_pairs={{0,4},{1,5},{2,14},{3,15},{4,8},{5,9},{6,2},{7,3},{8,12},{9,13},{1... | collective-permute-start | bytes 393224 | tf_op jit(solution)/shard_map/ppermute | solution.py:40
  7.8 0.7 %copy-done.4 = s32[112,2]{0,1:T(2,128)S(1)} copy-done((s32[112,2]{0,1:T(2,128)S(1)}, s32[112,2]{0,1:T(2,128)}, u32[]{:S(2)}) %copy-start.4) | copy-done | bytes 920
  8.4 2.5 %shard_map.104 = (s32[2,136]{1,0:T(2,128)S(1)}, s32[34]{0:T(128)S(1)}) custom-call(s32[2,112]{1,0:T(2,128)S(1)} %bitcast.45), custom_call_target="tpu_custom_call" | custom-call | flops 4000000000 | bytes 10000000 | tf_op jit(solution)/shard_map/pallas_call | solution.py:158
  11.0 0.0 collective-permute-done.rest_1_
  11.0 1.5 %collective-permute-start.1 = (bf16[256,256]{1,0:T(8,128)(2,1)S(1)}, bf16[256,256]{1,0:T(8,128)(2,1)S(1)}, u32[]{:S(2)}, u32[]{:S(2)}) collective-permute-start(bf16[256,256]{1,0:T(8,128)(2,1)S(1)} %collective-permute-done.rest_1_), channel_id=1, source_target_pairs={{0,2},{1,3},{2,0},{3,1},{4,6},{5,7},{6,4},{7,5},{8,10},{9,11},{10,... | collective-permute-start | bytes 393224 | tf_op jit(solution)/shard_map/ppermute | solution.py:25
  12.5 2.3 %collective-permute-start.7 = (bf16[256,256]{1,0:T(8,128)(2,1)S(1)}, bf16[256,256]{1,0:T(8,128)(2,1)S(1)}, u32[]{:S(2)}, u32[]{:S(2)}) collective-permute-start(bf16[256,256]{1,0:T(8,128)(2,1)S(1)} %collective-permute-done.rest_1_), channel_id=1, source_target_pairs={{0,12},{1,13},{2,6},{3,7},{4,0},{5,1},{6,10},{7,11},{8,4},{9,5},{1... | collective-permute-start | bytes 393224 | tf_op jit(solution)/shard_map/ppermute | solution.py:40
  14.8 0.0 copy-done.1
  14.8 0.0 copy-done.2
  14.8 0.0 copy-done.3
  14.8 0.7 %shard_map.105 = (bf16[4,256,128]{2,1,0:T(8,128)(2,1)S(1)}, bf16[4,128,256]{2,1,0:T(8,128)(2,1)S(1)}) custom-call(s32[4,4]{1,0:T(4,128)S(1)} %copy-done.3, bf16[4,4,32,256]{3,2,1,0:T(8,128)(2,1)S(1)} %copy-done.1, bf16[4,4,32,256]{3,2,1,0:T(8,128)(2,1)S(1)} %copy-done.2), custom_call_target="tpu_custom_call" | custom-call | flops 1024 | bytes 1000000 | tf_op jit(solution)/shard_map/pallas_call | solution.py:178
  15.6 0.0 collective-permute-done.2
  15.6 0.1 collective-permute-start.4
  15.7 1.0 %collective-permute-done.1 = bf16[256,256]{1,0:T(8,128)(2,1)S(1)} collective-permute-done((bf16[256,256]{1,0:T(8,128)(2,1)S(1)}, bf16[256,256]{1,0:T(8,128)(2,1)S(1)}, u32[]{:S(2)}, u32[]{:S(2)}) %collective-permute-start.1) | collective-permute-done | bytes 131104 | tf_op jit(solution)/shard_map/ppermute | solution.py:25
  16.7 0.1 collective-permute-start.5
  16.8 0.0 collective-permute-done.3
  16.8 0.2 collective-permute-done.4
  17.0 1.3 %collective-permute-done.5 = bf16[512,256]{1,0:T(8,128)(2,1)S(1)} collective-permute-done((bf16[512,256]{1,0:T(8,128)(2,1)S(1)}, bf16[512,256]{1,0:T(8,128)(2,1)S(1)}, u32[]{:S(2)}, u32[]{:S(2)}) %collective-permute-start.5) | collective-permute-done | bytes 262176 | tf_op jit(solution)/shard_map/ppermute | solution.py:19
  18.4 0.0 collective-permute-done.6.rest_2_
  18.4 0.0 collective-permute-done.7.rest_3_
  18.4 2.4 %shard_map.106 = f32[1024,256]{1,0:T(8,128)S(1)} custom-call(s32[2,136]{1,0:T(2,128)S(1)} %get-tuple-element.33.plan, s32[34]{0:T(128)S(1)} %get-tuple-element.34.rows, bf16[112,128,128]{2,1,0:T(8,128)(2,1)S(1)} %copy-done, bf16[2176,256]{1,0:T(8,128)(2,1)S(1)} %constant_dynamic-update-slice_fusion.window, bf16[4,256,128]{2,1,0:T(8,128)(2,1)S(1)} %get-tuple-element.36.far_u, ...), custom_call_target="tpu_custom_call" | custom-call | flops 1073741824 | bytes 1048576 | tf_op jit(solution)/shard_map/pallas_call | solution.py:195
  20.8 0.0 copy-start.8
  20.9 0.0 copy-start.6
  20.9 0.0 copy-start.7
  20.9 0.2 collective-permute-start.9
  21.1 0.4 collective-permute-start.8
  21.5 1.0 %collective-permute-done.9 = f32[256,256]{1,0:T(8,128)S(1)} collective-permute-done((f32[256,256]{1,0:T(8,128)S(1)}, f32[256,256]{1,0:T(8,128)S(1)}, u32[]{:S(2)}, u32[]{:S(2)}) %collective-permute-start.9) | collective-permute-done | bytes 262176 | tf_op jit(solution)/shard_map/ppermute | solution.py:19
  22.6 0.0 copy-start.5
  22.6 1.9 %collective-permute-start.10 = (bf16[256,256]{1,0:T(8,128)(2,1)S(1)}, bf16[256,256]{1,0:T(8,128)(2,1)S(1)}, u32[]{:S(2)}, u32[]{:S(2)}) collective-permute-start(bf16[256,256]{1,0:T(8,128)(2,1)S(1)} %fusion.4), channel_id=1, source_target_pairs={{0,2},{1,3},{2,0},{3,1},{4,6},{5,7},{6,4},{7,5},{8,10},{9,11},{10,... | collective-permute-start | bytes 393224 | tf_op jit(solution)/shard_map/ppermute | solution.py:25
  24.5 0.0 collective-permute-done.8
  24.5 3.8 %collective-permute-done.10 = bf16[256,256]{1,0:T(8,128)(2,1)S(1)} collective-permute-done((bf16[256,256]{1,0:T(8,128)(2,1)S(1)}, bf16[256,256]{1,0:T(8,128)(2,1)S(1)}, u32[]{:S(2)}, u32[]{:S(2)}) %collective-permute-start.10) | collective-permute-done | bytes 131104 | tf_op jit(solution)/shard_map/ppermute | solution.py:25
  28.3 0.0 copy-done.7
  28.3 0.4 multiply_add_fusion
  28.7 0.0 copy-done.5
  28.8 3.2 %collective-permute-start.11 = (bf16[256,256]{1,0:T(8,128)(2,1)S(1)}, bf16[256,256]{1,0:T(8,128)(2,1)S(1)}, u32[]{:S(2)}, u32[]{:S(2)}) collective-permute-start(bf16[256,256]{1,0:T(8,128)(2,1)S(1)} %get-tuple-element.41.rest_0_), channel_id=1, source_target_pairs={{0,12},{1,13},{2,6},{3,7},{4,0},{5,1},{6,10},{7,11},{8,4},{9,5},{1... | collective-permute-start | bytes 393224 | tf_op jit(solution)/shard_map/ppermute | solution.py:40
  31.9 0.0 collective-permute-start.13
  31.9 0.0 collective-permute-start.14
  31.9 0.0 collective-permute-start.17
  31.9 3.7 %collective-permute-done.11.rest_1_ = bf16[256,256]{1,0:T(8,128)(2,1)S(1)} collective-permute-done((bf16[256,256]{1,0:T(8,128)(2,1)S(1)}, bf16[256,256]{1,0:T(8,128)(2,1)S(1)}, u32[]{:S(2)}, u32[]{:S(2)}) %collective-permute-start.11) | collective-permute-done | bytes 131104 | tf_op jit(solution)/shard_map/ppermute | solution.py:40
  35.6 2.8 %collective-permute-start.12 = (bf16[256,256]{1,0:T(8,128)(2,1)S(1)}, bf16[256,256]{1,0:T(8,128)(2,1)S(1)}, u32[]{:S(2)}, u32[]{:S(2)}) collective-permute-start(bf16[256,256]{1,0:T(8,128)(2,1)S(1)} %collective-permute-done.11.rest_1_), channel_id=1, source_target_pairs={{0,2},{1,3},{2,0},{3,1},{4,6},{5,7},{6,4},{7,5},{8,10},{9,11},{10,... | collective-permute-start | bytes 393224 | tf_op jit(solution)/shard_map/ppermute | solution.py:25
  38.4 1.6 %collective-permute-start.18 = (bf16[256,256]{1,0:T(8,128)(2,1)S(1)}, bf16[256,256]{1,0:T(8,128)(2,1)S(1)}, u32[]{:S(2)}, u32[]{:S(2)}) collective-permute-start(bf16[256,256]{1,0:T(8,128)(2,1)S(1)} %collective-permute-done.11.rest_1_), channel_id=1, source_target_pairs={{0,12},{1,13},{2,6},{3,7},{4,0},{5,1},{6,10},{7,11},{8,4},{9,5},{1... | collective-permute-start | bytes 393224 | tf_op jit(solution)/shard_map/ppermute | solution.py:40
  40.0 0.0 collective-permute-done.13
  40.0 0.0 collective-permute-start.15
  40.1 1.3 %collective-permute-done.12 = bf16[256,256]{1,0:T(8,128)(2,1)S(1)} collective-permute-done((bf16[256,256]{1,0:T(8,128)(2,1)S(1)}, bf16[256,256]{1,0:T(8,128)(2,1)S(1)}, u32[]{:S(2)}, u32[]{:S(2)}) %collective-permute-start.12) | collective-permute-done | bytes 131104 | tf_op jit(solution)/shard_map/ppermute | solution.py:25
  41.4 0.1 collective-permute-start.16
  41.5 0.0 collective-permute-done.14
  41.5 0.0 collective-permute-done.15
  41.5 1.4 %collective-permute-done.16 = bf16[512,256]{1,0:T(8,128)(2,1)S(1)} collective-permute-done((bf16[512,256]{1,0:T(8,128)(2,1)S(1)}, bf16[512,256]{1,0:T(8,128)(2,1)S(1)}, u32[]{:S(2)}, u32[]{:S(2)}) %collective-permute-start.16) | collective-permute-done | bytes 262176 | tf_op jit(solution)/shard_map/ppermute | solution.py:19
  43.0 0.0 collective-permute-done.17.rest_2_
  43.0 0.4 collective-permute-done.18.rest_3_
  43.4 2.3 %shard_map.107 = f32[1024,256]{1,0:T(8,128)S(1)} custom-call(s32[2,136]{1,0:T(2,128)S(1)} %get-tuple-element.33.plan, s32[34]{0:T(128)S(1)} %get-tuple-element.34.rows, bf16[112,128,128]{2,1,0:T(8,128)(2,1)S(1)} %copy-done, bf16[2176,256]{1,0:T(8,128)(2,1)S(1)} %constant_dynamic-update-slice_fusion.8.window, ...), custom_call_target="tpu_custom_call" | custom-call | flops 1073741824 | bytes 1048576 | tf_op jit(solution)/shard_map/pallas_call | solution.py:195
  45.7 0.1 slice_bitcast_fusion
  45.7 0.1 collective-permute-start.20
  45.8 0.5 collective-permute-start.19
  46.3 1.0 %collective-permute-done.20 = f32[256,256]{1,0:T(8,128)S(1)} collective-permute-done((f32[256,256]{1,0:T(8,128)S(1)}, f32[256,256]{1,0:T(8,128)S(1)}, u32[]{:S(2)}, u32[]{:S(2)}) %collective-permute-start.20) | collective-permute-done | bytes 262176 | tf_op jit(solution)/shard_map/ppermute | solution.py:19
  47.4 1.9 %collective-permute-start.21 = (bf16[256,256]{1,0:T(8,128)(2,1)S(1)}, bf16[256,256]{1,0:T(8,128)(2,1)S(1)}, u32[]{:S(2)}, u32[]{:S(2)}) collective-permute-start(bf16[256,256]{1,0:T(8,128)(2,1)S(1)} %fusion.2), channel_id=1, source_target_pairs={{0,2},{1,3},{2,0},{3,1},{4,6},{5,7},{6,4},{7,5},{8,10},{9,11},{10,... | collective-permute-start | bytes 393224 | tf_op jit(solution)/shard_map/ppermute | solution.py:25
  49.2 0.2 multiply_add_fusion.1
  49.4 0.0 collective-permute-done.19.mate
  49.4 3.6 %collective-permute-done.21 = bf16[256,256]{1,0:T(8,128)(2,1)S(1)} collective-permute-done((bf16[256,256]{1,0:T(8,128)(2,1)S(1)}, bf16[256,256]{1,0:T(8,128)(2,1)S(1)}, u32[]{:S(2)}, u32[]{:S(2)}) %collective-permute-start.21) | collective-permute-done | bytes 131104 | tf_op jit(solution)/shard_map/ppermute | solution.py:25
  53.0 0.1 broadcast_in_dim.5.scale
  53.1 1.0 %shard_map.108 = (f32[256,256]{1,0:T(8,128)}, f32[256,256]{1,0:T(8,128)}) custom-call(f32[256,256]{1,0:T(8,128)S(1)} %get-tuple-element.46.near, f32[256,256]{1,0:T(8,128)S(1)} %collective-permute-done.19.mate, bf16[1,256,256]{2,1,0:T(8,128)(2,1)S(1)} %bitcast.44, f32[256,256]{1,0:T(8,128)S(1)} %broadcast_in_dim.5.scale, ...), custom_call_target="tpu_custom_call" | custom-call | flops 1048576 | bytes 2097152 | tf_op jit(solution)/shard_map/pallas_call | solution.py:270
  (29 shorter events, 0.4 us)
Async XLA Ops:
  1.6 9.4 %collective-permute-start = (bf16[256,256]{1,0:T(8,128)(2,1)S(1)}, bf16[256,256]{1,0:T(8,128)(2,1)S(1)}, u32[]{:S(2)}, u32[]{:S(2)}) collective-permute-start(bf16[256,256]{1,0:T(8,128)(2,1)S(1)} %get-tuple-element.43.rest_0_), channel_id=1, source_target_pairs={{0,12},{1,13},{2,6},{3,7},{4,0},{5,1},{6,10},{7,11},{8,4},{9,5},{1... | collective-permute-start | bytes 393224 | tf_op jit(solution)/shard_map/ppermute | solution.py:40
  6.7 8.9 %collective-permute-start.2 = (bf16[256,256]{1,0:T(8,128)(2,1)S(1)}, bf16[256,256]{1,0:T(8,128)(2,1)S(1)}, u32[]{:S(2)}, u32[]{:S(2)}) collective-permute-start(bf16[256,256]{1,0:T(8,128)(2,1)S(1)} %get-tuple-element.43.rest_0_), channel_id=1, source_target_pairs={{0,2},{1,3},{2,0},{3,1},{4,6},{5,7},{6,4},{7,5},{8,10},{9,11},{10,... | collective-permute-start | bytes 393224 | tf_op jit(solution)/shard_map/ppermute | solution.py:25
  6.7 10.1 %collective-permute-start.3 = (bf16[256,256]{1,0:T(8,128)(2,1)S(1)}, bf16[256,256]{1,0:T(8,128)(2,1)S(1)}, u32[]{:S(2)}, u32[]{:S(2)}) collective-permute-start(bf16[256,256]{1,0:T(8,128)(2,1)S(1)} %get-tuple-element.43.rest_0_), channel_id=1, source_target_pairs={{0,1},{1,0},{2,3},{3,2},{4,5},{5,4},{6,7},{7,6},{8,9},{9,8},{10,11... | collective-permute-start | bytes 393224 | tf_op jit(solution)/shard_map/ppermute | solution.py:19
  6.7 11.6 %collective-permute-start.6 = (bf16[256,256]{1,0:T(8,128)(2,1)S(1)}, bf16[256,256]{1,0:T(8,128)(2,1)S(1)}, u32[]{:S(2)}, u32[]{:S(2)}) collective-permute-start(bf16[256,256]{1,0:T(8,128)(2,1)S(1)} %get-tuple-element.43.rest_0_), channel_id=1, source_target_pairs={{0,4},{1,5},{2,14},{3,15},{4,8},{5,9},{6,2},{7,3},{8,12},{9,13},{1... | collective-permute-start | bytes 393224 | tf_op jit(solution)/shard_map/ppermute | solution.py:40
  7.8 0.7 %copy-start.4 = (s32[112,2]{0,1:T(2,128)S(1)}, s32[112,2]{0,1:T(2,128)}, u32[]{:S(2)}) copy-start(s32[112,2]{0,1:T(2,128)} %param.14) | copy-start | bytes 2692
  8.4 6.4 %copy-start.1 = (bf16[4,4,32,256]{3,2,1,0:T(8,128)(2,1)S(1)}, bf16[4,4,32,256]{3,2,1,0:T(8,128)(2,1)}, u32[]{:S(2)}) copy-start(bf16[4,4,32,256]{3,2,1,0:T(8,128)(2,1)} %far_u) | copy-start | bytes 786436
  8.4 6.4 %copy-start.2 = (bf16[4,4,32,256]{3,2,1,0:T(8,128)(2,1)S(1)}, bf16[4,4,32,256]{3,2,1,0:T(8,128)(2,1)}, u32[]{:S(2)}) copy-start(bf16[4,4,32,256]{3,2,1,0:T(8,128)(2,1)} %far_v) | copy-start | bytes 786436
  8.4 6.4 %copy-start.3 = (s32[4,4]{1,0:T(4,128)S(1)}, s32[4,4]{1,0:T(4,128)}, u32[]{:S(2)}) copy-start(s32[4,4]{1,0:T(4,128)} %ranks) | copy-start | bytes 196
  8.4 9.9 %copy-start = (bf16[112,128,128]{2,1,0:T(8,128)(2,1)S(1)}, bf16[112,128,128]{2,1,0:T(8,128)(2,1)}, u32[]{:S(2)}) copy-start(bf16[112,128,128]{2,1,0:T(8,128)(2,1)} %blocks.3) | copy-start | bytes 11010052
  11.0 5.7 %collective-permute-start.1 = (bf16[256,256]{1,0:T(8,128)(2,1)S(1)}, bf16[256,256]{1,0:T(8,128)(2,1)S(1)}, u32[]{:S(2)}, u32[]{:S(2)}) collective-permute-start(bf16[256,256]{1,0:T(8,128)(2,1)S(1)} %collective-permute-done.rest_1_), channel_id=1, source_target_pairs={{0,2},{1,3},{2,0},{3,1},{4,6},{5,7},{6,4},{7,5},{8,10},{9,11},{10,... | collective-permute-start | bytes 393224 | tf_op jit(solution)/shard_map/ppermute | solution.py:25
  12.5 5.9 %collective-permute-start.7 = (bf16[256,256]{1,0:T(8,128)(2,1)S(1)}, bf16[256,256]{1,0:T(8,128)(2,1)S(1)}, u32[]{:S(2)}, u32[]{:S(2)}) collective-permute-start(bf16[256,256]{1,0:T(8,128)(2,1)S(1)} %collective-permute-done.rest_1_), channel_id=1, source_target_pairs={{0,12},{1,13},{2,6},{3,7},{4,0},{5,1},{6,10},{7,11},{8,4},{9,5},{1... | collective-permute-start | bytes 393224 | tf_op jit(solution)/shard_map/ppermute | solution.py:40
  15.6 1.4 %collective-permute-start.4 = (bf16[256,256]{1,0:T(8,128)(2,1)S(1)}, bf16[256,256]{1,0:T(8,128)(2,1)S(1)}, u32[]{:S(2)}, u32[]{:S(2)}) collective-permute-start(bf16[256,256]{1,0:T(8,128)(2,1)S(1)} %collective-permute-done.2), channel_id=1, source_target_pairs={{0,1},{1,0},{2,3},{3,2},{4,5},{5,4},{6,7},{7,6},{8,9},{9,8},{10,11... | collective-permute-start | bytes 393224 | tf_op jit(solution)/shard_map/ppermute | solution.py:19
  16.7 1.6 %collective-permute-start.5 = (bf16[512,256]{1,0:T(8,128)(2,1)S(1)}, bf16[512,256]{1,0:T(8,128)(2,1)S(1)}, u32[]{:S(2)}, u32[]{:S(2)}) collective-permute-start(bf16[512,256]{1,0:T(8,128)(2,1)S(1)} %pad_maximum_fusion), channel_id=1, source_target_pairs={{0,1},{1,0},{2,3},{3,2},{4,5},{5,4},{6,7},{7,6},{8,9},{9,8},{10,11... | collective-permute-start | bytes 786440 | tf_op jit(solution)/shard_map/ppermute | solution.py:19
  20.8 3.7 %copy-start.8 = (f32[256]{0:T(256)S(1)}, f32[256]{0:T(256)}, u32[]{:S(2)}) copy-start(f32[256]{0:T(256)} %param.12) | copy-start | bytes 3076
  20.9 7.4 %copy-start.6 = (f32[256,256]{1,0:T(8,128)S(1)}, f32[256,256]{1,0:T(8,128)}, u32[]{:S(2)}) copy-start(f32[256,256]{1,0:T(8,128)} %param.10) | copy-start | bytes 786436
  20.9 7.4 %copy-start.7 = (f32[256,256]{1,0:T(8,128)S(1)}, f32[256,256]{1,0:T(8,128)}, u32[]{:S(2)}) copy-start(f32[256,256]{1,0:T(8,128)} %param.11) | copy-start | bytes 786436
  20.9 1.6 %collective-permute-start.9 = (f32[256,256]{1,0:T(8,128)S(1)}, f32[256,256]{1,0:T(8,128)S(1)}, u32[]{:S(2)}, u32[]{:S(2)}) collective-permute-start(f32[256,256]{1,0:T(8,128)S(1)} %get-tuple-element.48), channel_id=1, source_target_pairs={{0,1},{1,0},{2,3},{3,2},{4,5},{5,4},{6,7},{7,6},{8,9},{9,8},{10,11... | collective-permute-start | bytes 786440 | tf_op jit(solution)/shard_map/ppermute | solution.py:19
  21.1 3.4 %collective-permute-start.8 = (f32[256,256]{1,0:T(8,128)S(1)}, f32[256,256]{1,0:T(8,128)S(1)}, u32[]{:S(2)}, u32[]{:S(2)}) collective-permute-start(f32[256,256]{1,0:T(8,128)S(1)} %get-tuple-element.47), channel_id=1, source_target_pairs={{0,1},{1,0},{2,3},{3,2},{4,5},{5,4},{6,7},{7,6},{8,9},{9,8},{10,11... | collective-permute-start | bytes 786440 | tf_op jit(solution)/shard_map/ppermute | solution.py:19
  22.6 6.1 %copy-start.5 = (f32[256,256]{1,0:T(8,128)S(1)}, f32[256,256]{1,0:T(8,128)}, u32[]{:S(2)}) copy-start(f32[256,256]{1,0:T(8,128)} %param.9) | copy-start | bytes 786436
  22.6 5.7 %collective-permute-start.10 = (bf16[256,256]{1,0:T(8,128)(2,1)S(1)}, bf16[256,256]{1,0:T(8,128)(2,1)S(1)}, u32[]{:S(2)}, u32[]{:S(2)}) collective-permute-start(bf16[256,256]{1,0:T(8,128)(2,1)S(1)} %fusion.4), channel_id=1, source_target_pairs={{0,2},{1,3},{2,0},{3,1},{4,6},{5,7},{6,4},{7,5},{8,10},{9,11},{10,... | collective-permute-start | bytes 393224 | tf_op jit(solution)/shard_map/ppermute | solution.py:25
  28.8 6.9 %collective-permute-start.11 = (bf16[256,256]{1,0:T(8,128)(2,1)S(1)}, bf16[256,256]{1,0:T(8,128)(2,1)S(1)}, u32[]{:S(2)}, u32[]{:S(2)}) collective-permute-start(bf16[256,256]{1,0:T(8,128)(2,1)S(1)} %get-tuple-element.41.rest_0_), channel_id=1, source_target_pairs={{0,12},{1,13},{2,6},{3,7},{4,0},{5,1},{6,10},{7,11},{8,4},{9,5},{1... | collective-permute-start | bytes 393224 | tf_op jit(solution)/shard_map/ppermute | solution.py:40
  31.9 8.1 %collective-permute-start.13 = (bf16[256,256]{1,0:T(8,128)(2,1)S(1)}, bf16[256,256]{1,0:T(8,128)(2,1)S(1)}, u32[]{:S(2)}, u32[]{:S(2)}) collective-permute-start(bf16[256,256]{1,0:T(8,128)(2,1)S(1)} %get-tuple-element.41.rest_0_), channel_id=1, source_target_pairs={{0,2},{1,3},{2,0},{3,1},{4,6},{5,7},{6,4},{7,5},{8,10},{9,11},{10,... | collective-permute-start | bytes 393224 | tf_op jit(solution)/shard_map/ppermute | solution.py:25
  31.9 9.6 %collective-permute-start.14 = (bf16[256,256]{1,0:T(8,128)(2,1)S(1)}, bf16[256,256]{1,0:T(8,128)(2,1)S(1)}, u32[]{:S(2)}, u32[]{:S(2)}) collective-permute-start(bf16[256,256]{1,0:T(8,128)(2,1)S(1)} %get-tuple-element.41.rest_0_), channel_id=1, source_target_pairs={{0,1},{1,0},{2,3},{3,2},{4,5},{5,4},{6,7},{7,6},{8,9},{9,8},{10,11... | collective-permute-start | bytes 393224 | tf_op jit(solution)/shard_map/ppermute | solution.py:19
  31.9 11.1 %collective-permute-start.17 = (bf16[256,256]{1,0:T(8,128)(2,1)S(1)}, bf16[256,256]{1,0:T(8,128)(2,1)S(1)}, u32[]{:S(2)}, u32[]{:S(2)}) collective-permute-start(bf16[256,256]{1,0:T(8,128)(2,1)S(1)} %get-tuple-element.41.rest_0_), channel_id=1, source_target_pairs={{0,4},{1,5},{2,14},{3,15},{4,8},{5,9},{6,2},{7,3},{8,12},{9,13},{1... | collective-permute-start | bytes 393224 | tf_op jit(solution)/shard_map/ppermute | solution.py:40
  35.6 5.7 %collective-permute-start.12 = (bf16[256,256]{1,0:T(8,128)(2,1)S(1)}, bf16[256,256]{1,0:T(8,128)(2,1)S(1)}, u32[]{:S(2)}, u32[]{:S(2)}) collective-permute-start(bf16[256,256]{1,0:T(8,128)(2,1)S(1)} %collective-permute-done.11.rest_1_), channel_id=1, source_target_pairs={{0,2},{1,3},{2,0},{3,1},{4,6},{5,7},{6,4},{7,5},{8,10},{9,11},{10,... | collective-permute-start | bytes 393224 | tf_op jit(solution)/shard_map/ppermute | solution.py:25
  38.4 5.0 %collective-permute-start.18 = (bf16[256,256]{1,0:T(8,128)(2,1)S(1)}, bf16[256,256]{1,0:T(8,128)(2,1)S(1)}, u32[]{:S(2)}, u32[]{:S(2)}) collective-permute-start(bf16[256,256]{1,0:T(8,128)(2,1)S(1)} %collective-permute-done.11.rest_1_), channel_id=1, source_target_pairs={{0,12},{1,13},{2,6},{3,7},{4,0},{5,1},{6,10},{7,11},{8,4},{9,5},{1... | collective-permute-start | bytes 393224 | tf_op jit(solution)/shard_map/ppermute | solution.py:40
  40.0 1.5 %collective-permute-start.15 = (bf16[256,256]{1,0:T(8,128)(2,1)S(1)}, bf16[256,256]{1,0:T(8,128)(2,1)S(1)}, u32[]{:S(2)}, u32[]{:S(2)}) collective-permute-start(bf16[256,256]{1,0:T(8,128)(2,1)S(1)} %collective-permute-done.13), channel_id=1, source_target_pairs={{0,1},{1,0},{2,3},{3,2},{4,5},{5,4},{6,7},{7,6},{8,9},{9,8},{10,11... | collective-permute-start | bytes 393224 | tf_op jit(solution)/shard_map/ppermute | solution.py:19
  41.4 1.6 %collective-permute-start.16 = (bf16[512,256]{1,0:T(8,128)(2,1)S(1)}, bf16[512,256]{1,0:T(8,128)(2,1)S(1)}, u32[]{:S(2)}, u32[]{:S(2)}) collective-permute-start(bf16[512,256]{1,0:T(8,128)(2,1)S(1)} %pad_maximum_fusion.1), channel_id=1, source_target_pairs={{0,1},{1,0},{2,3},{3,2},{4,5},{5,4},{6,7},{7,6},{8,9},{9,8},{10,11... | collective-permute-start | bytes 786440 | tf_op jit(solution)/shard_map/ppermute | solution.py:19
  45.7 1.6 %collective-permute-start.20 = (f32[256,256]{1,0:T(8,128)S(1)}, f32[256,256]{1,0:T(8,128)S(1)}, u32[]{:S(2)}, u32[]{:S(2)}) collective-permute-start(f32[256,256]{1,0:T(8,128)S(1)} %get-tuple-element.44), channel_id=1, source_target_pairs={{0,1},{1,0},{2,3},{3,2},{4,5},{5,4},{6,7},{7,6},{8,9},{9,8},{10,11... | collective-permute-start | bytes 786440 | tf_op jit(solution)/shard_map/ppermute | solution.py:19
  45.8 3.6 %collective-permute-start.19 = (f32[256,256]{1,0:T(8,128)S(1)}, f32[256,256]{1,0:T(8,128)S(1)}, u32[]{:S(2)}, u32[]{:S(2)}) collective-permute-start(f32[256,256]{1,0:T(8,128)S(1)} %get-tuple-element.45), channel_id=1, source_target_pairs={{0,1},{1,0},{2,3},{3,2},{4,5},{5,4},{6,7},{7,6},{8,9},{9,8},{10,11... | collective-permute-start | bytes 786440 | tf_op jit(solution)/shard_map/ppermute | solution.py:19
  47.4 5.7 %collective-permute-start.21 = (bf16[256,256]{1,0:T(8,128)(2,1)S(1)}, bf16[256,256]{1,0:T(8,128)(2,1)S(1)}, u32[]{:S(2)}, u32[]{:S(2)}) collective-permute-start(bf16[256,256]{1,0:T(8,128)(2,1)S(1)} %fusion.2), channel_id=1, source_target_pairs={{0,2},{1,3},{2,0},{3,1},{4,6},{5,7},{6,4},{7,5},{8,10},{9,11},{10,... | collective-permute-start | bytes 393224 | tf_op jit(solution)/shard_map/ppermute | solution.py:25

commit v6 on v5

--- a/solution.py
+++ b/solution.py
@@ -12,6 +12,7 @@
 STEP = 0.2
 LOG_TWO = 0.6931471805599453
 WIDTH = 4
+PARTS = 4
 
 
 def core_swap(array):
@@ -50,7 +51,7 @@
     return lax.axis_index("clu"), lax.div(row, CORES), lax.rem(row, CORES)
 
 
-def plan_kernel(leaf, own, pairs, plan, rows, free, source_rows, target_rows):
+def plan_kernel(leaf, own, pairs, plan, free, source_rows, target_rows):
     devices = lax.axis_size("row")
     chips, clusters = devices // CORES, devices * own
     group, chip, core = here()
@@ -72,8 +73,7 @@
     for i in range(plan.shape[1]):
         plan[0, i] = 0
         plan[1, i] = 4 * chips * own * leaf
-    for i in range(rows.shape[0]):
-        rows[i] = 0
+        plan[2, i] = 0
 
     def put(j, used):
         target = pairs[0, j] - group * clusters
@@ -83,13 +83,13 @@
         free[target] = at + 1
         plan[0, at] = j
         plan[1, at] = source_rows[pairs[1, j] - group * clusters + REACH]
-        rows[lax.shift_right_logical(at, WIDTH.bit_length() - 1)] = target_rows[target]
+        plan[2, lax.shift_right_logical(at, WIDTH.bit_length() - 1)] = target_rows[target]
         return used + full.astype(jnp.int32)
 
     lax.fori_loop(0, pairs.shape[1], put, jnp.int32(0), unroll=8)
 
 
-def stress_kernel(leaf, plan, rows, blocks, window, far_u, far_v, *rest):
+def stress_kernel(leaf, plan, blocks, window, far_u, far_v, *rest):
     targets, elems, ranks = far_u.shape
     groups, rank = far_v.shape[0], far_v.shape[1] // targets
     columns, out = rest[:groups], rest[groups]
@@ -104,7 +104,8 @@
             preferred_element_type=jnp.float32,
         )
     products = []
-    for i in range(rows.shape[0]):
+    chunks = plan.shape[1] // WIDTH
+    for i in range(chunks):
         places = range(i * WIDTH, (i + 1) * WIDTH)
         sources = [pl.ds(pl.multiple_of(plan[1, p], leaf), leaf) for p in places]
         products.append(
@@ -114,8 +115,8 @@
                 preferred_element_type=jnp.float32,
             )
         )
-    for i in range(rows.shape[0]):
-        out[pl.ds(pl.multiple_of(rows[i], leaf), leaf), :] += products[i]
+    for i in range(chunks):
+        out[pl.ds(pl.multiple_of(plan[2, i], leaf), leaf), :] += products[i]
 
 
 def bases_kernel(ranks, far_u, far_v, by_target, by_source):
@@ -136,15 +137,27 @@
         by_target[t] = bases.astype(jnp.float32).T.astype(jnp.bfloat16)
 
 
-def finish_kernel(near, mate, received, scale, shift, weight, slip, state, slip_out, state_out):
-    stress = near[...] + mate[...]
-    for s in range(received.shape[0]):
-        stress = stress + received[s].astype(jnp.float32)
-    halved = stress * scale[...] + shift[...]
-    velocity = weight[...] * (jnp.exp(halved - LOG_TWO) - jnp.exp(-halved - LOG_TWO))
-    speed = jnp.abs(velocity)
-    slip_out[...] = slip[...] + 0.5 * STEP * velocity
-    state_out[...] = state[...] - 0.5 * STEP * (speed / (1.0 + speed))
+def finish_kernel(
+    near, mate, received, scale, shift, weight, slip, state, slip_out, state_out, slips, states, done
+):
+    parts = done.shape[0]
+    size = near.shape[0] // parts
+    copies = []
+    for part in range(parts):
+        rows = pl.ds(part * size, size)
+        stress = near[rows, :] + mate[rows, :]
+        for s in range(received.shape[0]):
+            stress = stress + received[s, rows, :].astype(jnp.float32)
+        halved = stress * scale[rows, :] + shift[rows, :]
+        velocity = weight[rows, :] * (jnp.exp(halved - LOG_TWO) - jnp.exp(-halved - LOG_TWO))
+        speed = jnp.abs(velocity)
+        slips[rows, :] = slip[rows, :] + 0.5 * STEP * velocity
+        states[rows, :] = state[rows, :] - 0.5 * STEP * (speed / (1.0 + speed))
+        for at, (held, out) in enumerate(((slips, slip_out), (states, state_out))):
+            copies.append(pltpu.make_async_copy(held.at[rows], out.at[rows], done.at[part, at]))
+            copies[-1].start()
+    for copy in copies:
+        copy.wait()
 
 
 VMEM = pl.BlockSpec(memory_space=pltpu.VMEM)
@@ -157,12 +170,9 @@
     chunks = (pairs.shape[1] + targets * (WIDTH - 1)) // WIDTH
     return pl.pallas_call(
         functools.partial(plan_kernel, leaf, own),
-        out_shape=(
-            jax.ShapeDtypeStruct((2, chunks * WIDTH), jnp.int32),
-            jax.ShapeDtypeStruct((chunks,), jnp.int32),
-        ),
+        out_shape=jax.ShapeDtypeStruct((3, chunks * WIDTH), jnp.int32),
         in_specs=[SMEM],
-        out_specs=(SMEM, SMEM),
+        out_specs=SMEM,
         scratch_shapes=[
             pltpu.SMEM((targets,), jnp.int32),
             pltpu.SMEM((targets + 2 * REACH,), jnp.int32),
@@ -195,7 +205,7 @@
     return pl.pallas_call(
         functools.partial(stress_kernel, leaf),
         out_shape=jax.ShapeDtypeStruct((targets * elems, members), jnp.float32),
-        in_specs=[SMEM] * 2 + [VMEM] * (4 + groups),
+        in_specs=[SMEM] + [VMEM] * (4 + groups),
         out_specs=VMEM,
         compiler_params=PARAMS,
         cost_estimate=pl.CostEstimate(
@@ -203,7 +213,7 @@
             bytes_accessed=4 * targets * elems * members,
             transcendentals=0,
         ),
-    )(plan[0], plan[1], blocks, window, far_u, far_v, *columns)
+    )(plan, blocks, window, far_u, far_v, *columns)
 
 
 def slip_rates(stress, state, load, friction_a):
@@ -235,9 +245,9 @@
 
     def section_stress(field):
         half = field.astype(jnp.bfloat16)
+        near = jnp.concatenate([half] + [chip_shift(half, s) for s in range(1, chips)])
         straight = end_shift(half, 1)
         straight, (plan, bases) = planned(straight)
-        near = jnp.concatenate([half] + [chip_shift(half, s) for s in range(1, chips)])
         column = [half, straight, end_shift(half, -1)]
         while len(column) < groups:
             column.append(end_shift(column[-2], 1 if len(column) % 2 else -1))
@@ -274,7 +284,12 @@
             jax.ShapeDtypeStruct(slip.shape, jnp.float32),
         ),
         in_specs=[VMEM] * 8,
-        out_specs=(VMEM, VMEM),
+        out_specs=(pl.BlockSpec(memory_space=pl.ANY), pl.BlockSpec(memory_space=pl.ANY)),
+        scratch_shapes=[
+            pltpu.VMEM(slip.shape, jnp.float32),
+            pltpu.VMEM(slip.shape, jnp.float32),
+            pltpu.SemaphoreType.DMA((PARTS, 2)),
+        ],
         compiler_params=PARAMS,
         cost_estimate=pl.CostEstimate(
             flops=16 * slip.size, bytes_accessed=32 * slip.size, transcendentals=2 * slip.size

time: 54.3 us -> 54.3 us (level)
  transfers between devices with their start and end apart: 22 -> 22, of which waited for: 11 -> 10; matrix products, arithmetic and copies ran while one was open for 1% -> 1% of each run, Pallas kernels for 6% -> 6%
where the time goes in v6:
time: 54.3 us; the launch traced here: 54.1 us
  starting transfers between devices  22.4 us (41%)
  waiting for transfers between devices  19 us (35%)
  Pallas kernels  9 us (17%)
  other arithmetic  1.66 us (3%)
  local copies, waits for them, and re-layouts  1.06 us (2%)
  between operations  1 us (2%)
    ppermute x6, starting transfers between devices, end_shift(): return lax.ppermute(array, ('clu', 'row'), pairs)  12.8 us
    ppermute x6, waiting for transfers between devices, chip_shift(): return lax.ppermute(array, 'row', pairs)  10 us
    ppermute x6, starting transfers between devices, chip_shift(): return lax.ppermute(array, 'row', pairs)  8.25 us
    ppermute x10, waiting for transfers between devices, core_swap(): return lax.ppermute(array, 'row', [(i, i ^ 1) for i in range(devices)])  4.95 us
    pallas_call x2, Pallas kernels, partial_stress(): pl.pallas_call(functools.partial(stress_kernel, leaf), out_shape=jax.Shap...  4.62 us
    ppermute x6, waiting for transfers between devices, end_shift(): return lax.ppermute(array, ('clu', 'row'), pairs)  4.03 us
    pallas_call x1, Pallas kernels, planned_blocks(): pl.pallas_call(functools.partial(plan_kernel, leaf, own), out_shape=jax.S...  2.71 us
    ppermute x10, starting transfers between devices, core_swap(): return lax.ppermute(array, 'row', [(i, i ^ 1) for i in range(devices)])  1.36 us
  transfers between devices with their start and end apart: 22, of which 10 were waited for; matrix products, arithmetic and copies ran while one was open for 1% of the time, Pallas kernels for 6%

profile of v6, /device:TPU:0, one launch (start us, length us, event | category | flops | bytes accessed | tf_op | source)
XLA Modules:
  0.0 54.1 jit_solution(16178899045817182479)
XLA Ops:
  0.6 1.0 %constant_dynamic-update-slice_fusion.7 = (bf16[2176,256]{1,0:T(8,128)(2,1)S(1)}, bf16[256,256]{1,0:T(8,128)(2,1)S(1)}) fusion(f32[256,256]{1,0:T(8,128)} %param.9), kind=kLoop, calls=%fused_computation.34 | loop fusion | flops 65535 | bytes 524288
  1.6 5.1 %collective-permute-start = (bf16[256,256]{1,0:T(8,128)(2,1)S(1)}, bf16[256,256]{1,0:T(8,128)(2,1)S(1)}, u32[]{:S(2)}, u32[]{:S(2)}) collective-permute-start(bf16[256,256]{1,0:T(8,128)(2,1)S(1)} %get-tuple-element.35.rest_0_), channel_id=1, source_target_pairs={{0,12},{1,13},{2,6},{3,7},{4,0},{5,1},{6,10},{7,11},{8,4},{9,5},{1... | collective-permute-start | bytes 393224 | tf_op jit(solution)/shard_map/ppermute | solution.py:41
  6.7 0.0 collective-permute-start.2
  6.7 0.0 collective-permute-start.3
  6.7 1.0 %collective-permute-start.6 = (bf16[256,256]{1,0:T(8,128)(2,1)S(1)}, bf16[256,256]{1,0:T(8,128)(2,1)S(1)}, u32[]{:S(2)}, u32[]{:S(2)}) collective-permute-start(bf16[256,256]{1,0:T(8,128)(2,1)S(1)} %get-tuple-element.35.rest_0_), channel_id=1, source_target_pairs={{0,4},{1,5},{2,14},{3,15},{4,8},{5,9},{6,2},{7,3},{8,12},{9,13},{1... | collective-permute-start | bytes 393224 | tf_op jit(solution)/shard_map/ppermute | solution.py:41
  7.8 0.7 %copy-done.4 = s32[112,2]{0,1:T(2,128)S(1)} copy-done((s32[112,2]{0,1:T(2,128)S(1)}, s32[112,2]{0,1:T(2,128)}, u32[]{:S(2)}) %copy-start.4) | copy-done | bytes 920
  8.4 2.7 %shard_map.104.plan = s32[3,136]{1,0:T(4,128)S(1)} custom-call(s32[2,112]{1,0:T(2,128)S(1)} %bitcast.45), custom_call_target="tpu_custom_call" | custom-call | flops 4000000000 | bytes 10000000 | tf_op jit(solution)/shard_map/pallas_call | solution.py:171
  11.2 0.0 collective-permute-done.rest_1_
  11.2 1.5 %collective-permute-start.1 = (bf16[256,256]{1,0:T(8,128)(2,1)S(1)}, bf16[256,256]{1,0:T(8,128)(2,1)S(1)}, u32[]{:S(2)}, u32[]{:S(2)}) collective-permute-start(bf16[256,256]{1,0:T(8,128)(2,1)S(1)} %collective-permute-done.rest_1_), channel_id=1, source_target_pairs={{0,2},{1,3},{2,0},{3,1},{4,6},{5,7},{6,4},{7,5},{8,10},{9,11},{10,... | collective-permute-start | bytes 393224 | tf_op jit(solution)/shard_map/ppermute | solution.py:26
  12.7 2.2 %collective-permute-start.7 = (bf16[256,256]{1,0:T(8,128)(2,1)S(1)}, bf16[256,256]{1,0:T(8,128)(2,1)S(1)}, u32[]{:S(2)}, u32[]{:S(2)}) collective-permute-start(bf16[256,256]{1,0:T(8,128)(2,1)S(1)} %collective-permute-done.rest_1_), channel_id=1, source_target_pairs={{0,12},{1,13},{2,6},{3,7},{4,0},{5,1},{6,10},{7,11},{8,4},{9,5},{1... | collective-permute-start | bytes 393224 | tf_op jit(solution)/shard_map/ppermute | solution.py:41
  14.8 0.0 copy-done.1
  14.8 0.0 copy-done.2
  14.8 0.0 copy-done.3
  14.8 0.7 %shard_map.105 = (bf16[4,256,128]{2,1,0:T(8,128)(2,1)S(1)}, bf16[4,128,256]{2,1,0:T(8,128)(2,1)S(1)}) custom-call(s32[4,4]{1,0:T(4,128)S(1)} %copy-done.3, bf16[4,4,32,256]{3,2,1,0:T(8,128)(2,1)S(1)} %copy-done.1, bf16[4,4,32,256]{3,2,1,0:T(8,128)(2,1)S(1)} %copy-done.2), custom_call_target="tpu_custom_call" | custom-call | flops 1024 | bytes 1000000 | tf_op jit(solution)/shard_map/pallas_call | solution.py:188
  15.6 0.0 collective-permute-done.2
  15.6 0.1 collective-permute-start.4
  15.7 1.2 %collective-permute-done.1 = bf16[256,256]{1,0:T(8,128)(2,1)S(1)} collective-permute-done((bf16[256,256]{1,0:T(8,128)(2,1)S(1)}, bf16[256,256]{1,0:T(8,128)(2,1)S(1)}, u32[]{:S(2)}, u32[]{:S(2)}) %collective-permute-start.1) | collective-permute-done | bytes 131104 | tf_op jit(solution)/shard_map/ppermute | solution.py:26
  16.9 0.1 collective-permute-start.5
  17.0 0.0 collective-permute-done.3
  17.0 0.0 collective-permute-done.4
  17.0 1.4 %collective-permute-done.5 = bf16[512,256]{1,0:T(8,128)(2,1)S(1)} collective-permute-done((bf16[512,256]{1,0:T(8,128)(2,1)S(1)}, bf16[512,256]{1,0:T(8,128)(2,1)S(1)}, u32[]{:S(2)}, u32[]{:S(2)}) %collective-permute-start.5) | collective-permute-done | bytes 262176 | tf_op jit(solution)/shard_map/ppermute | solution.py:20
  18.5 0.0 collective-permute-done.6.rest_2_
  18.5 0.0 collective-permute-done.7.rest_3_
  18.5 0.0 copy-done
  18.6 2.3 %shard_map.106 = f32[1024,256]{1,0:T(8,128)S(1)} custom-call(s32[3,136]{1,0:T(4,128)S(1)} %shard_map.104.plan, bf16[112,128,128]{2,1,0:T(8,128)(2,1)S(1)} %copy-done, bf16[2176,256]{1,0:T(8,128)(2,1)S(1)} %constant_dynamic-update-slice_fusion.window, bf16[4,256,128]{2,1,0:T(8,128)(2,1)S(1)} %get-tuple-element.28.far_u, ...), custom_call_target="tpu_custom_call" | custom-call | flops 1073741824 | bytes 1048576 | tf_op jit(solution)/shard_map/pallas_call | solution.py:205
  20.9 0.0 copy-start.8
  20.9 0.0 copy-start.6
  20.9 0.0 copy-start.7
  21.0 0.2 collective-permute-start.9
  21.2 0.4 collective-permute-start.8
  21.5 1.0 %collective-permute-done.9 = f32[256,256]{1,0:T(8,128)S(1)} collective-permute-done((f32[256,256]{1,0:T(8,128)S(1)}, f32[256,256]{1,0:T(8,128)S(1)}, u32[]{:S(2)}, u32[]{:S(2)}) %collective-permute-start.9) | collective-permute-done | bytes 262176 | tf_op jit(solution)/shard_map/ppermute | solution.py:20
  22.6 0.0 copy-start.5
  22.6 1.9 %collective-permute-start.10 = (bf16[256,256]{1,0:T(8,128)(2,1)S(1)}, bf16[256,256]{1,0:T(8,128)(2,1)S(1)}, u32[]{:S(2)}, u32[]{:S(2)}) collective-permute-start(bf16[256,256]{1,0:T(8,128)(2,1)S(1)} %fusion.4), channel_id=1, source_target_pairs={{0,2},{1,3},{2,0},{3,1},{4,6},{5,7},{6,4},{7,5},{8,10},{9,11},{10,... | collective-permute-start | bytes 393224 | tf_op jit(solution)/shard_map/ppermute | solution.py:26
  24.5 0.0 collective-permute-done.8
  24.5 3.8 %collective-permute-done.10 = bf16[256,256]{1,0:T(8,128)(2,1)S(1)} collective-permute-done((bf16[256,256]{1,0:T(8,128)(2,1)S(1)}, bf16[256,256]{1,0:T(8,128)(2,1)S(1)}, u32[]{:S(2)}, u32[]{:S(2)}) %collective-permute-start.10) | collective-permute-done | bytes 131104 | tf_op jit(solution)/shard_map/ppermute | solution.py:26
  28.3 0.0 copy-done.7
  28.3 0.4 multiply_add_fusion
  28.8 3.0 %collective-permute-start.11 = (bf16[256,256]{1,0:T(8,128)(2,1)S(1)}, bf16[256,256]{1,0:T(8,128)(2,1)S(1)}, u32[]{:S(2)}, u32[]{:S(2)}) collective-permute-start(bf16[256,256]{1,0:T(8,128)(2,1)S(1)} %get-tuple-element.33.rest_0_), channel_id=1, source_target_pairs={{0,12},{1,13},{2,6},{3,7},{4,0},{5,1},{6,10},{7,11},{8,4},{9,5},{1... | collective-permute-start | bytes 393224 | tf_op jit(solution)/shard_map/ppermute | solution.py:41
  31.8 0.0 collective-permute-start.13
  31.8 0.0 collective-permute-start.14
  31.8 0.0 collective-permute-start.17
  31.8 3.7 %collective-permute-done.11.rest_1_ = bf16[256,256]{1,0:T(8,128)(2,1)S(1)} collective-permute-done((bf16[256,256]{1,0:T(8,128)(2,1)S(1)}, bf16[256,256]{1,0:T(8,128)(2,1)S(1)}, u32[]{:S(2)}, u32[]{:S(2)}) %collective-permute-start.11) | collective-permute-done | bytes 131104 | tf_op jit(solution)/shard_map/ppermute | solution.py:41
  35.5 3.0 %collective-permute-start.12 = (bf16[256,256]{1,0:T(8,128)(2,1)S(1)}, bf16[256,256]{1,0:T(8,128)(2,1)S(1)}, u32[]{:S(2)}, u32[]{:S(2)}) collective-permute-start(bf16[256,256]{1,0:T(8,128)(2,1)S(1)} %collective-permute-done.11.rest_1_), channel_id=1, source_target_pairs={{0,2},{1,3},{2,0},{3,1},{4,6},{5,7},{6,4},{7,5},{8,10},{9,11},{10,... | collective-permute-start | bytes 393224 | tf_op jit(solution)/shard_map/ppermute | solution.py:26
  38.4 1.4 %collective-permute-start.18 = (bf16[256,256]{1,0:T(8,128)(2,1)S(1)}, bf16[256,256]{1,0:T(8,128)(2,1)S(1)}, u32[]{:S(2)}, u32[]{:S(2)}) collective-permute-start(bf16[256,256]{1,0:T(8,128)(2,1)S(1)} %collective-permute-done.11.rest_1_), channel_id=1, source_target_pairs={{0,12},{1,13},{2,6},{3,7},{4,0},{5,1},{6,10},{7,11},{8,4},{9,5},{1... | collective-permute-start | bytes 393224 | tf_op jit(solution)/shard_map/ppermute | solution.py:41
  39.9 0.0 collective-permute-done.13
  39.9 0.0 collective-permute-start.15
  39.9 1.5 %collective-permute-done.12 = bf16[256,256]{1,0:T(8,128)(2,1)S(1)} collective-permute-done((bf16[256,256]{1,0:T(8,128)(2,1)S(1)}, bf16[256,256]{1,0:T(8,128)(2,1)S(1)}, u32[]{:S(2)}, u32[]{:S(2)}) %collective-permute-start.12) | collective-permute-done | bytes 131104 | tf_op jit(solution)/shard_map/ppermute | solution.py:26
  41.4 0.1 collective-permute-start.16
  41.5 0.0 collective-permute-done.14
  41.5 0.0 collective-permute-done.15
  41.6 1.4 %collective-permute-done.16 = bf16[512,256]{1,0:T(8,128)(2,1)S(1)} collective-permute-done((bf16[512,256]{1,0:T(8,128)(2,1)S(1)}, bf16[512,256]{1,0:T(8,128)(2,1)S(1)}, u32[]{:S(2)}, u32[]{:S(2)}) %collective-permute-start.16) | collective-permute-done | bytes 262176 | tf_op jit(solution)/shard_map/ppermute | solution.py:20
  43.0 0.0 collective-permute-done.17.rest_2_
  43.1 0.4 collective-permute-done.18.rest_3_
  43.4 2.3 %shard_map.107 = f32[1024,256]{1,0:T(8,128)S(1)} custom-call(s32[3,136]{1,0:T(4,128)S(1)} %shard_map.104.plan, bf16[112,128,128]{2,1,0:T(8,128)(2,1)S(1)} %copy-done, bf16[2176,256]{1,0:T(8,128)(2,1)S(1)} %constant_dynamic-update-slice_fusion.8.window, bf16[4,256,128]{2,1,0:T(8,128)(2,1)S(1)} %get-tuple-element.28.far_u, ...), custom_call_target="tpu_custom_call" | custom-call | flops 1073741824 | bytes 1048576 | tf_op jit(solution)/shard_map/pallas_call | solution.py:205
  45.7 0.1 slice_bitcast_fusion
  45.8 0.1 collective-permute-start.20
  45.9 0.5 collective-permute-start.19
  46.4 1.0 %collective-permute-done.20 = f32[256,256]{1,0:T(8,128)S(1)} collective-permute-done((f32[256,256]{1,0:T(8,128)S(1)}, f32[256,256]{1,0:T(8,128)S(1)}, u32[]{:S(2)}, u32[]{:S(2)}) %collective-permute-start.20) | collective-permute-done | bytes 262176 | tf_op jit(solution)/shard_map/ppermute | solution.py:20
  47.4 1.9 %collective-permute-start.21 = (bf16[256,256]{1,0:T(8,128)(2,1)S(1)}, bf16[256,256]{1,0:T(8,128)(2,1)S(1)}, u32[]{:S(2)}, u32[]{:S(2)}) collective-permute-start(bf16[256,256]{1,0:T(8,128)(2,1)S(1)} %fusion.2), channel_id=1, source_target_pairs={{0,2},{1,3},{2,0},{3,1},{4,6},{5,7},{6,4},{7,5},{8,10},{9,11},{10,... | collective-permute-start | bytes 393224 | tf_op jit(solution)/shard_map/ppermute | solution.py:26
  49.3 0.2 multiply_add_fusion.1
  49.5 0.0 collective-permute-done.19.mate
  49.5 3.6 %collective-permute-done.21 = bf16[256,256]{1,0:T(8,128)(2,1)S(1)} collective-permute-done((bf16[256,256]{1,0:T(8,128)(2,1)S(1)}, bf16[256,256]{1,0:T(8,128)(2,1)S(1)}, u32[]{:S(2)}, u32[]{:S(2)}) %collective-permute-start.21) | collective-permute-done | bytes 131104 | tf_op jit(solution)/shard_map/ppermute | solution.py:26
  53.1 0.1 broadcast_in_dim.5.scale
  53.2 0.9 %shard_map.108 = (f32[256,256]{1,0:T(8,128)}, f32[256,256]{1,0:T(8,128)}) custom-call(f32[256,256]{1,0:T(8,128)S(1)} %get-tuple-element.38.near, f32[256,256]{1,0:T(8,128)S(1)} %collective-permute-done.19.mate, bf16[1,256,256]{2,1,0:T(8,128)(2,1)S(1)} %bitcast.44, f32[256,256]{1,0:T(8,128)S(1)} %broadcast_in_dim.5.scale, ...), custom_call_target="tpu_custom_call" | custom-call | flops 1048576 | bytes 2097152 | tf_op jit(solution)/shard_map/pallas_call | solution.py:280
  (29 shorter events, 0.4 us)
Async XLA Ops:
  1.6 9.6 %collective-permute-start = (bf16[256,256]{1,0:T(8,128)(2,1)S(1)}, bf16[256,256]{1,0:T(8,128)(2,1)S(1)}, u32[]{:S(2)}, u32[]{:S(2)}) collective-permute-start(bf16[256,256]{1,0:T(8,128)(2,1)S(1)} %get-tuple-element.35.rest_0_), channel_id=1, source_target_pairs={{0,12},{1,13},{2,6},{3,7},{4,0},{5,1},{6,10},{7,11},{8,4},{9,5},{1... | collective-permute-start | bytes 393224 | tf_op jit(solution)/shard_map/ppermute | solution.py:41
  6.7 8.9 %collective-permute-start.2 = (bf16[256,256]{1,0:T(8,128)(2,1)S(1)}, bf16[256,256]{1,0:T(8,128)(2,1)S(1)}, u32[]{:S(2)}, u32[]{:S(2)}) collective-permute-start(bf16[256,256]{1,0:T(8,128)(2,1)S(1)} %get-tuple-element.35.rest_0_), channel_id=1, source_target_pairs={{0,2},{1,3},{2,0},{3,1},{4,6},{5,7},{6,4},{7,5},{8,10},{9,11},{10,... | collective-permute-start | bytes 393224 | tf_op jit(solution)/shard_map/ppermute | solution.py:26
  6.7 10.3 %collective-permute-start.3 = (bf16[256,256]{1,0:T(8,128)(2,1)S(1)}, bf16[256,256]{1,0:T(8,128)(2,1)S(1)}, u32[]{:S(2)}, u32[]{:S(2)}) collective-permute-start(bf16[256,256]{1,0:T(8,128)(2,1)S(1)} %get-tuple-element.35.rest_0_), channel_id=1, source_target_pairs={{0,1},{1,0},{2,3},{3,2},{4,5},{5,4},{6,7},{7,6},{8,9},{9,8},{10,11... | collective-permute-start | bytes 393224 | tf_op jit(solution)/shard_map/ppermute | solution.py:20
  6.7 11.8 %collective-permute-start.6 = (bf16[256,256]{1,0:T(8,128)(2,1)S(1)}, bf16[256,256]{1,0:T(8,128)(2,1)S(1)}, u32[]{:S(2)}, u32[]{:S(2)}) collective-permute-start(bf16[256,256]{1,0:T(8,128)(2,1)S(1)} %get-tuple-element.35.rest_0_), channel_id=1, source_target_pairs={{0,4},{1,5},{2,14},{3,15},{4,8},{5,9},{6,2},{7,3},{8,12},{9,13},{1... | collective-permute-start | bytes 393224 | tf_op jit(solution)/shard_map/ppermute | solution.py:41
  7.8 0.7 %copy-start.4 = (s32[112,2]{0,1:T(2,128)S(1)}, s32[112,2]{0,1:T(2,128)}, u32[]{:S(2)}) copy-start(s32[112,2]{0,1:T(2,128)} %param.14) | copy-start | bytes 2692
  8.4 6.4 %copy-start.1 = (bf16[4,4,32,256]{3,2,1,0:T(8,128)(2,1)S(1)}, bf16[4,4,32,256]{3,2,1,0:T(8,128)(2,1)}, u32[]{:S(2)}) copy-start(bf16[4,4,32,256]{3,2,1,0:T(8,128)(2,1)} %far_u) | copy-start | bytes 786436
  8.4 6.4 %copy-start.2 = (bf16[4,4,32,256]{3,2,1,0:T(8,128)(2,1)S(1)}, bf16[4,4,32,256]{3,2,1,0:T(8,128)(2,1)}, u32[]{:S(2)}) copy-start(bf16[4,4,32,256]{3,2,1,0:T(8,128)(2,1)} %far_v) | copy-start | bytes 786436
  8.4 6.4 %copy-start.3 = (s32[4,4]{1,0:T(4,128)S(1)}, s32[4,4]{1,0:T(4,128)}, u32[]{:S(2)}) copy-start(s32[4,4]{1,0:T(4,128)} %ranks) | copy-start | bytes 196
  8.4 10.1 %copy-start = (bf16[112,128,128]{2,1,0:T(8,128)(2,1)S(1)}, bf16[112,128,128]{2,1,0:T(8,128)(2,1)}, u32[]{:S(2)}) copy-start(bf16[112,128,128]{2,1,0:T(8,128)(2,1)} %blocks.3) | copy-start | bytes 11010052
  11.2 5.7 %collective-permute-start.1 = (bf16[256,256]{1,0:T(8,128)(2,1)S(1)}, bf16[256,256]{1,0:T(8,128)(2,1)S(1)}, u32[]{:S(2)}, u32[]{:S(2)}) collective-permute-start(bf16[256,256]{1,0:T(8,128)(2,1)S(1)} %collective-permute-done.rest_1_), channel_id=1, source_target_pairs={{0,2},{1,3},{2,0},{3,1},{4,6},{5,7},{6,4},{7,5},{8,10},{9,11},{10,... | collective-permute-start | bytes 393224 | tf_op jit(solution)/shard_map/ppermute | solution.py:26
  12.7 5.9 %collective-permute-start.7 = (bf16[256,256]{1,0:T(8,128)(2,1)S(1)}, bf16[256,256]{1,0:T(8,128)(2,1)S(1)}, u32[]{:S(2)}, u32[]{:S(2)}) collective-permute-start(bf16[256,256]{1,0:T(8,128)(2,1)S(1)} %collective-permute-done.rest_1_), channel_id=1, source_target_pairs={{0,12},{1,13},{2,6},{3,7},{4,0},{5,1},{6,10},{7,11},{8,4},{9,5},{1... | collective-permute-start | bytes 393224 | tf_op jit(solution)/shard_map/ppermute | solution.py:41
  15.6 1.4 %collective-permute-start.4 = (bf16[256,256]{1,0:T(8,128)(2,1)S(1)}, bf16[256,256]{1,0:T(8,128)(2,1)S(1)}, u32[]{:S(2)}, u32[]{:S(2)}) collective-permute-start(bf16[256,256]{1,0:T(8,128)(2,1)S(1)} %collective-permute-done.2), channel_id=1, source_target_pairs={{0,1},{1,0},{2,3},{3,2},{4,5},{5,4},{6,7},{7,6},{8,9},{9,8},{10,11... | collective-permute-start | bytes 393224 | tf_op jit(solution)/shard_map/ppermute | solution.py:20
  16.9 1.6 %collective-permute-start.5 = (bf16[512,256]{1,0:T(8,128)(2,1)S(1)}, bf16[512,256]{1,0:T(8,128)(2,1)S(1)}, u32[]{:S(2)}, u32[]{:S(2)}) collective-permute-start(bf16[512,256]{1,0:T(8,128)(2,1)S(1)} %pad_maximum_fusion), channel_id=1, source_target_pairs={{0,1},{1,0},{2,3},{3,2},{4,5},{5,4},{6,7},{7,6},{8,9},{9,8},{10,11... | collective-permute-start | bytes 786440 | tf_op jit(solution)/shard_map/ppermute | solution.py:20
  20.9 3.7 %copy-start.8 = (f32[256]{0:T(256)S(1)}, f32[256]{0:T(256)}, u32[]{:S(2)}) copy-start(f32[256]{0:T(256)} %param.12) | copy-start | bytes 3076
  20.9 7.4 %copy-start.6 = (f32[256,256]{1,0:T(8,128)S(1)}, f32[256,256]{1,0:T(8,128)}, u32[]{:S(2)}) copy-start(f32[256,256]{1,0:T(8,128)} %param.10) | copy-start | bytes 786436
  20.9 7.4 %copy-start.7 = (f32[256,256]{1,0:T(8,128)S(1)}, f32[256,256]{1,0:T(8,128)}, u32[]{:S(2)}) copy-start(f32[256,256]{1,0:T(8,128)} %param.11) | copy-start | bytes 786436
  21.0 1.6 %collective-permute-start.9 = (f32[256,256]{1,0:T(8,128)S(1)}, f32[256,256]{1,0:T(8,128)S(1)}, u32[]{:S(2)}, u32[]{:S(2)}) collective-permute-start(f32[256,256]{1,0:T(8,128)S(1)} %get-tuple-element.40), channel_id=1, source_target_pairs={{0,1},{1,0},{2,3},{3,2},{4,5},{5,4},{6,7},{7,6},{8,9},{9,8},{10,11... | collective-permute-start | bytes 786440 | tf_op jit(solution)/shard_map/ppermute | solution.py:20
  21.2 3.4 %collective-permute-start.8 = (f32[256,256]{1,0:T(8,128)S(1)}, f32[256,256]{1,0:T(8,128)S(1)}, u32[]{:S(2)}, u32[]{:S(2)}) collective-permute-start(f32[256,256]{1,0:T(8,128)S(1)} %get-tuple-element.39), channel_id=1, source_target_pairs={{0,1},{1,0},{2,3},{3,2},{4,5},{5,4},{6,7},{7,6},{8,9},{9,8},{10,11... | collective-permute-start | bytes 786440 | tf_op jit(solution)/shard_map/ppermute | solution.py:20
  22.6 6.1 %copy-start.5 = (f32[256,256]{1,0:T(8,128)S(1)}, f32[256,256]{1,0:T(8,128)}, u32[]{:S(2)}) copy-start(f32[256,256]{1,0:T(8,128)} %param.9) | copy-start | bytes 786436
  22.6 5.7 %collective-permute-start.10 = (bf16[256,256]{1,0:T(8,128)(2,1)S(1)}, bf16[256,256]{1,0:T(8,128)(2,1)S(1)}, u32[]{:S(2)}, u32[]{:S(2)}) collective-permute-start(bf16[256,256]{1,0:T(8,128)(2,1)S(1)} %fusion.4), channel_id=1, source_target_pairs={{0,2},{1,3},{2,0},{3,1},{4,6},{5,7},{6,4},{7,5},{8,10},{9,11},{10,... | collective-permute-start | bytes 393224 | tf_op jit(solution)/shard_map/ppermute | solution.py:26
  28.8 6.7 %collective-permute-start.11 = (bf16[256,256]{1,0:T(8,128)(2,1)S(1)}, bf16[256,256]{1,0:T(8,128)(2,1)S(1)}, u32[]{:S(2)}, u32[]{:S(2)}) collective-permute-start(bf16[256,256]{1,0:T(8,128)(2,1)S(1)} %get-tuple-element.33.rest_0_), channel_id=1, source_target_pairs={{0,12},{1,13},{2,6},{3,7},{4,0},{5,1},{6,10},{7,11},{8,4},{9,5},{1... | collective-permute-start | bytes 393224 | tf_op jit(solution)/shard_map/ppermute | solution.py:41
  31.8 8.1 %collective-permute-start.13 = (bf16[256,256]{1,0:T(8,128)(2,1)S(1)}, bf16[256,256]{1,0:T(8,128)(2,1)S(1)}, u32[]{:S(2)}, u32[]{:S(2)}) collective-permute-start(bf16[256,256]{1,0:T(8,128)(2,1)S(1)} %get-tuple-element.33.rest_0_), channel_id=1, source_target_pairs={{0,2},{1,3},{2,0},{3,1},{4,6},{5,7},{6,4},{7,5},{8,10},{9,11},{10,... | collective-permute-start | bytes 393224 | tf_op jit(solution)/shard_map/ppermute | solution.py:26
  31.8 9.7 %collective-permute-start.14 = (bf16[256,256]{1,0:T(8,128)(2,1)S(1)}, bf16[256,256]{1,0:T(8,128)(2,1)S(1)}, u32[]{:S(2)}, u32[]{:S(2)}) collective-permute-start(bf16[256,256]{1,0:T(8,128)(2,1)S(1)} %get-tuple-element.33.rest_0_), channel_id=1, source_target_pairs={{0,1},{1,0},{2,3},{3,2},{4,5},{5,4},{6,7},{7,6},{8,9},{9,8},{10,11... | collective-permute-start | bytes 393224 | tf_op jit(solution)/shard_map/ppermute | solution.py:20
  31.8 11.3 %collective-permute-start.17 = (bf16[256,256]{1,0:T(8,128)(2,1)S(1)}, bf16[256,256]{1,0:T(8,128)(2,1)S(1)}, u32[]{:S(2)}, u32[]{:S(2)}) collective-permute-start(bf16[256,256]{1,0:T(8,128)(2,1)S(1)} %get-tuple-element.33.rest_0_), channel_id=1, source_target_pairs={{0,4},{1,5},{2,14},{3,15},{4,8},{5,9},{6,2},{7,3},{8,12},{9,13},{1... | collective-permute-start | bytes 393224 | tf_op jit(solution)/shard_map/ppermute | solution.py:41
  35.5 5.9 %collective-permute-start.12 = (bf16[256,256]{1,0:T(8,128)(2,1)S(1)}, bf16[256,256]{1,0:T(8,128)(2,1)S(1)}, u32[]{:S(2)}, u32[]{:S(2)}) collective-permute-start(bf16[256,256]{1,0:T(8,128)(2,1)S(1)} %collective-permute-done.11.rest_1_), channel_id=1, source_target_pairs={{0,2},{1,3},{2,0},{3,1},{4,6},{5,7},{6,4},{7,5},{8,10},{9,11},{10,... | collective-permute-start | bytes 393224 | tf_op jit(solution)/shard_map/ppermute | solution.py:26
  38.4 5.0 %collective-permute-start.18 = (bf16[256,256]{1,0:T(8,128)(2,1)S(1)}, bf16[256,256]{1,0:T(8,128)(2,1)S(1)}, u32[]{:S(2)}, u32[]{:S(2)}) collective-permute-start(bf16[256,256]{1,0:T(8,128)(2,1)S(1)} %collective-permute-done.11.rest_1_), channel_id=1, source_target_pairs={{0,12},{1,13},{2,6},{3,7},{4,0},{5,1},{6,10},{7,11},{8,4},{9,5},{1... | collective-permute-start | bytes 393224 | tf_op jit(solution)/shard_map/ppermute | solution.py:41
  39.9 1.7 %collective-permute-start.15 = (bf16[256,256]{1,0:T(8,128)(2,1)S(1)}, bf16[256,256]{1,0:T(8,128)(2,1)S(1)}, u32[]{:S(2)}, u32[]{:S(2)}) collective-permute-start(bf16[256,256]{1,0:T(8,128)(2,1)S(1)} %collective-permute-done.13), channel_id=1, source_target_pairs={{0,1},{1,0},{2,3},{3,2},{4,5},{5,4},{6,7},{7,6},{8,9},{9,8},{10,11... | collective-permute-start | bytes 393224 | tf_op jit(solution)/shard_map/ppermute | solution.py:20
  41.4 1.6 %collective-permute-start.16 = (bf16[512,256]{1,0:T(8,128)(2,1)S(1)}, bf16[512,256]{1,0:T(8,128)(2,1)S(1)}, u32[]{:S(2)}, u32[]{:S(2)}) collective-permute-start(bf16[512,256]{1,0:T(8,128)(2,1)S(1)} %pad_maximum_fusion.1), channel_id=1, source_target_pairs={{0,1},{1,0},{2,3},{3,2},{4,5},{5,4},{6,7},{7,6},{8,9},{9,8},{10,11... | collective-permute-start | bytes 786440 | tf_op jit(solution)/shard_map/ppermute | solution.py:20
  45.8 1.6 %collective-permute-start.20 = (f32[256,256]{1,0:T(8,128)S(1)}, f32[256,256]{1,0:T(8,128)S(1)}, u32[]{:S(2)}, u32[]{:S(2)}) collective-permute-start(f32[256,256]{1,0:T(8,128)S(1)} %get-tuple-element.36), channel_id=1, source_target_pairs={{0,1},{1,0},{2,3},{3,2},{4,5},{5,4},{6,7},{7,6},{8,9},{9,8},{10,11... | collective-permute-start | bytes 786440 | tf_op jit(solution)/shard_map/ppermute | solution.py:20
  45.9 3.6 %collective-permute-start.19 = (f32[256,256]{1,0:T(8,128)S(1)}, f32[256,256]{1,0:T(8,128)S(1)}, u32[]{:S(2)}, u32[]{:S(2)}) collective-permute-start(f32[256,256]{1,0:T(8,128)S(1)} %get-tuple-element.37), channel_id=1, source_target_pairs={{0,1},{1,0},{2,3},{3,2},{4,5},{5,4},{6,7},{7,6},{8,9},{9,8},{10,11... | collective-permute-start | bytes 786440 | tf_op jit(solution)/shard_map/ppermute | solution.py:20
  47.4 5.7 %collective-permute-start.21 = (bf16[256,256]{1,0:T(8,128)(2,1)S(1)}, bf16[256,256]{1,0:T(8,128)(2,1)S(1)}, u32[]{:S(2)}, u32[]{:S(2)}) collective-permute-start(bf16[256,256]{1,0:T(8,128)(2,1)S(1)} %fusion.2), channel_id=1, source_target_pairs={{0,2},{1,3},{2,0},{3,1},{4,6},{5,7},{6,4},{7,5},{8,10},{9,11},{10,... | collective-permute-start | bytes 393224 | tf_op jit(solution)/shard_map/ppermute | solution.py:26

commit v7 on v6

--- a/solution.py
+++ b/solution.py
@@ -210,7 +210,7 @@
         compiler_params=PARAMS,
         cost_estimate=pl.CostEstimate(
             flops=2 * members * (count * leaf * leaf + 2 * targets * ranks * elems),
-            bytes_accessed=4 * targets * elems * members,
+            bytes_accessed=2 * count * leaf * leaf + 4 * targets * elems * members,
             transcendentals=0,
         ),
     )(plan, blocks, window, far_u, far_v, *columns)

time: 54.3 us -> 54.3 us (level)
  no operation moved by 1% of the time
where the time goes in v7:
time: 54.3 us; the launch traced here: 54.1 us
  starting transfers between devices  22.4 us (41%)
  waiting for transfers between devices  19 us (35%)
  Pallas kernels  9 us (17%)
  other arithmetic  1.66 us (3%)
  local copies, waits for them, and re-layouts  1.06 us (2%)
  between operations  1 us (2%)
    ppermute x6, starting transfers between devices, end_shift(): return lax.ppermute(array, ('clu', 'row'), pairs)  12.8 us
    ppermute x6, waiting for transfers between devices, chip_shift(): return lax.ppermute(array, 'row', pairs)  10 us
    ppermute x6, starting transfers between devices, chip_shift(): return lax.ppermute(array, 'row', pairs)  8.25 us
    ppermute x10, waiting for transfers between devices, core_swap(): return lax.ppermute(array, 'row', [(i, i ^ 1) for i in range(devices)])  4.95 us
    pallas_call x2, Pallas kernels, partial_stress(): pl.pallas_call(functools.partial(stress_kernel, leaf), out_shape=jax.Shap...  4.62 us
    ppermute x6, waiting for transfers between devices, end_shift(): return lax.ppermute(array, ('clu', 'row'), pairs)  4.03 us
    pallas_call x1, Pallas kernels, planned_blocks(): pl.pallas_call(functools.partial(plan_kernel, leaf, own), out_shape=jax.S...  2.71 us
    ppermute x10, starting transfers between devices, core_swap(): return lax.ppermute(array, 'row', [(i, i ^ 1) for i in range(devices)])  1.36 us
  transfers between devices with their start and end apart: 22, of which 10 were waited for; matrix products, arithmetic and copies ran while one was open for 1% of the time, Pallas kernels for 6%

profile of v7, /device:TPU:0, one launch (start us, length us, event | category | flops | bytes accessed | tf_op | source)
XLA Modules:
  0.0 54.1 jit_solution(16178899045817182479)
XLA Ops:
  0.6 1.0 %constant_dynamic-update-slice_fusion.7 = (bf16[2176,256]{1,0:T(8,128)(2,1)S(1)}, bf16[256,256]{1,0:T(8,128)(2,1)S(1)}) fusion(f32[256,256]{1,0:T(8,128)} %param.9), kind=kLoop, calls=%fused_computation.34 | loop fusion | flops 65535 | bytes 524288
  1.6 5.1 %collective-permute-start = (bf16[256,256]{1,0:T(8,128)(2,1)S(1)}, bf16[256,256]{1,0:T(8,128)(2,1)S(1)}, u32[]{:S(2)}, u32[]{:S(2)}) collective-permute-start(bf16[256,256]{1,0:T(8,128)(2,1)S(1)} %get-tuple-element.35.rest_0_), channel_id=1, source_target_pairs={{0,12},{1,13},{2,6},{3,7},{4,0},{5,1},{6,10},{7,11},{8,4},{9,5},{1... | collective-permute-start | bytes 393224 | tf_op jit(solution)/shard_map/ppermute | solution.py:41
  6.7 0.0 collective-permute-start.2
  6.7 0.0 collective-permute-start.3
  6.7 1.0 %collective-permute-start.6 = (bf16[256,256]{1,0:T(8,128)(2,1)S(1)}, bf16[256,256]{1,0:T(8,128)(2,1)S(1)}, u32[]{:S(2)}, u32[]{:S(2)}) collective-permute-start(bf16[256,256]{1,0:T(8,128)(2,1)S(1)} %get-tuple-element.35.rest_0_), channel_id=1, source_target_pairs={{0,4},{1,5},{2,14},{3,15},{4,8},{5,9},{6,2},{7,3},{8,12},{9,13},{1... | collective-permute-start | bytes 393224 | tf_op jit(solution)/shard_map/ppermute | solution.py:41
  7.8 0.7 %copy-done.4 = s32[112,2]{0,1:T(2,128)S(1)} copy-done((s32[112,2]{0,1:T(2,128)S(1)}, s32[112,2]{0,1:T(2,128)}, u32[]{:S(2)}) %copy-start.4) | copy-done | bytes 920
  8.4 2.7 %shard_map.104.plan = s32[3,136]{1,0:T(4,128)S(1)} custom-call(s32[2,112]{1,0:T(2,128)S(1)} %bitcast.45), custom_call_target="tpu_custom_call" | custom-call | flops 4000000000 | bytes 10000000 | tf_op jit(solution)/shard_map/pallas_call | solution.py:171
  11.2 0.0 collective-permute-done.rest_1_
  11.2 1.5 %collective-permute-start.1 = (bf16[256,256]{1,0:T(8,128)(2,1)S(1)}, bf16[256,256]{1,0:T(8,128)(2,1)S(1)}, u32[]{:S(2)}, u32[]{:S(2)}) collective-permute-start(bf16[256,256]{1,0:T(8,128)(2,1)S(1)} %collective-permute-done.rest_1_), channel_id=1, source_target_pairs={{0,2},{1,3},{2,0},{3,1},{4,6},{5,7},{6,4},{7,5},{8,10},{9,11},{10,... | collective-permute-start | bytes 393224 | tf_op jit(solution)/shard_map/ppermute | solution.py:26
  12.7 2.2 %collective-permute-start.7 = (bf16[256,256]{1,0:T(8,128)(2,1)S(1)}, bf16[256,256]{1,0:T(8,128)(2,1)S(1)}, u32[]{:S(2)}, u32[]{:S(2)}) collective-permute-start(bf16[256,256]{1,0:T(8,128)(2,1)S(1)} %collective-permute-done.rest_1_), channel_id=1, source_target_pairs={{0,12},{1,13},{2,6},{3,7},{4,0},{5,1},{6,10},{7,11},{8,4},{9,5},{1... | collective-permute-start | bytes 393224 | tf_op jit(solution)/shard_map/ppermute | solution.py:41
  14.8 0.0 copy-done.1
  14.8 0.0 copy-done.2
  14.8 0.0 copy-done.3
  14.8 0.7 %shard_map.105 = (bf16[4,256,128]{2,1,0:T(8,128)(2,1)S(1)}, bf16[4,128,256]{2,1,0:T(8,128)(2,1)S(1)}) custom-call(s32[4,4]{1,0:T(4,128)S(1)} %copy-done.3, bf16[4,4,32,256]{3,2,1,0:T(8,128)(2,1)S(1)} %copy-done.1, bf16[4,4,32,256]{3,2,1,0:T(8,128)(2,1)S(1)} %copy-done.2), custom_call_target="tpu_custom_call" | custom-call | flops 1024 | bytes 1000000 | tf_op jit(solution)/shard_map/pallas_call | solution.py:188
  15.6 0.0 collective-permute-done.2
  15.6 0.1 collective-permute-start.4
  15.7 1.2 %collective-permute-done.1 = bf16[256,256]{1,0:T(8,128)(2,1)S(1)} collective-permute-done((bf16[256,256]{1,0:T(8,128)(2,1)S(1)}, bf16[256,256]{1,0:T(8,128)(2,1)S(1)}, u32[]{:S(2)}, u32[]{:S(2)}) %collective-permute-start.1) | collective-permute-done | bytes 131104 | tf_op jit(solution)/shard_map/ppermute | solution.py:26
  16.9 0.1 collective-permute-start.5
  17.0 0.0 collective-permute-done.3
  17.0 0.0 collective-permute-done.4
  17.0 1.4 %collective-permute-done.5 = bf16[512,256]{1,0:T(8,128)(2,1)S(1)} collective-permute-done((bf16[512,256]{1,0:T(8,128)(2,1)S(1)}, bf16[512,256]{1,0:T(8,128)(2,1)S(1)}, u32[]{:S(2)}, u32[]{:S(2)}) %collective-permute-start.5) | collective-permute-done | bytes 262176 | tf_op jit(solution)/shard_map/ppermute | solution.py:20
  18.5 0.0 collective-permute-done.6.rest_2_
  18.5 0.0 collective-permute-done.7.rest_3_
  18.5 0.0 copy-done
  18.6 2.3 %shard_map.106 = f32[1024,256]{1,0:T(8,128)S(1)} custom-call(s32[3,136]{1,0:T(4,128)S(1)} %shard_map.104.plan, bf16[112,128,128]{2,1,0:T(8,128)(2,1)S(1)} %copy-done, bf16[2176,256]{1,0:T(8,128)(2,1)S(1)} %constant_dynamic-update-slice_fusion.window, bf16[4,256,128]{2,1,0:T(8,128)(2,1)S(1)} %get-tuple-element.28.far_u, ...), custom_call_target="tpu_custom_call" | custom-call | flops 1073741824 | bytes 4718592 | tf_op jit(solution)/shard_map/pallas_call | solution.py:205
  20.9 0.0 copy-start.8
  20.9 0.0 copy-start.6
  20.9 0.0 copy-start.7
  21.0 0.2 collective-permute-start.9
  21.2 0.4 collective-permute-start.8
  21.5 1.0 %collective-permute-done.9 = f32[256,256]{1,0:T(8,128)S(1)} collective-permute-done((f32[256,256]{1,0:T(8,128)S(1)}, f32[256,256]{1,0:T(8,128)S(1)}, u32[]{:S(2)}, u32[]{:S(2)}) %collective-permute-start.9) | collective-permute-done | bytes 262176 | tf_op jit(solution)/shard_map/ppermute | solution.py:20
  22.6 0.0 copy-start.5
  22.6 1.9 %collective-permute-start.10 = (bf16[256,256]{1,0:T(8,128)(2,1)S(1)}, bf16[256,256]{1,0:T(8,128)(2,1)S(1)}, u32[]{:S(2)}, u32[]{:S(2)}) collective-permute-start(bf16[256,256]{1,0:T(8,128)(2,1)S(1)} %fusion.4), channel_id=1, source_target_pairs={{0,2},{1,3},{2,0},{3,1},{4,6},{5,7},{6,4},{7,5},{8,10},{9,11},{10,... | collective-permute-start | bytes 393224 | tf_op jit(solution)/shard_map/ppermute | solution.py:26
  24.5 0.0 collective-permute-done.8
  24.5 3.8 %collective-permute-done.10 = bf16[256,256]{1,0:T(8,128)(2,1)S(1)} collective-permute-done((bf16[256,256]{1,0:T(8,128)(2,1)S(1)}, bf16[256,256]{1,0:T(8,128)(2,1)S(1)}, u32[]{:S(2)}, u32[]{:S(2)}) %collective-permute-start.10) | collective-permute-done | bytes 131104 | tf_op jit(solution)/shard_map/ppermute | solution.py:26
  28.3 0.0 copy-done.7
  28.3 0.4 multiply_add_fusion
  28.8 3.0 %collective-permute-start.11 = (bf16[256,256]{1,0:T(8,128)(2,1)S(1)}, bf16[256,256]{1,0:T(8,128)(2,1)S(1)}, u32[]{:S(2)}, u32[]{:S(2)}) collective-permute-start(bf16[256,256]{1,0:T(8,128)(2,1)S(1)} %get-tuple-element.33.rest_0_), channel_id=1, source_target_pairs={{0,12},{1,13},{2,6},{3,7},{4,0},{5,1},{6,10},{7,11},{8,4},{9,5},{1... | collective-permute-start | bytes 393224 | tf_op jit(solution)/shard_map/ppermute | solution.py:41
  31.8 0.0 collective-permute-start.13
  31.8 0.0 collective-permute-start.14
  31.8 0.0 collective-permute-start.17
  31.8 3.7 %collective-permute-done.11.rest_1_ = bf16[256,256]{1,0:T(8,128)(2,1)S(1)} collective-permute-done((bf16[256,256]{1,0:T(8,128)(2,1)S(1)}, bf16[256,256]{1,0:T(8,128)(2,1)S(1)}, u32[]{:S(2)}, u32[]{:S(2)}) %collective-permute-start.11) | collective-permute-done | bytes 131104 | tf_op jit(solution)/shard_map/ppermute | solution.py:41
  35.5 3.0 %collective-permute-start.12 = (bf16[256,256]{1,0:T(8,128)(2,1)S(1)}, bf16[256,256]{1,0:T(8,128)(2,1)S(1)}, u32[]{:S(2)}, u32[]{:S(2)}) collective-permute-start(bf16[256,256]{1,0:T(8,128)(2,1)S(1)} %collective-permute-done.11.rest_1_), channel_id=1, source_target_pairs={{0,2},{1,3},{2,0},{3,1},{4,6},{5,7},{6,4},{7,5},{8,10},{9,11},{10,... | collective-permute-start | bytes 393224 | tf_op jit(solution)/shard_map/ppermute | solution.py:26
  38.4 1.4 %collective-permute-start.18 = (bf16[256,256]{1,0:T(8,128)(2,1)S(1)}, bf16[256,256]{1,0:T(8,128)(2,1)S(1)}, u32[]{:S(2)}, u32[]{:S(2)}) collective-permute-start(bf16[256,256]{1,0:T(8,128)(2,1)S(1)} %collective-permute-done.11.rest_1_), channel_id=1, source_target_pairs={{0,12},{1,13},{2,6},{3,7},{4,0},{5,1},{6,10},{7,11},{8,4},{9,5},{1... | collective-permute-start | bytes 393224 | tf_op jit(solution)/shard_map/ppermute | solution.py:41
  39.9 0.0 collective-permute-done.13
  39.9 0.0 collective-permute-start.15
  39.9 1.5 %collective-permute-done.12 = bf16[256,256]{1,0:T(8,128)(2,1)S(1)} collective-permute-done((bf16[256,256]{1,0:T(8,128)(2,1)S(1)}, bf16[256,256]{1,0:T(8,128)(2,1)S(1)}, u32[]{:S(2)}, u32[]{:S(2)}) %collective-permute-start.12) | collective-permute-done | bytes 131104 | tf_op jit(solution)/shard_map/ppermute | solution.py:26
  41.4 0.1 collective-permute-start.16
  41.5 0.0 collective-permute-done.14
  41.5 0.0 collective-permute-done.15
  41.6 1.4 %collective-permute-done.16 = bf16[512,256]{1,0:T(8,128)(2,1)S(1)} collective-permute-done((bf16[512,256]{1,0:T(8,128)(2,1)S(1)}, bf16[512,256]{1,0:T(8,128)(2,1)S(1)}, u32[]{:S(2)}, u32[]{:S(2)}) %collective-permute-start.16) | collective-permute-done | bytes 262176 | tf_op jit(solution)/shard_map/ppermute | solution.py:20
  43.0 0.0 collective-permute-done.17.rest_2_
  43.1 0.4 collective-permute-done.18.rest_3_
  43.4 2.3 %shard_map.107 = f32[1024,256]{1,0:T(8,128)S(1)} custom-call(s32[3,136]{1,0:T(4,128)S(1)} %shard_map.104.plan, bf16[112,128,128]{2,1,0:T(8,128)(2,1)S(1)} %copy-done, bf16[2176,256]{1,0:T(8,128)(2,1)S(1)} %constant_dynamic-update-slice_fusion.8.window, bf16[4,256,128]{2,1,0:T(8,128)(2,1)S(1)} %get-tuple-element.28.far_u, ...), custom_call_target="tpu_custom_call" | custom-call | flops 1073741824 | bytes 4718592 | tf_op jit(solution)/shard_map/pallas_call | solution.py:205
  45.7 0.1 slice_bitcast_fusion
  45.8 0.1 collective-permute-start.20
  45.9 0.5 collective-permute-start.19
  46.4 1.0 %collective-permute-done.20 = f32[256,256]{1,0:T(8,128)S(1)} collective-permute-done((f32[256,256]{1,0:T(8,128)S(1)}, f32[256,256]{1,0:T(8,128)S(1)}, u32[]{:S(2)}, u32[]{:S(2)}) %collective-permute-start.20) | collective-permute-done | bytes 262176 | tf_op jit(solution)/shard_map/ppermute | solution.py:20
  47.4 1.9 %collective-permute-start.21 = (bf16[256,256]{1,0:T(8,128)(2,1)S(1)}, bf16[256,256]{1,0:T(8,128)(2,1)S(1)}, u32[]{:S(2)}, u32[]{:S(2)}) collective-permute-start(bf16[256,256]{1,0:T(8,128)(2,1)S(1)} %fusion.2), channel_id=1, source_target_pairs={{0,2},{1,3},{2,0},{3,1},{4,6},{5,7},{6,4},{7,5},{8,10},{9,11},{10,... | collective-permute-start | bytes 393224 | tf_op jit(solution)/shard_map/ppermute | solution.py:26
  49.3 0.2 multiply_add_fusion.1
  49.5 0.0 collective-permute-done.19.mate
  49.5 3.6 %collective-permute-done.21 = bf16[256,256]{1,0:T(8,128)(2,1)S(1)} collective-permute-done((bf16[256,256]{1,0:T(8,128)(2,1)S(1)}, bf16[256,256]{1,0:T(8,128)(2,1)S(1)}, u32[]{:S(2)}, u32[]{:S(2)}) %collective-permute-start.21) | collective-permute-done | bytes 131104 | tf_op jit(solution)/shard_map/ppermute | solution.py:26
  53.1 0.1 broadcast_in_dim.5.scale
  53.2 0.9 %shard_map.108 = (f32[256,256]{1,0:T(8,128)}, f32[256,256]{1,0:T(8,128)}) custom-call(f32[256,256]{1,0:T(8,128)S(1)} %get-tuple-element.38.near, f32[256,256]{1,0:T(8,128)S(1)} %collective-permute-done.19.mate, bf16[1,256,256]{2,1,0:T(8,128)(2,1)S(1)} %bitcast.44, f32[256,256]{1,0:T(8,128)S(1)} %broadcast_in_dim.5.scale, ...), custom_call_target="tpu_custom_call" | custom-call | flops 1048576 | bytes 2097152 | tf_op jit(solution)/shard_map/pallas_call | solution.py:280
  (29 shorter events, 0.4 us)
Async XLA Ops:
  1.6 9.6 %collective-permute-start = (bf16[256,256]{1,0:T(8,128)(2,1)S(1)}, bf16[256,256]{1,0:T(8,128)(2,1)S(1)}, u32[]{:S(2)}, u32[]{:S(2)}) collective-permute-start(bf16[256,256]{1,0:T(8,128)(2,1)S(1)} %get-tuple-element.35.rest_0_), channel_id=1, source_target_pairs={{0,12},{1,13},{2,6},{3,7},{4,0},{5,1},{6,10},{7,11},{8,4},{9,5},{1... | collective-permute-start | bytes 393224 | tf_op jit(solution)/shard_map/ppermute | solution.py:41
  6.7 8.9 %collective-permute-start.2 = (bf16[256,256]{1,0:T(8,128)(2,1)S(1)}, bf16[256,256]{1,0:T(8,128)(2,1)S(1)}, u32[]{:S(2)}, u32[]{:S(2)}) collective-permute-start(bf16[256,256]{1,0:T(8,128)(2,1)S(1)} %get-tuple-element.35.rest_0_), channel_id=1, source_target_pairs={{0,2},{1,3},{2,0},{3,1},{4,6},{5,7},{6,4},{7,5},{8,10},{9,11},{10,... | collective-permute-start | bytes 393224 | tf_op jit(solution)/shard_map/ppermute | solution.py:26
  6.7 10.3 %collective-permute-start.3 = (bf16[256,256]{1,0:T(8,128)(2,1)S(1)}, bf16[256,256]{1,0:T(8,128)(2,1)S(1)}, u32[]{:S(2)}, u32[]{:S(2)}) collective-permute-start(bf16[256,256]{1,0:T(8,128)(2,1)S(1)} %get-tuple-element.35.rest_0_), channel_id=1, source_target_pairs={{0,1},{1,0},{2,3},{3,2},{4,5},{5,4},{6,7},{7,6},{8,9},{9,8},{10,11... | collective-permute-start | bytes 393224 | tf_op jit(solution)/shard_map/ppermute | solution.py:20
  6.7 11.8 %collective-permute-start.6 = (bf16[256,256]{1,0:T(8,128)(2,1)S(1)}, bf16[256,256]{1,0:T(8,128)(2,1)S(1)}, u32[]{:S(2)}, u32[]{:S(2)}) collective-permute-start(bf16[256,256]{1,0:T(8,128)(2,1)S(1)} %get-tuple-element.35.rest_0_), channel_id=1, source_target_pairs={{0,4},{1,5},{2,14},{3,15},{4,8},{5,9},{6,2},{7,3},{8,12},{9,13},{1... | collective-permute-start | bytes 393224 | tf_op jit(solution)/shard_map/ppermute | solution.py:41
  7.8 0.7 %copy-start.4 = (s32[112,2]{0,1:T(2,128)S(1)}, s32[112,2]{0,1:T(2,128)}, u32[]{:S(2)}) copy-start(s32[112,2]{0,1:T(2,128)} %param.14) | copy-start | bytes 2692
  8.4 6.4 %copy-start.1 = (bf16[4,4,32,256]{3,2,1,0:T(8,128)(2,1)S(1)}, bf16[4,4,32,256]{3,2,1,0:T(8,128)(2,1)}, u32[]{:S(2)}) copy-start(bf16[4,4,32,256]{3,2,1,0:T(8,128)(2,1)} %far_u) | copy-start | bytes 786436
  8.4 6.4 %copy-start.2 = (bf16[4,4,32,256]{3,2,1,0:T(8,128)(2,1)S(1)}, bf16[4,4,32,256]{3,2,1,0:T(8,128)(2,1)}, u32[]{:S(2)}) copy-start(bf16[4,4,32,256]{3,2,1,0:T(8,128)(2,1)} %far_v) | copy-start | bytes 786436
  8.4 6.4 %copy-start.3 = (s32[4,4]{1,0:T(4,128)S(1)}, s32[4,4]{1,0:T(4,128)}, u32[]{:S(2)}) copy-start(s32[4,4]{1,0:T(4,128)} %ranks) | copy-start | bytes 196
  8.4 10.1 %copy-start = (bf16[112,128,128]{2,1,0:T(8,128)(2,1)S(1)}, bf16[112,128,128]{2,1,0:T(8,128)(2,1)}, u32[]{:S(2)}) copy-start(bf16[112,128,128]{2,1,0:T(8,128)(2,1)} %blocks.3) | copy-start | bytes 11010052
  11.2 5.7 %collective-permute-start.1 = (bf16[256,256]{1,0:T(8,128)(2,1)S(1)}, bf16[256,256]{1,0:T(8,128)(2,1)S(1)}, u32[]{:S(2)}, u32[]{:S(2)}) collective-permute-start(bf16[256,256]{1,0:T(8,128)(2,1)S(1)} %collective-permute-done.rest_1_), channel_id=1, source_target_pairs={{0,2},{1,3},{2,0},{3,1},{4,6},{5,7},{6,4},{7,5},{8,10},{9,11},{10,... | collective-permute-start | bytes 393224 | tf_op jit(solution)/shard_map/ppermute | solution.py:26
  12.7 5.9 %collective-permute-start.7 = (bf16[256,256]{1,0:T(8,128)(2,1)S(1)}, bf16[256,256]{1,0:T(8,128)(2,1)S(1)}, u32[]{:S(2)}, u32[]{:S(2)}) collective-permute-start(bf16[256,256]{1,0:T(8,128)(2,1)S(1)} %collective-permute-done.rest_1_), channel_id=1, source_target_pairs={{0,12},{1,13},{2,6},{3,7},{4,0},{5,1},{6,10},{7,11},{8,4},{9,5},{1... | collective-permute-start | bytes 393224 | tf_op jit(solution)/shard_map/ppermute | solution.py:41
  15.6 1.4 %collective-permute-start.4 = (bf16[256,256]{1,0:T(8,128)(2,1)S(1)}, bf16[256,256]{1,0:T(8,128)(2,1)S(1)}, u32[]{:S(2)}, u32[]{:S(2)}) collective-permute-start(bf16[256,256]{1,0:T(8,128)(2,1)S(1)} %collective-permute-done.2), channel_id=1, source_target_pairs={{0,1},{1,0},{2,3},{3,2},{4,5},{5,4},{6,7},{7,6},{8,9},{9,8},{10,11... | collective-permute-start | bytes 393224 | tf_op jit(solution)/shard_map/ppermute | solution.py:20
  16.9 1.6 %collective-permute-start.5 = (bf16[512,256]{1,0:T(8,128)(2,1)S(1)}, bf16[512,256]{1,0:T(8,128)(2,1)S(1)}, u32[]{:S(2)}, u32[]{:S(2)}) collective-permute-start(bf16[512,256]{1,0:T(8,128)(2,1)S(1)} %pad_maximum_fusion), channel_id=1, source_target_pairs={{0,1},{1,0},{2,3},{3,2},{4,5},{5,4},{6,7},{7,6},{8,9},{9,8},{10,11... | collective-permute-start | bytes 786440 | tf_op jit(solution)/shard_map/ppermute | solution.py:20
  20.9 3.7 %copy-start.8 = (f32[256]{0:T(256)S(1)}, f32[256]{0:T(256)}, u32[]{:S(2)}) copy-start(f32[256]{0:T(256)} %param.12) | copy-start | bytes 3076
  20.9 7.4 %copy-start.6 = (f32[256,256]{1,0:T(8,128)S(1)}, f32[256,256]{1,0:T(8,128)}, u32[]{:S(2)}) copy-start(f32[256,256]{1,0:T(8,128)} %param.10) | copy-start | bytes 786436
  20.9 7.4 %copy-start.7 = (f32[256,256]{1,0:T(8,128)S(1)}, f32[256,256]{1,0:T(8,128)}, u32[]{:S(2)}) copy-start(f32[256,256]{1,0:T(8,128)} %param.11) | copy-start | bytes 786436
  21.0 1.6 %collective-permute-start.9 = (f32[256,256]{1,0:T(8,128)S(1)}, f32[256,256]{1,0:T(8,128)S(1)}, u32[]{:S(2)}, u32[]{:S(2)}) collective-permute-start(f32[256,256]{1,0:T(8,128)S(1)} %get-tuple-element.40), channel_id=1, source_target_pairs={{0,1},{1,0},{2,3},{3,2},{4,5},{5,4},{6,7},{7,6},{8,9},{9,8},{10,11... | collective-permute-start | bytes 786440 | tf_op jit(solution)/shard_map/ppermute | solution.py:20
  21.2 3.4 %collective-permute-start.8 = (f32[256,256]{1,0:T(8,128)S(1)}, f32[256,256]{1,0:T(8,128)S(1)}, u32[]{:S(2)}, u32[]{:S(2)}) collective-permute-start(f32[256,256]{1,0:T(8,128)S(1)} %get-tuple-element.39), channel_id=1, source_target_pairs={{0,1},{1,0},{2,3},{3,2},{4,5},{5,4},{6,7},{7,6},{8,9},{9,8},{10,11... | collective-permute-start | bytes 786440 | tf_op jit(solution)/shard_map/ppermute | solution.py:20
  22.6 6.1 %copy-start.5 = (f32[256,256]{1,0:T(8,128)S(1)}, f32[256,256]{1,0:T(8,128)}, u32[]{:S(2)}) copy-start(f32[256,256]{1,0:T(8,128)} %param.9) | copy-start | bytes 786436
  22.6 5.7 %collective-permute-start.10 = (bf16[256,256]{1,0:T(8,128)(2,1)S(1)}, bf16[256,256]{1,0:T(8,128)(2,1)S(1)}, u32[]{:S(2)}, u32[]{:S(2)}) collective-permute-start(bf16[256,256]{1,0:T(8,128)(2,1)S(1)} %fusion.4), channel_id=1, source_target_pairs={{0,2},{1,3},{2,0},{3,1},{4,6},{5,7},{6,4},{7,5},{8,10},{9,11},{10,... | collective-permute-start | bytes 393224 | tf_op jit(solution)/shard_map/ppermute | solution.py:26
  28.8 6.7 %collective-permute-start.11 = (bf16[256,256]{1,0:T(8,128)(2,1)S(1)}, bf16[256,256]{1,0:T(8,128)(2,1)S(1)}, u32[]{:S(2)}, u32[]{:S(2)}) collective-permute-start(bf16[256,256]{1,0:T(8,128)(2,1)S(1)} %get-tuple-element.33.rest_0_), channel_id=1, source_target_pairs={{0,12},{1,13},{2,6},{3,7},{4,0},{5,1},{6,10},{7,11},{8,4},{9,5},{1... | collective-permute-start | bytes 393224 | tf_op jit(solution)/shard_map/ppermute | solution.py:41
  31.8 8.1 %collective-permute-start.13 = (bf16[256,256]{1,0:T(8,128)(2,1)S(1)}, bf16[256,256]{1,0:T(8,128)(2,1)S(1)}, u32[]{:S(2)}, u32[]{:S(2)}) collective-permute-start(bf16[256,256]{1,0:T(8,128)(2,1)S(1)} %get-tuple-element.33.rest_0_), channel_id=1, source_target_pairs={{0,2},{1,3},{2,0},{3,1},{4,6},{5,7},{6,4},{7,5},{8,10},{9,11},{10,... | collective-permute-start | bytes 393224 | tf_op jit(solution)/shard_map/ppermute | solution.py:26
  31.8 9.7 %collective-permute-start.14 = (bf16[256,256]{1,0:T(8,128)(2,1)S(1)}, bf16[256,256]{1,0:T(8,128)(2,1)S(1)}, u32[]{:S(2)}, u32[]{:S(2)}) collective-permute-start(bf16[256,256]{1,0:T(8,128)(2,1)S(1)} %get-tuple-element.33.rest_0_), channel_id=1, source_target_pairs={{0,1},{1,0},{2,3},{3,2},{4,5},{5,4},{6,7},{7,6},{8,9},{9,8},{10,11... | collective-permute-start | bytes 393224 | tf_op jit(solution)/shard_map/ppermute | solution.py:20
  31.8 11.3 %collective-permute-start.17 = (bf16[256,256]{1,0:T(8,128)(2,1)S(1)}, bf16[256,256]{1,0:T(8,128)(2,1)S(1)}, u32[]{:S(2)}, u32[]{:S(2)}) collective-permute-start(bf16[256,256]{1,0:T(8,128)(2,1)S(1)} %get-tuple-element.33.rest_0_), channel_id=1, source_target_pairs={{0,4},{1,5},{2,14},{3,15},{4,8},{5,9},{6,2},{7,3},{8,12},{9,13},{1... | collective-permute-start | bytes 393224 | tf_op jit(solution)/shard_map/ppermute | solution.py:41
  35.5 5.9 %collective-permute-start.12 = (bf16[256,256]{1,0:T(8,128)(2,1)S(1)}, bf16[256,256]{1,0:T(8,128)(2,1)S(1)}, u32[]{:S(2)}, u32[]{:S(2)}) collective-permute-start(bf16[256,256]{1,0:T(8,128)(2,1)S(1)} %collective-permute-done.11.rest_1_), channel_id=1, source_target_pairs={{0,2},{1,3},{2,0},{3,1},{4,6},{5,7},{6,4},{7,5},{8,10},{9,11},{10,... | collective-permute-start | bytes 393224 | tf_op jit(solution)/shard_map/ppermute | solution.py:26
  38.4 5.0 %collective-permute-start.18 = (bf16[256,256]{1,0:T(8,128)(2,1)S(1)}, bf16[256,256]{1,0:T(8,128)(2,1)S(1)}, u32[]{:S(2)}, u32[]{:S(2)}) collective-permute-start(bf16[256,256]{1,0:T(8,128)(2,1)S(1)} %collective-permute-done.11.rest_1_), channel_id=1, source_target_pairs={{0,12},{1,13},{2,6},{3,7},{4,0},{5,1},{6,10},{7,11},{8,4},{9,5},{1... | collective-permute-start | bytes 393224 | tf_op jit(solution)/shard_map/ppermute | solution.py:41
  39.9 1.7 %collective-permute-start.15 = (bf16[256,256]{1,0:T(8,128)(2,1)S(1)}, bf16[256,256]{1,0:T(8,128)(2,1)S(1)}, u32[]{:S(2)}, u32[]{:S(2)}) collective-permute-start(bf16[256,256]{1,0:T(8,128)(2,1)S(1)} %collective-permute-done.13), channel_id=1, source_target_pairs={{0,1},{1,0},{2,3},{3,2},{4,5},{5,4},{6,7},{7,6},{8,9},{9,8},{10,11... | collective-permute-start | bytes 393224 | tf_op jit(solution)/shard_map/ppermute | solution.py:20
  41.4 1.6 %collective-permute-start.16 = (bf16[512,256]{1,0:T(8,128)(2,1)S(1)}, bf16[512,256]{1,0:T(8,128)(2,1)S(1)}, u32[]{:S(2)}, u32[]{:S(2)}) collective-permute-start(bf16[512,256]{1,0:T(8,128)(2,1)S(1)} %pad_maximum_fusion.1), channel_id=1, source_target_pairs={{0,1},{1,0},{2,3},{3,2},{4,5},{5,4},{6,7},{7,6},{8,9},{9,8},{10,11... | collective-permute-start | bytes 786440 | tf_op jit(solution)/shard_map/ppermute | solution.py:20
  45.8 1.6 %collective-permute-start.20 = (f32[256,256]{1,0:T(8,128)S(1)}, f32[256,256]{1,0:T(8,128)S(1)}, u32[]{:S(2)}, u32[]{:S(2)}) collective-permute-start(f32[256,256]{1,0:T(8,128)S(1)} %get-tuple-element.36), channel_id=1, source_target_pairs={{0,1},{1,0},{2,3},{3,2},{4,5},{5,4},{6,7},{7,6},{8,9},{9,8},{10,11... | collective-permute-start | bytes 786440 | tf_op jit(solution)/shard_map/ppermute | solution.py:20
  45.9 3.6 %collective-permute-start.19 = (f32[256,256]{1,0:T(8,128)S(1)}, f32[256,256]{1,0:T(8,128)S(1)}, u32[]{:S(2)}, u32[]{:S(2)}) collective-permute-start(f32[256,256]{1,0:T(8,128)S(1)} %get-tuple-element.37), channel_id=1, source_target_pairs={{0,1},{1,0},{2,3},{3,2},{4,5},{5,4},{6,7},{7,6},{8,9},{9,8},{10,11... | collective-permute-start | bytes 786440 | tf_op jit(solution)/shard_map/ppermute | solution.py:20
  47.4 5.7 %collective-permute-start.21 = (bf16[256,256]{1,0:T(8,128)(2,1)S(1)}, bf16[256,256]{1,0:T(8,128)(2,1)S(1)}, u32[]{:S(2)}, u32[]{:S(2)}) collective-permute-start(bf16[256,256]{1,0:T(8,128)(2,1)S(1)} %fusion.2), channel_id=1, source_target_pairs={{0,2},{1,3},{2,0},{3,1},{4,6},{5,7},{6,4},{7,5},{8,10},{9,11},{10,... | collective-permute-start | bytes 393224 | tf_op jit(solution)/shard_map/ppermute | solution.py:26
